TPU v7x, 32 devices: a whole 2x2x4 slice. The times are simulated.
32 devices in a mesh: dp: 4 (over z), seq: 8 (over y, x, core).
Axes of the slice: x: 2, y: 2, z: 4, core: 2. Of those that a mesh axis runs over, the one named last changes fastest.
Arguments:
- hidden_in: bfloat16 [8, 1024, 768], P('dp', 'seq'), may hold values from -6 to 6
- cotangent: bfloat16 [8, 1024, 768], P('dp', 'seq'), may hold values from -6 to 6
- segment_ids: int32 [8, 1024], P('dp', 'seq'), may hold values from 0 to 5, as said below
- query_weight: bfloat16 [768, 768], P(('dp', 'seq')), may hold values from -0.21875 to 0.21875
- key_weight: bfloat16 [768, 768], P(('dp', 'seq')), may hold values from -0.21875 to 0.21875
- value_weight: bfloat16 [768, 768], P(('dp', 'seq')), may hold values from -0.21875 to 0.21875
- out_weight: bfloat16 [768, 768], P(('dp', 'seq')), may hold values from -1.25 to 1.25
- up_weight: bfloat16 [768, 3072], P(('dp', 'seq')), may hold values from -0.21875 to 0.21875
- down_weight: bfloat16 [3072, 768], P(('dp', 'seq')), may hold values from -0.109375 to 0.109375
- query_bias: bfloat16 [768], P(('dp', 'seq')), may hold values from -1.796875 to 1.796875
- value_bias: bfloat16 [768], P(('dp', 'seq')), may hold values from -1.796875 to 1.796875
- out_bias: bfloat16 [768], P(('dp', 'seq')), may hold values from -1.796875 to 1.796875
- up_bias: bfloat16 [3072], P(('dp', 'seq')), may hold values from -1.796875 to 1.796875
- down_bias: bfloat16 [768], P(('dp', 'seq')), may hold values from -1.796875 to 1.796875
- first_gain: bfloat16 [768], P(('dp', 'seq')), may hold values from 0.5 to 1.5
- first_shift: bfloat16 [768], P(('dp', 'seq')), may hold values from -1.796875 to 1.796875
- second_gain: bfloat16 [768], P(('dp', 'seq')), may hold values from 0.5 to 1.5
- second_shift: bfloat16 [768], P(('dp', 'seq')), may hold values from -1.796875 to 1.796875
Outputs:
- hidden_out: bfloat16 [8, 1024, 768], P('dp', 'seq')
- grad_input: float32 [8, 1024, 768], P('dp', 'seq')
- grad_query_weight: float32 [768, 768], P(('dp', 'seq'))
- grad_key_weight: float32 [768, 768], P(('dp', 'seq'))
- grad_value_weight: float32 [768, 768], P(('dp', 'seq'))
- grad_out_weight: float32 [768, 768], P(('dp', 'seq'))
- grad_up_weight: float32 [768, 3072], P(('dp', 'seq'))
- grad_down_weight: float32 [3072, 768], P(('dp', 'seq'))
- grad_query_bias: float32 [768], P(('dp', 'seq'))
- grad_value_bias: float32 [768], P(('dp', 'seq'))
- grad_out_bias: float32 [768], P(('dp', 'seq'))
- grad_up_bias: float32 [3072], P(('dp', 'seq'))
- grad_down_bias: float32 [768], P(('dp', 'seq'))
- grad_first_gain: float32 [768], P(('dp', 'seq'))
- grad_first_shift: float32 [768], P(('dp', 'seq'))
- grad_second_gain: float32 [768], P(('dp', 'seq'))
- grad_second_shift: float32 [768], P(('dp', 'seq'))
Inputs may be any that keep to these rules, and one draw needn't show every extreme that they name: `segment_ids`: ids start at 0 in each sequence and never fall along it. In each group of 2 sequences of one index of dp, one sequence, drawn from the seed, is a single document; in the first group another sequence holds documents of exactly 200 tokens; the others hold documents of 200 to 2000 tokens; the last document of a sequence may be shorter.
All inputs are finite; a program needn't handle non-finite values.
Results may differ from a plain program's by a relative error of at most 0.017.
Values may be sent and summed in bfloat16 or wider, within the bound.
No kernel may reach another device: no remote copies, remote signals or barrier semaphores. Data moves between devices by JAX's collectives and lax.ppermute only.
A program may use at most 256 MiB of HBM per device.

v0:
```python
import jax
import jax.numpy as jnp
from jax import lax
from jax.sharding import PartitionSpec as P

HEADS = 12
HEAD_DIM = 64
MICRO = 2


def layer_norm(value, gain, shift):
    center = value - jnp.mean(value, -1, keepdims=True)
    spread = jnp.mean(center * center, -1, keepdims=True)
    return center * lax.rsqrt(spread + 1e-05) * gain + shift


def project(left, weight):
    return jnp.einsum("spd,de->spe", left, weight, preferred_element_type=jnp.float32)


def project_back(left, weight):
    return jnp.einsum("spe,de->spd", left, weight, preferred_element_type=jnp.float32)


def weight_term(left, right):
    return jnp.einsum("spd,spe->de", left, right, preferred_element_type=jnp.float32)


def row_total(value):
    return jnp.sum(value.astype(jnp.float32), axis=(0, 1))


def local(
    hidden_in,
    cotangent,
    segment_ids,
    query_weight,
    key_weight,
    value_weight,
    out_weight,
    up_weight,
    down_weight,
    query_bias,
    value_bias,
    out_bias,
    up_bias,
    down_bias,
    first_gain,
    first_shift,
    second_gain,
    second_shift,
):
    params = (
        query_weight,
        key_weight,
        value_weight,
        out_weight,
        up_weight,
        down_weight,
        query_bias,
        value_bias,
        out_bias,
        up_bias,
        down_bias,
        first_gain,
        first_shift,
        second_gain,
        second_shift,
    )
    local_seqs, shard_rows, model_width = hidden_in.shape
    group_size = local_seqs // MICRO
    owners = lax.axis_size("dp") * lax.axis_size("seq")
    seg_all = lax.all_gather(segment_ids, "seq", axis=1, tiled=True)
    query_pos = lax.axis_index("seq") * shard_rows + jnp.arange(shard_rows)
    totals = tuple(
        (jnp.zeros((item.shape[0] * owners,) + item.shape[1:], jnp.float32) for item in params)
    )
    outs_rows = []
    outs_grads = []
    for micro_step in range(MICRO):
        lower = micro_step * group_size
        upper_end = lower + group_size
        gathered = (
            lax.all_gather(params[0], ("dp", "seq"), axis=0, tiled=True),
            lax.all_gather(params[1], ("dp", "seq"), axis=0, tiled=True),
            lax.all_gather(params[2], ("dp", "seq"), axis=0, tiled=True),
            lax.all_gather(params[3], ("dp", "seq"), axis=0, tiled=True),
            lax.all_gather(params[4], ("dp", "seq"), axis=0, tiled=True),
            lax.all_gather(params[5], ("dp", "seq"), axis=0, tiled=True),
            lax.all_gather(params[6], ("dp", "seq"), axis=0, tiled=True),
            lax.all_gather(params[7], ("dp", "seq"), axis=0, tiled=True),
            lax.all_gather(params[8], ("dp", "seq"), axis=0, tiled=True),
            lax.all_gather(params[9], ("dp", "seq"), axis=0, tiled=True),
            lax.all_gather(params[10], ("dp", "seq"), axis=0, tiled=True),
            lax.all_gather(params[11], ("dp", "seq"), axis=0, tiled=True),
            lax.all_gather(params[12], ("dp", "seq"), axis=0, tiled=True),
            lax.all_gather(params[13], ("dp", "seq"), axis=0, tiled=True),
            lax.all_gather(params[14], ("dp", "seq"), axis=0, tiled=True),
        )
        wq, wk, wv, wo, wu, wd = gathered[:6]
        bq, bv, bo, bu, bd, gain_one, shift_one, gain_two, shift_two = tuple(
            (item.astype(jnp.float32) for item in gathered[6:])
        )
        block_in = hidden_in[lower:upper_end].astype(jnp.float32)
        seg_here = segment_ids[lower:upper_end]
        seg_keys = seg_all[lower:upper_end]
        normed_low = layer_norm(block_in, gain_one, shift_one).astype(jnp.bfloat16)
        queries = (
            ((project(normed_low, wq) + bq) * 0.125)
            .astype(jnp.bfloat16)
            .reshape(group_size, shard_rows, HEADS, HEAD_DIM)
        )
        key_rows = project(normed_low, wk).astype(jnp.bfloat16)
        value_rows = (project(normed_low, wv) + bv).astype(jnp.bfloat16)

        def masked_scores(key_heads):
            count_keys = key_heads.shape[1]
            raw_scores = jnp.einsum(
                "sqhd,skhd->shqk", queries, key_heads, preferred_element_type=jnp.float32
            )
            key_pos = jnp.arange(count_keys)
            same_doc = seg_here[:, :, None] == seg_keys[:, None, :]
            causal = key_pos[None, :] <= query_pos[:, None]
            allowed = (same_doc & causal[None])[:, None]
            return jnp.where(allowed, raw_scores, -1000000000.0)

        pieces = (
            lax.all_gather(key_rows, "seq", axis=1, tiled=True),
            lax.all_gather(value_rows, "seq", axis=1, tiled=True),
        )
        run_max = jnp.full((group_size, HEADS, shard_rows), -1e30, jnp.float32)
        forward_count_keys = pieces[0].shape[1]
        forward_key_heads = pieces[0].reshape(group_size, forward_count_keys, HEADS, HEAD_DIM)
        value_heads = pieces[1].reshape(group_size, forward_count_keys, HEADS, HEAD_DIM)
        forward_raw_scores = masked_scores(forward_key_heads)
        new_max = jnp.maximum(run_max, jnp.max(forward_raw_scores, -1))
        expo = jnp.exp(forward_raw_scores - new_max[..., None])
        run_sum = jnp.sum(expo, -1)
        run_acc = jnp.einsum(
            "shqk,skhd->shqd",
            expo.astype(jnp.bfloat16),
            value_heads,
            preferred_element_type=jnp.float32,
        )
        run_max, run_sum, run_acc = (new_max, run_sum, run_acc)
        attended_full = (run_acc / run_sum[..., None]).transpose(0, 2, 1, 3)
        log_total = run_max + jnp.log(run_sum)
        attended_low = attended_full.reshape(group_size, shard_rows, model_width).astype(
            jnp.bfloat16
        )
        middle = block_in + project(attended_low, wo) + bo
        second_low = layer_norm(middle, gain_two, shift_two).astype(jnp.bfloat16)
        upper_pre = project(second_low, wu) + bu
        act_full, act_back = jax.vjp(jax.nn.gelu, upper_pre)
        act_low = act_full.astype(jnp.bfloat16)
        output_rows = middle + project(act_low, wd) + bd
        outs_rows.append(output_rows.astype(jnp.bfloat16))
        back_weights = (
            lax.all_gather(params[0], ("dp", "seq"), axis=0, tiled=True),
            lax.all_gather(params[1], ("dp", "seq"), axis=0, tiled=True),
            lax.all_gather(params[2], ("dp", "seq"), axis=0, tiled=True),
            lax.all_gather(params[3], ("dp", "seq"), axis=0, tiled=True),
            lax.all_gather(params[4], ("dp", "seq"), axis=0, tiled=True),
            lax.all_gather(params[5], ("dp", "seq"), axis=0, tiled=True),
            lax.all_gather(params[6], ("dp", "seq"), axis=0, tiled=True),
            lax.all_gather(params[7], ("dp", "seq"), axis=0, tiled=True),
            lax.all_gather(params[8], ("dp", "seq"), axis=0, tiled=True),
            lax.all_gather(params[9], ("dp", "seq"), axis=0, tiled=True),
            lax.all_gather(params[10], ("dp", "seq"), axis=0, tiled=True),
            lax.all_gather(params[11], ("dp", "seq"), axis=0, tiled=True),
            lax.all_gather(params[12], ("dp", "seq"), axis=0, tiled=True),
            lax.all_gather(params[13], ("dp", "seq"), axis=0, tiled=True),
            lax.all_gather(params[14], ("dp", "seq"), axis=0, tiled=True),
        )
        wq, wk, wv, wo, wu, wd = back_weights[:6]
        grad_out = cotangent[lower:upper_end].astype(jnp.float32)
        grad_low = grad_out.astype(jnp.bfloat16)
        d_act = project_back(grad_low, wd)
        d_upper = act_back(d_act)[0].astype(jnp.bfloat16)
        d_second = project_back(d_upper, wu)
        second_norm_back = jax.vjp(layer_norm, middle, gain_two, shift_two)[1]
        d_middle_part, d_gain_two, d_shift_two = second_norm_back(d_second)
        d_middle = grad_out + d_middle_part
        d_branch = d_middle.astype(jnp.bfloat16)
        d_attended = (
            project_back(d_branch, wo)
            .astype(jnp.bfloat16)
            .reshape(group_size, shard_rows, HEADS, HEAD_DIM)
        )
        row_dots = jnp.sum(d_attended.astype(jnp.float32) * attended_full, -1).transpose(0, 2, 1)
        backward_pieces = (
            lax.all_gather(key_rows, "seq", axis=1, tiled=True),
            lax.all_gather(value_rows, "seq", axis=1, tiled=True),
        )
        backward_count_keys = backward_pieces[0].shape[1]
        backward_key_heads = backward_pieces[0].reshape(
            group_size, backward_count_keys, HEADS, HEAD_DIM
        )
        backward_value_heads = backward_pieces[1].reshape(
            group_size, backward_count_keys, HEADS, HEAD_DIM
        )
        probs = jnp.exp(masked_scores(backward_key_heads) - log_total[..., None])
        d_probs = jnp.einsum(
            "sqhd,skhd->shqk", d_attended, backward_value_heads, preferred_element_type=jnp.float32
        )
        d_scores = (probs * (d_probs - row_dots[..., None])).astype(jnp.bfloat16)
        value_term = jnp.einsum(
            "shqk,sqhd->skhd",
            probs.astype(jnp.bfloat16),
            d_attended,
            preferred_element_type=jnp.float32,
        )
        key_term = jnp.einsum(
            "shqk,sqhd->skhd", d_scores, queries, preferred_element_type=jnp.float32
        )
        d_query = jnp.einsum(
            "shqk,skhd->sqhd", d_scores, backward_key_heads, preferred_element_type=jnp.float32
        )
        d_keys_all = key_term.reshape(group_size, backward_count_keys, model_width)
        d_values_all = value_term.reshape(group_size, backward_count_keys, model_width)
        d_query, d_keys_all, d_values_all = (d_query, d_keys_all, d_values_all)
        d_keys, d_values = (
            lax.psum_scatter(
                d_keys_all.astype(jnp.bfloat16), "seq", scatter_dimension=1, tiled=True
            ).astype(jnp.float32),
            lax.psum_scatter(
                d_values_all.astype(jnp.bfloat16), "seq", scatter_dimension=1, tiled=True
            ).astype(jnp.float32),
        )
        d_query_low = d_query.reshape(group_size, shard_rows, model_width).astype(jnp.bfloat16)
        d_keys_low = d_keys.astype(jnp.bfloat16)
        d_values_low = d_values.astype(jnp.bfloat16)
        d_first = (
            0.125 * project_back(d_query_low, wq)
            + project_back(d_keys_low, wk)
            + project_back(d_values_low, wv)
        )
        first_norm_back = jax.vjp(layer_norm, block_in, gain_one, shift_one)[1]
        d_input_part, d_gain_one, d_shift_one = first_norm_back(d_first)
        outs_grads.append(d_middle + d_input_part)
        grad_terms = (
            0.125 * weight_term(normed_low, d_query_low),
            weight_term(normed_low, d_keys_low),
            weight_term(normed_low, d_values_low),
            weight_term(attended_low, d_branch),
            weight_term(second_low, d_upper),
            weight_term(act_low, grad_low),
            0.125 * row_total(d_query_low),
            row_total(d_values_low),
            row_total(d_branch),
            row_total(d_upper),
            row_total(grad_low),
            d_gain_one,
            d_shift_one,
            d_gain_two,
            d_shift_two,
        )
        totals = tuple((left + right for left, right in zip(totals, grad_terms)))
    grads = lax.psum_scatter(totals, ("dp", "seq"), scatter_dimension=0, tiled=True)
    return (jnp.concatenate(outs_rows, 0), jnp.concatenate(outs_grads, 0)) + tuple(grads)


def solution(mesh):
    placed = (
        P("dp", "seq", None),
        P("dp", "seq", None),
        P("dp", "seq"),
        P(("dp", "seq"), None),
        P(("dp", "seq"), None),
        P(("dp", "seq"), None),
        P(("dp", "seq"), None),
        P(("dp", "seq"), None),
        P(("dp", "seq"), None),
        P(("dp", "seq")),
        P(("dp", "seq")),
        P(("dp", "seq")),
        P(("dp", "seq")),
        P(("dp", "seq")),
        P(("dp", "seq")),
        P(("dp", "seq")),
        P(("dp", "seq")),
        P(("dp", "seq")),
    )
    return jax.shard_map(
        local,
        mesh=mesh,
        in_specs=placed,
        out_specs=(
            P("dp", "seq", None),
            P("dp", "seq", None),
            P(("dp", "seq"), None),
            P(("dp", "seq"), None),
            P(("dp", "seq"), None),
            P(("dp", "seq"), None),
            P(("dp", "seq"), None),
            P(("dp", "seq"), None),
            P(("dp", "seq")),
            P(("dp", "seq")),
            P(("dp", "seq")),
            P(("dp", "seq")),
            P(("dp", "seq")),
            P(("dp", "seq")),
            P(("dp", "seq")),
            P(("dp", "seq")),
            P(("dp", "seq")),
        ),
        check_vma=False,
    )
```

profile of v0, /device:TPU:0, one launch (start us, length us, event | category | flops | bytes accessed | tf_op | source)
XLA Modules:
  0.0 1378.5 jit_solution(3144937666261775236)
XLA Ops:
  17.0 42.6 %all-reduce.19 = (bf16[768]{0:T(1024)(128)(2,1)S(1)}, bf16[768]{0:T(1024)(128)(2,1)S(1)}, bf16[768]{0:T(1024)(128)(2,1)S(1)}, bf16[768]{0:T(1024)(128)(2,1)S(1)}...) all-reduce(bf16[768]{0:T(1024)(128)(2,1)S(1)} %dynamic-update-slice, ...), channel_id=1, replica_groups=mesh['dp'=4,'seq'=8] {'dp','seq'}, use_global_device_ids=true, to_apply=%add.3 | all-reduce | flops 9216 | bytes 36864
  62.1 5.9 all-gather.17.cloned.1.call-done
  68.1 2.4 convolution_convert_fusion.5
  70.6 53.2 %all-gather.19.cloned.1.call-done = bf16[768,768]{1,0:T(8,128)(2,1)} async-done(((bf16[24,768]{1,0:T(8,128)(2,1)}), bf16[768,768]{1,0:T(8,128)(2,1)}) %all-gather.19.cloned.1.call-update) | async-done | bytes 1179664 | tf_op jit(solution)/shard_map/all_gather | solution.py:86
  123.8 2.5 fusion.60
  132.0 8.8 all_gather.40
  141.8 37.9 %all-gather.15.cloned.1.call-done = bf16[768,768]{1,0:T(8,128)(2,1)} async-done(((bf16[24,768]{1,0:T(8,128)(2,1)}), bf16[768,768]{1,0:T(8,128)(2,1)}) %all-gather.15.cloned.1.call-update) | async-done | bytes 1179664 | tf_op jit(solution)/shard_map/all_gather | solution.py:84
  179.7 1.7 fusion.58
  183.5 23.2 %all-gather.27.cloned.1.call-done = bf16[1024,768]{1,0:T(8,128)(2,1)} async-done(((bf16[128,768]{1,0:T(8,128)(2,1)}), bf16[1024,768]{1,0:T(8,128)(2,1)}) %all-gather.27.cloned.1.call-update) | async-done | bytes 1572880 | tf_op jit(solution)/shard_map/all_gather | solution.py:128
  206.7 1.7 copy.64
  208.4 25.7 %all-gather.29.cloned.1.call-done = bf16[1024,768]{1,0:T(8,128)(2,1)} async-done(((bf16[128,768]{1,0:T(8,128)(2,1)}), bf16[1024,768]{1,0:T(8,128)(2,1)}) %all-gather.29.cloned.1.call-update) | async-done | bytes 1572880 | tf_op jit(solution)/shard_map/all_gather | solution.py:129
  234.1 2.6 copy.65
  236.7 25.4 %all-gather.33.cloned.1.call-done = bf16[1024,768]{1,0:T(8,128)(2,1)} async-done(((bf16[128,768]{1,0:T(8,128)(2,1)}), bf16[1024,768]{1,0:T(8,128)(2,1)}) %all-gather.33.cloned.1.call-update) | async-done | bytes 1572880 | tf_op jit(solution)/shard_map/all_gather | solution.py:129
  262.2 2.6 copy.68
  264.8 25.5 %all-gather.31.cloned.1.call-done = bf16[1024,768]{1,0:T(8,128)(2,1)} async-done(((bf16[128,768]{1,0:T(8,128)(2,1)}), bf16[1024,768]{1,0:T(8,128)(2,1)}) %all-gather.31.cloned.1.call-update) | async-done | bytes 1572880 | tf_op jit(solution)/shard_map/all_gather | solution.py:128
  290.3 2.2 copy.67
  292.6 2.7 select_reduce_fusion.1
  298.5 2.4 fusion.173
  300.8 46.5 %all-gather.21.cloned.1.call-done = bf16[768,768]{1,0:T(8,128)(2,1)} async-done(((bf16[24,768]{1,0:T(8,128)(2,1)}), bf16[768,768]{1,0:T(8,128)(2,1)}) %all-gather.21.cloned.1.call-update) | async-done | bytes 1179664 | tf_op jit(solution)/shard_map/all_gather | solution.py:87
  347.3 1.7 fusion.174
  353.6 2.3 fusion.171
  356.7 56.1 %all-gather.23.cloned.1.call-done = bf16[768,3072]{1,0:T(8,128)(2,1)} async-done(((bf16[24,3072]{1,0:T(8,128)(2,1)}), bf16[768,3072]{1,0:T(8,128)(2,1)}) %all-gather.23.cloned.1.call-update) | async-done | bytes 4718608 | tf_op jit(solution)/shard_map/all_gather | solution.py:88
  412.8 4.5 convolution_add_fusion.3
  417.3 2.0 convolution_add_fusion.2
  419.4 58.7 %all-gather.25.cloned.1.call-done = bf16[3072,768]{1,0:T(8,128)(2,1)} async-done(((bf16[96,768]{1,0:T(8,128)(2,1)}), bf16[3072,768]{1,0:T(8,128)(2,1)}) %all-gather.25.cloned.1.call-update) | async-done | bytes 4718608 | tf_op jit(solution)/shard_map/all_gather | solution.py:89
  478.1 5.5 convert_reduce_fusion.1
  483.6 2.7 convert_reduce_fusion
  486.4 2.3 fusion.176
  488.6 2.3 fusion.99
  494.4 4.6 fusion.26
  498.9 5.8 copy.75
  504.7 3.3 copy.91
  509.6 5.7 fusion.29
  515.4 7.2 copy.79
  525.2 5.9 multiply_convert_fusion.1
  531.1 1.7 convolution_convert_fusion.1
  532.8 8.7 copy.73
  541.5 3.3 copy.92
  544.8 1.8 copy.72
  547.9 5.6 multiply_convert_fusion
  553.5 2.1 convolution_convert_fusion
  555.6 8.4 copy.77
  564.1 3.3 copy.90
  569.1 1.9 convolution_add_fusion.4
  571.1 3.4 convert_reduce_fusion.11
  576.1 1.9 convert_reduce_fusion.10
  578.6 2.0 add_multiply_fusion
  582.3 4.8 reduce-scatter.37.cloned.1.call-done
  589.3 2.0 convolution_add_fusion.5
  591.4 37.5 %reduce-scatter.31.cloned.1.call-done = bf16[128,768]{1,0:T(8,128)(2,1)} async-done(((bf16[1024,768]{1,0:T(8,128)(2,1)}), bf16[128,768]{1,0:T(8,128)(2,1)}) %reduce-scatter.31.cloned.1.call-update) | async-done | bytes 196624
  630.4 40.1 %reduce-scatter.35.cloned.1.call-done = bf16[128,768]{1,0:T(8,128)(2,1)} async-done(((bf16[1024,768]{1,0:T(8,128)(2,1)}), bf16[128,768]{1,0:T(8,128)(2,1)}) %reduce-scatter.35.cloned.1.call-update) | async-done | bytes 196624
  672.7 2.0 convolution_add_fusion.6
  677.7 5.4 convolution_add_fusion
  684.1 2.7 fusion.150
  686.8 5.2 convolution_add_fusion.1
  700.0 3.6 fusion.57
  703.6 3.6 fusion.56
  713.8 40.6 %all-reduce.18 = (f32[768]{0:T(1024)S(1)}, f32[768]{0:T(1024)S(1)}, f32[768]{0:T(1024)S(1)}, f32[3072]{0:T(1024)S(1)}, f32[768]{0:T(1024)S(1)}, /*index=5*/f32[7...) all-reduce(f32[768]{0:T(1024)S(1)} %add.382, ...), channel_id=16, replica_groups=mesh['dp'=4,'seq'=8] {'dp','seq'}, use_global_device_ids=true, to_apply=%region_34.35.clone | all-reduce | flops 9216 | bytes 73728
  761.0 14.4 %reduce-scatter.25.cloned.1.call-done = f32[24,768]{1,0:T(8,128)} async-done(((f32[768,768]{1,0:T(8,128)}), f32[24,768]{1,0:T(8,128)}) %reduce-scatter.25.cloned.1.call-update) | async-done | bytes 73744 | tf_op jit(solution)/shard_map/reduce_scatter | solution.py:259
  775.4 104.6 %reduce-scatter.19.cloned.1.call-done = f32[24,768]{1,0:T(8,128)} async-done(((f32[768,768]{1,0:T(8,128)}), f32[24,768]{1,0:T(8,128)}) %reduce-scatter.19.cloned.1.call-update) | async-done | bytes 73744 | tf_op jit(solution)/shard_map/reduce_scatter | solution.py:259
  880.1 103.8 %reduce-scatter.23.cloned.1.call-done = f32[24,768]{1,0:T(8,128)} async-done(((f32[768,768]{1,0:T(8,128)}), f32[24,768]{1,0:T(8,128)}) %reduce-scatter.23.cloned.1.call-update) | async-done | bytes 73744 | tf_op jit(solution)/shard_map/reduce_scatter | solution.py:259
  983.8 104.6 %reduce-scatter.21.cloned.1.call-done = f32[24,768]{1,0:T(8,128)} async-done(((f32[768,768]{1,0:T(8,128)}), f32[24,768]{1,0:T(8,128)}) %reduce-scatter.21.cloned.1.call-update) | async-done | bytes 73744 | tf_op jit(solution)/shard_map/reduce_scatter | solution.py:259
  1088.4 141.2 %reduce-scatter.29.cloned.1.call-done = f32[96,768]{1,0:T(8,128)} async-done(((f32[3072,768]{1,0:T(8,128)}), f32[96,768]{1,0:T(8,128)}) %reduce-scatter.29.cloned.1.call-update) | async-done | bytes 294928 | tf_op jit(solution)/shard_map/reduce_scatter | solution.py:259
  1229.5 142.0 %reduce-scatter.27.cloned.1.call-done = f32[24,3072]{1,0:T(8,128)} async-done(((f32[768,3072]{1,0:T(8,128)}), f32[24,3072]{1,0:T(8,128)}) %reduce-scatter.27.cloned.1.call-update) | async-done | bytes 294928 | tf_op jit(solution)/shard_map/reduce_scatter | solution.py:259
  (403 shorter events, 74.1 us)
Async XLA Ops:
  7.2 116.6 %copy-start.3 = (bf16[2,128,768]{2,1,0:T(8,128)(2,1)S(1)}, bf16[2,128,768]{2,1,0:T(8,128)(2,1)}, u32[]{:S(2)}) copy-start(bf16[2,128,768]{2,1,0:T(8,128)(2,1)} %param.18) | copy-start | bytes 1179652
  7.2 60.9 %all-gather.17.cloned.1.call-start = ((), (), s32[]{:S(2)}) async-start(), calls=%async_computation.11 | async-start | bytes 1216512 | tf_op jit(solution)/shard_map/all_gather | solution.py:85
  7.9 115.9 %all-gather.19.cloned.1.call-start = ((), (), s32[]{:S(2)}) async-start(), calls=%async_computation.12 | async-start | bytes 1216512 | tf_op jit(solution)/shard_map/all_gather | solution.py:86
  8.7 171.0 %all-gather.15.cloned.1.call-start = ((), (), s32[]{:S(2)}) async-start(), calls=%async_computation.10 | async-start | bytes 1216512 | tf_op jit(solution)/shard_map/all_gather | solution.py:84
  9.4 197.2 %all-gather.27.cloned.1.call-start = ((), (), s32[]{:S(2)}) async-start(), calls=%async_computation.22 | async-start | bytes 1769472 | tf_op jit(solution)/shard_map/all_gather | solution.py:128
  60.8 118.9 %copy-start.77 = (f32[128]{0:T(128)}, f32[128]{0:T(128)S(1)}, u32[]{:S(2)}) copy-start(f32[128]{0:T(128)S(1)} %get-tuple-element.103) | copy-start | bytes 1540
  60.8 121.5 %copy-start.80 = (f32[128]{0:T(128)}, f32[128]{0:T(128)S(1)}, u32[]{:S(2)}) copy-start(f32[128]{0:T(128)S(1)} %get-tuple-element.104) | copy-start | bytes 1540
  62.1 8.5 copy-start.114
  62.1 64.2 %copy-start.112 = (f32[128]{0:T(128)}, f32[128]{0:T(128)S(1)}, u32[]{:S(2)}) copy-start(f32[128]{0:T(128)S(1)} %get-tuple-element.32) | copy-start | bytes 1540
  62.1 120.1 %copy-start.90 = (f32[128]{0:T(128)}, f32[128]{0:T(128)S(1)}, u32[]{:S(2)}) copy-start(f32[128]{0:T(128)S(1)} %fusion.138) | copy-start | bytes 1540
  70.5 163.6 %all-gather.29.cloned.1.call-start = ((), (), s32[]{:S(2)}) async-start(), calls=%async_computation.23 | async-start | bytes 1769472 | tf_op jit(solution)/shard_map/all_gather | solution.py:129
  126.3 135.9 %all-gather.33.cloned.1.call-start = ((), (), s32[]{:S(2)}) async-start(), calls=%async_computation.25 | async-start | bytes 1769472 | tf_op jit(solution)/shard_map/all_gather | solution.py:129
  126.4 53.3 %copy-start.94 = (f32[128]{0:T(128)}, f32[128]{0:T(128)S(1)}, u32[]{:S(2)}) copy-start(f32[128]{0:T(128)S(1)} %fusion.140) | copy-start | bytes 1540
  127.4 4.5 copy-start.106
  127.5 162.9 %all-gather.31.cloned.1.call-start = ((), (), s32[]{:S(2)}) async-start(), calls=%async_computation.24 | async-start | bytes 1769472 | tf_op jit(solution)/shard_map/all_gather | solution.py:128
  128.6 218.7 %all-gather.21.cloned.1.call-start = ((), (), s32[]{:S(2)}) async-start(), calls=%async_computation.13 | async-start | bytes 1216512 | tf_op jit(solution)/shard_map/all_gather | solution.py:87
  129.4 283.5 %all-gather.23.cloned.1.call-start = ((), (), s32[]{:S(2)}) async-start(), calls=%async_computation.14 | async-start | bytes 4866048 | tf_op jit(solution)/shard_map/all_gather | solution.py:88
  130.1 348.0 %all-gather.25.cloned.1.call-start = ((), (), s32[]{:S(2)}) async-start(), calls=%async_computation.15 | async-start | bytes 4866048 | tf_op jit(solution)/shard_map/all_gather | solution.py:89
  130.7 450.0 %reduce-scatter.33.cloned.1.call-start = ((), (), s32[]{:S(2)}) async-start(), calls=%async_computation.27 | async-start | bytes 1769472
  208.4 84.2 %copy-start.9 = (bf16[1024,768]{0,1:T(8,128)(2,1)}, bf16[1024,768]{0,1:T(8,128)(2,1)S(1)}, u32[]{:S(2)}) copy-start(bf16[1024,768]{0,1:T(8,128)(2,1)S(1)} %copy.64) | copy-start | bytes 4718596
  292.5 57.1 %copy-start.10 = (bf16[1024,768]{0,1:T(8,128)(2,1)}, bf16[1024,768]{0,1:T(8,128)(2,1)S(1)}, u32[]{:S(2)}) copy-start(bf16[1024,768]{0,1:T(8,128)(2,1)S(1)} %copy.67) | copy-start | bytes 4718596
  298.5 48.9 %copy-start.75 = (f32[768]{0:T(1024)S(1)}, f32[768]{0:T(1024)}, u32[]{:S(2)}) copy-start(f32[768]{0:T(1024)} %convert_element_type.382) | copy-start | bytes 9220
  300.8 50.0 %copy-start.65 = (bf16[1,128,12,64]{1,3,2,0:T(8,128)(2,1)}, bf16[1,128,12,64]{1,3,2,0:T(8,128)(2,1)S(1)}, u32[]{:S(2)}) copy-start(bf16[1,128,12,64]{1,3,2,0:T(8,128)(2,1)S(1)} %get-tuple-element.85) | copy-start | bytes 589828
  300.8 48.8 %copy-start.34 = (pred[128,1024]{1,0:T(8,128)(4,1)S(1)}, pred[128,1024]{1,0:T(8,128)(4,1)}, u32[]{:S(2)}) copy-start(pred[128,1024]{1,0:T(8,128)(4,1)} %get-tuple-element.76) | copy-start | bytes 393220
  300.8 48.8 %copy-start.53 = (bf16[128,768]{0,1:T(8,128)(2,1)S(1)}, bf16[128,768]{0,1:T(8,128)(2,1)}, u32[]{:S(2)}) copy-start(bf16[128,768]{0,1:T(8,128)(2,1)} %copy.66) | copy-start | bytes 589828
  349.0 142.0 %copy-start.7 = (f32[1,128,768]{2,1,0:T(8,128)}, f32[1,128,768]{2,1,0:T(8,128)S(1)}, u32[]{:S(2)}) copy-start(f32[1,128,768]{2,1,0:T(8,128)S(1)} %get-tuple-element.88) | copy-start | bytes 1179652
  349.3 7.4 copy-start.116
  355.9 56.9 %copy-start.63 = (bf16[1,128,12,64]{1,3,2,0:T(8,128)(2,1)}, bf16[1,128,12,64]{1,3,2,0:T(8,128)(2,1)S(1)}, u32[]{:S(2)}) copy-start(bf16[1,128,12,64]{1,3,2,0:T(8,128)(2,1)S(1)} %get-tuple-element.79) | copy-start | bytes 589828
  355.9 56.9 %copy-start.67 = (f32[3072]{0:T(1024)S(1)}, f32[3072]{0:T(1024)}, u32[]{:S(2)}) copy-start(f32[3072]{0:T(1024)} %convert_element_type.386) | copy-start | bytes 36868
  355.9 56.9 %copy-start.88 = (f32[128]{0:T(128)S(1)}, f32[128]{0:T(128)}, u32[]{:S(2)}) copy-start(f32[128]{0:T(128)} %copy-done.87) | copy-start | bytes 1540
  356.4 134.6 %copy-start.12 = (f32[1,128,768]{2,1,0:T(8,128)}, f32[1,128,768]{2,1,0:T(8,128)S(1)}, u32[]{:S(2)}) copy-start(f32[1,128,768]{2,1,0:T(8,128)S(1)} %get-tuple-element.82) | copy-start | bytes 1179652
  356.4 134.6 %copy-start.100 = (f32[128]{0:T(128)}, f32[128]{0:T(128)S(1)}, u32[]{:S(2)}) copy-start(f32[128]{0:T(128)S(1)} %broadcast_multiply_fusion) | copy-start | bytes 1540
  356.6 134.4 %copy-start.102 = (f32[128]{0:T(128)}, f32[128]{0:T(128)S(1)}, u32[]{:S(2)}) copy-start(f32[128]{0:T(128)S(1)} %fusion.139) | copy-start | bytes 1540
  356.7 134.4 %copy-start.104 = (f32[128]{0:T(128)}, f32[128]{0:T(128)S(1)}, u32[]{:S(2)}) copy-start(f32[128]{0:T(128)S(1)} %fusion.141) | copy-start | bytes 1540
  356.7 137.7 %copy-start.72 = (f32[12,128]{1,0:T(8,128)}, f32[12,128]{1,0:T(8,128)S(1)}, u32[]{:S(2)}) copy-start(f32[12,128]{1,0:T(8,128)S(1)} %log_add_fusion.1) | copy-start | bytes 18436
  417.3 60.7 %copy-start.26 = (bf16[2,128,768]{2,1,0:T(8,128)(2,1)S(1)}, bf16[2,128,768]{2,1,0:T(8,128)(2,1)}, u32[]{:S(2)}) copy-start(bf16[2,128,768]{2,1,0:T(8,128)(2,1)} %param.19) | copy-start | bytes 1179652
  478.1 5.5 copy-start.15
  478.1 5.5 copy-start.118
  478.1 8.3 slice-start
  483.6 5.0 copy-start.42
  508.0 79.1 %reduce-scatter.37.cloned.1.call-start = ((), (), s32[]{:S(2)}) async-start(), calls=%async_computation.29 | async-start | bytes 1769472
  508.7 6.7 copy-start.73
  509.5 5.9 copy-start.58
  509.6 5.8 copy-start.62
  524.1 104.8 %reduce-scatter.31.cloned.1.call-start = ((), (), s32[]{:S(2)}) async-start(), calls=%async_computation.26 | async-start | bytes 1769472
  525.2 5.9 copy-start.55
  544.8 125.7 %reduce-scatter.35.cloned.1.call-start = ((), (), s32[]{:S(2)}) async-start(), calls=%async_computation.28 | async-start | bytes 1769472
  547.9 5.6 copy-start.54
  567.5 208.0 %reduce-scatter.25.cloned.1.call-start = ((), (), s32[]{:S(2)}) async-start(), calls=%async_computation.19 | async-start | bytes 2433024 | tf_op jit(solution)/shard_map/reduce_scatter | solution.py:259
  571.0 309.0 %reduce-scatter.19.cloned.1.call-start = ((), (), s32[]{:S(2)}) async-start(), calls=%async_computation.16 | async-start | bytes 2433024 | tf_op jit(solution)/shard_map/reduce_scatter | solution.py:259
  571.1 4.7 copy-start.5
  580.6 8.0 copy-start.82
  580.6 8.0 copy-start.92
  580.6 403.2 %reduce-scatter.23.cloned.1.call-start = ((), (), s32[]{:S(2)}) async-start(), calls=%async_computation.18 | async-start | bytes 2433024 | tf_op jit(solution)/shard_map/reduce_scatter | solution.py:259
  582.3 7.0 copy-start.43
  591.3 497.0 %reduce-scatter.21.cloned.1.call-start = ((), (), s32[]{:S(2)}) async-start(), calls=%async_computation.17 | async-start | bytes 2433024 | tf_op jit(solution)/shard_map/reduce_scatter | solution.py:259
  630.4 42.3 %copy-start.56 = (bf16[1,128,768]{1,2,0:T(8,128)(2,1)}, bf16[1,128,768]{1,2,0:T(8,128)(2,1)S(1)}, u32[]{:S(2)}) copy-start(bf16[1,128,768]{1,2,0:T(8,128)(2,1)S(1)} %copy.74) | copy-start | bytes 589828
  674.7 554.9 %reduce-scatter.29.cloned.1.call-start = ((), (), s32[]{:S(2)}) async-start(), calls=%async_computation.21 | async-start | bytes 9732096 | tf_op jit(solution)/shard_map/reduce_scatter | solution.py:259
  683.1 688.4 %reduce-scatter.27.cloned.1.call-start = ((), (), s32[]{:S(2)}) async-start(), calls=%async_computation.20 | async-start | bytes 9732096 | tf_op jit(solution)/shard_map/reduce_scatter | solution.py:259
  692.0 4.8 copy-start.97
  712.9 46.8 %copy-start.31 = (f32[1,128,768]{2,1,0:T(8,128)S(1)}, f32[1,128,768]{2,1,0:T(8,128)}, u32[]{:S(2)}) copy-start(f32[1,128,768]{2,1,0:T(8,128)} %copy-done.30) | copy-start | bytes 1179652
  712.9 46.8 %copy-start.33 = (f32[1,128,768]{2,1,0:T(8,128)S(1)}, f32[1,128,768]{2,1,0:T(8,128)}, u32[]{:S(2)}) copy-start(f32[1,128,768]{2,1,0:T(8,128)} %copy-done.32) | copy-start | bytes 1179652
  712.9 46.8 %copy-start.109 = (f32[128]{0:T(128)S(1)}, f32[128]{0:T(128)}, u32[]{:S(2)}) copy-start(f32[128]{0:T(128)} %copy-done.108) | copy-start | bytes 1540
  712.9 46.8 %copy-start.111 = (f32[128]{0:T(128)S(1)}, f32[128]{0:T(128)}, u32[]{:S(2)}) copy-start(f32[128]{0:T(128)} %copy-done.110) | copy-start | bytes 1540
  (77 other events, 153.6 us)
Sparse Core Ops, SparseCore 0:
  10.9 57.0 all-gather.16
  71.0 52.7 all-gather.18
  126.7 52.9 all-gather.14
  182.0 24.6 all-gather.26
  208.4 25.6 all-gather.28
  236.4 25.6 all-gather.32
  264.6 25.6 all-gather.30
  293.2 54.0 all-gather.20
  350.2 62.5 all-gather.22
  415.6 62.4 all-gather.24
  508.1 37.2 reduce-scatter.32
  548.6 38.4 reduce-scatter.36
  590.4 38.4 reduce-scatter.30
  632.0 38.4 reduce-scatter.34
  676.2 99.1 reduce-scatter.24
  782.0 98.0 reduce-scatter.18
  885.8 97.9 reduce-scatter.22
  990.4 97.9 reduce-scatter.20
  1094.8 134.6 reduce-scatter.28
  1236.9 134.6 reduce-scatter.26
where the time goes:
time: 1390 us; the launch traced here: 1380 us
  waiting for transfers between devices  1060 us (76%)
  matrix products  108 us (8%)
  blocking collectives  92 us (7%)
  local copies, waits for them, and re-layouts  84.4 us (6%)
  other arithmetic  21.9 us (2%)
  between operations  16 us (1%)
    reduce_scatter x6, waiting for transfers between devices, local(): lax.psum_scatter(totals, ('dp', 'seq'), scatter_dimension=0, tiled=True)  610 us
    unnamed x24, waiting for transfers between devices  86.6 us
    unnamed x2, blocking collectives  83.2 us
    unnamed x285, local copies, waits for them, and re-layouts  70.7 us
    all_gather x1, waiting for transfers between devices, local(): lax.all_gather(params[5], ('dp', 'seq'), axis=0, tiled=True)  58.7 us
    all_gather x1, waiting for transfers between devices, local(): lax.all_gather(params[4], ('dp', 'seq'), axis=0, tiled=True)  56.1 us
    all_gather x1, waiting for transfers between devices, local(): lax.all_gather(params[2], ('dp', 'seq'), axis=0, tiled=True)  53.2 us
    all_gather x2, waiting for transfers between devices, local(): lax.all_gather(value_rows, 'seq', axis=1, tiled=True)  51.2 us
  transfers between devices with their start and end apart: 20, of which 19 were waited for; matrix products, arithmetic and copies ran while one was open for 13% of the time, Pallas kernels for 0%

commit v1 on v0

--- a/solution.py
+++ b/solution.py
@@ -30,7 +30,7 @@
     return jnp.sum(value.astype(jnp.float32), axis=(0, 1))
 
 
-def local(
+def wide_local(
     hidden_in,
     cotangent,
     segment_ids,
@@ -155,24 +155,6 @@
         act_low = act_full.astype(jnp.bfloat16)
         output_rows = middle + project(act_low, wd) + bd
         outs_rows.append(output_rows.astype(jnp.bfloat16))
-        back_weights = (
-            lax.all_gather(params[0], ("dp", "seq"), axis=0, tiled=True),
-            lax.all_gather(params[1], ("dp", "seq"), axis=0, tiled=True),
-            lax.all_gather(params[2], ("dp", "seq"), axis=0, tiled=True),
-            lax.all_gather(params[3], ("dp", "seq"), axis=0, tiled=True),
-            lax.all_gather(params[4], ("dp", "seq"), axis=0, tiled=True),
-            lax.all_gather(params[5], ("dp", "seq"), axis=0, tiled=True),
-            lax.all_gather(params[6], ("dp", "seq"), axis=0, tiled=True),
-            lax.all_gather(params[7], ("dp", "seq"), axis=0, tiled=True),
-            lax.all_gather(params[8], ("dp", "seq"), axis=0, tiled=True),
-            lax.all_gather(params[9], ("dp", "seq"), axis=0, tiled=True),
-            lax.all_gather(params[10], ("dp", "seq"), axis=0, tiled=True),
-            lax.all_gather(params[11], ("dp", "seq"), axis=0, tiled=True),
-            lax.all_gather(params[12], ("dp", "seq"), axis=0, tiled=True),
-            lax.all_gather(params[13], ("dp", "seq"), axis=0, tiled=True),
-            lax.all_gather(params[14], ("dp", "seq"), axis=0, tiled=True),
-        )
-        wq, wk, wv, wo, wu, wd = back_weights[:6]
         grad_out = cotangent[lower:upper_end].astype(jnp.float32)
         grad_low = grad_out.astype(jnp.bfloat16)
         d_act = project_back(grad_low, wd)
@@ -188,10 +170,7 @@
             .reshape(group_size, shard_rows, HEADS, HEAD_DIM)
         )
         row_dots = jnp.sum(d_attended.astype(jnp.float32) * attended_full, -1).transpose(0, 2, 1)
-        backward_pieces = (
-            lax.all_gather(key_rows, "seq", axis=1, tiled=True),
-            lax.all_gather(value_rows, "seq", axis=1, tiled=True),
-        )
+        backward_pieces = pieces
         backward_count_keys = backward_pieces[0].shape[1]
         backward_key_heads = backward_pieces[0].reshape(
             group_size, backward_count_keys, HEADS, HEAD_DIM
@@ -260,7 +239,368 @@
     return (jnp.concatenate(outs_rows, 0), jnp.concatenate(outs_grads, 0)) + tuple(grads)
 
 
+CORE, NEAR_X, NEAR_Y = 1, 2, 4
+GROUPS = 4
+
+
+def swap(value, bit):
+    return lax.ppermute(value, "seq", [(item, item ^ bit) for item in range(8)])
+
+
+def pick(value, index, axis=0):
+    return lax.dynamic_index_in_dim(value, index, axis, keepdims=False)
+
+
+def in_order(own, other, bit, axis):
+    return jnp.where(
+        bit == 0, jnp.stack([own, other], axis), jnp.stack([other, own], axis)
+    )
+
+
+def spread(value):
+    first, second = value[0], value[1]
+    first = jnp.stack([first, swap(first, NEAR_X)])
+    second = jnp.stack([second, swap(second, NEAR_Y)])
+    first = jnp.concatenate([first, swap(first, NEAR_Y)])
+    second = jnp.concatenate([second, swap(second, NEAR_X)])
+    chip = jnp.stack([first, second])
+    return jnp.stack([chip, swap(chip, CORE)])
+
+
+def collect(value):
+    chip = value[0] + swap(value[1], CORE)
+    first, second = chip[0], chip[1]
+    first = first[:2] + swap(first[2:], NEAR_Y)
+    second = second[:2] + swap(second[2:], NEAR_X)
+    first = first[0] + swap(first[1], NEAR_X)
+    second = second[0] + swap(second[1], NEAR_Y)
+    return jnp.stack([first, second])
+
+
+def column_gather(value, place, count):
+    parts = [value]
+    for shift in range(1, count):
+        parts.append(
+            lax.ppermute(value, "dp", [(item, (item + shift) % count) for item in range(count)])
+        )
+    parts = jnp.stack(parts)
+    ordered = [pick(parts, (place - item) % count) for item in range(count)]
+    return jnp.concatenate(ordered)
+
+
+def column_sum(value, place, count):
+    total = pick(value, place).astype(jnp.float32)
+    for shift in range(1, count):
+        sent = pick(value, (place + shift) % count)
+        total = total + lax.ppermute(
+            sent, "dp", [(item, (item + shift) % count) for item in range(count)]
+        ).astype(jnp.float32)
+    return total
+
+
+def norm_parts(value):
+    center = value - jnp.mean(value, -1, keepdims=True)
+    spread_rows = jnp.mean(center * center, -1, keepdims=True)
+    scale = lax.rsqrt(spread_rows + 1e-05)
+    return center * scale, scale
+
+
+def norm_back(normal, scale, gain, grad):
+    through = grad * gain
+    kept = through - jnp.mean(through, -1, keepdims=True)
+    kept = kept - normal * jnp.mean(through * normal, -1, keepdims=True)
+    rows = tuple(range(grad.ndim - 1))
+    return scale * kept, jnp.sum(grad * normal, rows), jnp.sum(grad, rows)
+
+
+def dot(left, right):
+    return jnp.dot(left, right, preferred_element_type=jnp.float32)
+
+
+def dot_right(left, right):
+    return lax.dot_general(
+        left, right, (((1,), (1,)), ((), ())), preferred_element_type=jnp.float32
+    )
+
+
+def dot_left(left, right):
+    return lax.dot_general(
+        left, right, (((0,), (0,)), ((), ())), preferred_element_type=jnp.float32
+    )
+
+
+def attend_scores(queries, keys, allowed):
+    scores = jnp.einsum("qhd,khd->hqk", queries, keys, preferred_element_type=jnp.float32)
+    return jnp.where(allowed, scores, -1000000000.0)
+
+
+def attend(queries, keys, values, segments):
+    length = queries.shape[0]
+    places = jnp.arange(length)
+    allowed = (places[None, :] <= places[:, None]) & (segments[:, None] == segments[None, :])
+    scores = attend_scores(queries, keys, allowed)
+    top = jnp.max(scores, -1, keepdims=True)
+    expo = jnp.exp(scores - top)
+    total = jnp.sum(expo, -1, keepdims=True)
+    out = jnp.einsum(
+        "hqk,khd->hqd", expo.astype(jnp.bfloat16), values, preferred_element_type=jnp.float32
+    )
+    out = (out / total).transpose(1, 0, 2)
+    return out, top + jnp.log(total), allowed
+
+
+def attend_back(queries, keys, values, allowed, log_total, out, d_out):
+    probs = jnp.exp(attend_scores(queries, keys, allowed) - log_total)
+    row_dots = jnp.sum(d_out.astype(jnp.float32) * out, -1).T[..., None]
+    d_probs = jnp.einsum("qhd,khd->hqk", d_out, values, preferred_element_type=jnp.float32)
+    d_scores = (probs * (d_probs - row_dots)).astype(jnp.bfloat16)
+    d_values = jnp.einsum(
+        "hqk,qhd->khd", probs.astype(jnp.bfloat16), d_out, preferred_element_type=jnp.float32
+    )
+    d_keys = jnp.einsum("hqk,qhd->khd", d_scores, queries, preferred_element_type=jnp.float32)
+    d_queries = jnp.einsum("hqk,khd->qhd", d_scores, keys, preferred_element_type=jnp.float32)
+    return d_queries, d_keys, d_values
+
+
+def plane_local(
+    hidden_in,
+    cotangent,
+    segment_ids,
+    query_weight,
+    key_weight,
+    value_weight,
+    out_weight,
+    up_weight,
+    down_weight,
+    query_bias,
+    value_bias,
+    out_bias,
+    up_bias,
+    down_bias,
+    first_gain,
+    first_shift,
+    second_gain,
+    second_shift,
+):
+    seqs, rows, width = hidden_in.shape
+    plane = lax.axis_size("seq")
+    columns = lax.axis_size("dp")
+    owners = plane * columns
+    share = query_weight.shape[0]
+    ff_share = down_weight.shape[0]
+    hidden = up_weight.shape[1]
+    group_width = width // GROUPS
+    group_heads = HEADS // GROUPS
+    length = rows * plane
+    place = lax.axis_index("seq")
+    column = lax.axis_index("dp")
+    bit_c, bit_x, bit_y = place % 2, (place // 2) % 2, place // 4
+    group = place % GROUPS
+    both = lambda item: jnp.concatenate([item, item])
+
+    sent_qkv = jnp.stack([query_weight, key_weight, value_weight], 1)
+    sent_qkv = sent_qkv.reshape(share, 3, GROUPS, group_width).transpose(2, 0, 1, 3)
+    sent_qkv = both(sent_qkv.reshape(GROUPS, share, 3 * group_width))
+    sent_up = up_weight.reshape(share, columns, plane, ff_share).transpose(2, 0, 1, 3)
+    sent_up = sent_up.reshape(plane, share, columns * ff_share)
+    per_row = -(-segment_ids.size // share)
+    small = jnp.stack(
+        [
+            query_bias,
+            value_bias,
+            out_bias,
+            down_bias,
+            first_gain,
+            first_shift,
+            second_gain,
+            second_shift,
+        ],
+        1,
+    )
+    numbers = segment_ids.astype(jnp.bfloat16).reshape(-1)
+    numbers = jnp.pad(numbers, (0, per_row * share - numbers.size))
+    small = jnp.concatenate(
+        [small, up_bias.reshape(share, -1), numbers.reshape(share, per_row)], -1
+    )
+    bias_columns = ff_share // share
+    small_width = small.shape[1]
+    first_width = 3 * group_width + small_width
+    small = jnp.broadcast_to(small, (plane,) + small.shape)
+    got = lax.all_to_all(
+        jnp.concatenate([sent_qkv, small, sent_up], -1), "seq", 0, 0, tiled=True
+    ).reshape(plane * share, -1)
+    first = column_gather(got[:, :first_width], column, columns)
+    got_up = got[:, first_width:]
+    half = plane * share // 2
+    later = jnp.concatenate([jnp.concatenate([got_up[:half], got_up[half:]], -1), down_weight])
+    first, later = lax.optimization_barrier((first, later))
+    later = column_gather(later, column, columns).reshape(columns, 2 * half, width)
+    w_up = jnp.concatenate(
+        [later[:, :half, : width // 2], later[:, :half, width // 2 :]], 1
+    ).reshape(width, columns * ff_share)
+    w_down = later[:, half:].reshape(columns * ff_share, width)
+    w_out = lax.all_gather(out_weight, ("dp", "seq"), axis=0, tiled=True)
+
+    w_qkv = first[:, : 3 * group_width]
+    small = first[:, 3 * group_width :]
+    bq, bv, bo, bd, gain_one, shift_one, gain_two, shift_two = [
+        small[:, i].astype(jnp.float32) for i in range(8)
+    ]
+    bu = small[:, 8 : 8 + bias_columns].reshape(columns, plane, ff_share)
+    bu = pick(bu, place, 1).reshape(-1).astype(jnp.float32)
+    segments = pick(small[:, 8 + bias_columns :].reshape(columns, plane, -1), column)
+    segments = segments[:, : seqs * rows].reshape(plane, seqs, rows)
+    segments = pick(segments, bit_y, 1).reshape(length)
+
+    mine = pick(hidden_in, bit_y)
+    mine = in_order(mine, swap(pick(hidden_in, 1 - bit_y), NEAR_Y), bit_y, 0)
+    mine = in_order(mine, swap(mine, NEAR_X), bit_x, 1)
+    mine = in_order(mine, swap(mine, CORE), bit_c, 2).reshape(length, width)
+    grads_all = spread(cotangent).reshape(-1, width)
+
+    normal_all, _ = norm_parts(mine.astype(jnp.float32))
+    normed = (normal_all * gain_one + shift_one).astype(jnp.bfloat16)
+    qkv = dot(normed, w_qkv)
+    own_columns = lambda item: lax.dynamic_slice_in_dim(item, group * group_width, group_width)
+    heads = lambda item: item.astype(jnp.bfloat16).reshape(length, group_heads, HEAD_DIM)
+    queries = heads((qkv[:, :group_width] + own_columns(bq)) * 0.125)
+    keys = heads(qkv[:, group_width : 2 * group_width])
+    values = heads(qkv[:, 2 * group_width :] + own_columns(bv))
+    out, log_total, allowed = attend(queries, keys, values, segments)
+
+    attended = out.astype(jnp.bfloat16).reshape(plane, rows, group_width)
+    attended, grads_all = lax.optimization_barrier((attended, grads_all))
+    attended = lax.all_to_all(attended, "seq", 0, 0, tiled=True)
+    attended = attended.reshape(seqs, GROUPS, rows, group_width).transpose(0, 2, 1, 3)
+    attended = attended.reshape(seqs * rows, width)
+    block_in = hidden_in.astype(jnp.float32).reshape(seqs * rows, width)
+    middle = block_in + dot(attended, w_out) + bo
+    normal_two, scale_two = norm_parts(middle)
+    second = (normal_two * gain_two + shift_two).astype(jnp.bfloat16)
+    second_all = spread(second.reshape(seqs, rows, width)).reshape(-1, width)
+
+    upper = dot(second_all, w_up) + bu
+    act, act_back = jax.vjp(jax.nn.gelu, upper)
+    act = act.astype(jnp.bfloat16)
+    d_upper = act_back(dot_right(grads_all, w_down))[0].astype(jnp.bfloat16)
+    halves = lambda item: item.astype(jnp.bfloat16).reshape(2, 2, 4, rows, width)
+    d_second = collect(halves(dot_right(d_upper, w_up))).reshape(seqs * rows, width)
+    down = halves(dot(act, w_down))
+
+    grad_up = dot_left(second_all, d_upper).astype(jnp.bfloat16)
+    grad_up = grad_up.reshape(columns, 2, half, columns * ff_share)
+    grad_down = dot_left(act, grads_all).astype(jnp.bfloat16).reshape(columns, ff_share, width)
+    late = jnp.concatenate(
+        [jnp.concatenate([grad_up[:, 0], grad_up[:, 1]], -1), grad_down], 1
+    )
+    late = column_sum(late, column, columns)
+    grad_down = late[half:]
+    grad_up = jnp.concatenate([late[:half, : width // 2], late[:half, width // 2 :]])
+
+    own_grad = cotangent.astype(jnp.float32).reshape(seqs * rows, width)
+    d_middle, d_gain_two, d_shift_two = norm_back(
+        normal_two, scale_two, gain_two, d_second.astype(jnp.float32)
+    )
+    d_middle = own_grad + d_middle
+    d_branch = d_middle.astype(jnp.bfloat16)
+    grad_out = lax.psum_scatter(
+        dot_left(attended, d_branch).astype(jnp.bfloat16),
+        ("dp", "seq"),
+        scatter_dimension=0,
+        tiled=True,
+    )
+    d_attended = dot_right(d_branch, w_out).astype(jnp.bfloat16)
+    d_attended = d_attended.reshape(seqs, rows, GROUPS, group_width).transpose(0, 2, 1, 3)
+    d_attended = d_attended.reshape(plane, rows, group_width)
+    d_attended = lax.all_to_all(d_attended, "seq", 0, 0, tiled=True)
+    d_attended, down = lax.optimization_barrier((d_attended, down))
+    down = collect(down).reshape(seqs * rows, width)
+    hidden_out = (middle + down.astype(jnp.float32) + bd).astype(jnp.bfloat16)
+    d_attended = d_attended.reshape(length, group_heads, HEAD_DIM)
+    d_queries, d_keys, d_values = attend_back(
+        queries, keys, values, allowed, log_total, out, d_attended
+    )
+    flat = lambda item: item.astype(jnp.bfloat16).reshape(length, group_width)
+    d_queries, d_keys, d_values = flat(d_queries), flat(d_keys), flat(d_values)
+    d_qkv = jnp.concatenate([d_queries * jnp.bfloat16(0.125), d_keys, d_values], -1)
+
+    grad_qkv = dot_left(normed, d_qkv).astype(jnp.bfloat16)
+    d_first = dot_right(d_qkv, w_qkv)
+
+    def placed(item):
+        zeros = jnp.zeros((width,), jnp.float32)
+        return lax.dynamic_update_slice_in_dim(zeros, item, group * group_width, 0)
+
+    total = lambda item: jnp.sum(item.astype(jnp.float32), 0)
+    d_bu = lax.dynamic_update_index_in_dim(
+        jnp.zeros((columns, plane, ff_share), jnp.float32),
+        total(d_upper).reshape(columns, ff_share),
+        place,
+        1,
+    ).reshape(width, bias_columns)
+    terms = [
+        placed(0.125 * total(d_queries)),
+        placed(total(d_values)),
+        total(d_branch),
+        total(own_grad),
+        total(d_first * normal_all),
+        total(d_first),
+        d_gain_two,
+        d_shift_two,
+    ]
+    terms = jnp.concatenate([jnp.stack(terms, 1), d_bu], -1)
+    coarse = lax.reduce_precision(terms, 8, 7)
+    terms = jnp.concatenate([coarse, terms - coarse], -1).astype(jnp.bfloat16)
+    last = jnp.concatenate([grad_qkv, terms], -1)
+    last = column_sum(last.reshape(columns, plane * share, -1), column, columns)
+    terms = last[:, 3 * group_width :]
+    coarse = lax.reduce_precision(terms, 8, 7)
+    last = jnp.concatenate([last[:, : 3 * group_width], coarse, terms - coarse, grad_up], -1)
+    last = lax.all_to_all(
+        last.astype(jnp.bfloat16).reshape(plane, share, -1), "seq", 0, 0, tiled=True
+    ).astype(jnp.float32)
+    grad_qkv = last[..., : 3 * group_width].reshape(2, GROUPS, share, 3, group_width)
+    grad_qkv = jnp.sum(grad_qkv, 0).transpose(2, 1, 0, 3).reshape(3, share, width)
+    grad_up = last[..., -columns * ff_share :].reshape(plane, share, columns, ff_share)
+    grad_up = grad_up.transpose(1, 2, 0, 3).reshape(share, hidden)
+    terms = jnp.sum(last[..., 3 * group_width : -columns * ff_share], 0)
+    terms = jnp.sum(terms.reshape(share, 4, -1), 1)
+    g_bq, g_bv, g_bo, g_bd, g_g1, g_s1, g_g2, g_s2 = [terms[:, i] for i in range(8)]
+    g_bu = terms[:, 8:].reshape(-1)
+
+    d_first = d_first.astype(jnp.bfloat16).reshape(2, 2, 2, rows, width)
+    d_first = pick(d_first, bit_c, 2) + swap(pick(d_first, 1 - bit_c, 2), CORE)
+    d_first = pick(d_first, bit_x, 1) + swap(pick(d_first, 1 - bit_x, 1), NEAR_X)
+    d_first = in_order(pick(d_first, bit_y), swap(pick(d_first, 1 - bit_y), NEAR_Y), bit_y, 0)
+    d_first = d_first.reshape(seqs * rows, width).astype(jnp.float32)
+    normal_one, scale_one = norm_parts(block_in)
+    d_input, _, _ = norm_back(normal_one, scale_one, gain_one, d_first)
+    grad_input = (d_middle + d_input).reshape(seqs, rows, width)
+
+    return (
+        hidden_out.reshape(seqs, rows, width),
+        grad_input,
+        grad_qkv[0],
+        grad_qkv[1],
+        grad_qkv[2],
+        grad_out.astype(jnp.float32),
+        grad_up,
+        grad_down,
+        g_bq,
+        g_bv,
+        g_bo,
+        g_bu,
+        g_bd,
+        g_g1,
+        g_s1,
+        g_g2,
+        g_s2,
+    )
+
+
 def solution(mesh):
+    plane = mesh.shape["seq"] == 8 and HEADS % 4 == 0
+    body = plane_local if plane else wide_local
     placed = (
         P("dp", "seq", None),
         P("dp", "seq", None),
@@ -282,7 +622,7 @@
         P(("dp", "seq")),
     )
     return jax.shard_map(
-        local,
+        body,
         mesh=mesh,
         in_specs=placed,
         out_specs=(

time: 1390 us -> 353 us (0.25)
  waiting for transfers between devices: 1060 us -> 108 us
  blocking collectives: 92 us -> 11 us
  starting transfers between devices: 1.21 us -> 59.2 us
  matrix products: 108 us -> 51.1 us
  local copies, waits for them, and re-layouts: 84.4 us -> 54.3 us
  other arithmetic: 21.9 us -> 48.6 us
    reduce_scatter x6 -> x1, waiting for transfers between devices: 610 us -> 7.63 us  [plane_local(): lax.psum_scatter(dot_left(attended, d_branch).astype(jnp.bfloat16), ('dp'...]
    all_gather x10 -> x1, waiting for transfers between devices: 358 us -> 0.02 us  [plane_local(): w_out = lax.all_gather(out_weight, ('dp', 'seq'), axis=0, tiled=True)]
    ppermute x0 -> x38, waiting for transfers between devices: none -> 91.8 us  [the longest x26 33.4 us: swap(): return lax.ppermute(value, 'seq', [(item, item ^ bit) for item in range(8)])]
    unnamed x24 -> x2, waiting for transfers between devices: 86.6 us -> 0.7 us
    unnamed x2 -> x0, blocking collectives: 83.2 us -> none
    unnamed x285 -> x111, local copies, waits for them, and re-layouts: 70.7 us -> 4.5 us
    dot_general x48 -> x18, matrix products: 108 us -> 51.1 us  [the longest x4 10.8 us: dot(): return jnp.dot(left, right, preferred_element_type=jnp.float32)]
    ppermute x0 -> x38, starting transfers between devices: none -> 47.9 us  [the longest x26 26.7 us: swap(): return lax.ppermute(value, 'seq', [(item, item ^ bit) for item in range(8)])]
  transfers between devices with their start and end apart: 20 -> 43, of which waited for: 19 -> 21; matrix products, arithmetic and copies ran while one was open for 13% -> 38% of each run, Pallas kernels for 0% -> 0%
where the time goes in v1:
time: 353 us; the launch traced here: 348 us
  waiting for transfers between devices  108 us (31%)
  starting transfers between devices  59.2 us (17%)
  local copies, waits for them, and re-layouts  54.3 us (15%)
  matrix products  51.1 us (14%)
  other arithmetic  48.6 us (14%)
  between operations  15.8 us (4%)
  blocking collectives  11 us (3%)
    ppermute x26, waiting for transfers between devices, swap(): return lax.ppermute(value, 'seq', [(item, item ^ bit) for item in range(8)])  33.4 us
    ppermute x6, waiting for transfers between devices, column_sum(): lax.ppermute(sent, 'dp', [(item, (item + shift) % count) for item in rang...  29.9 us
    ppermute x6, waiting for transfers between devices, column_gather(): lax.ppermute(value, 'dp', [(item, (item + shift) % count) for item in ran...  28.5 us
    ppermute x26, starting transfers between devices, swap(): return lax.ppermute(value, 'seq', [(item, item ^ bit) for item in range(8)])  26.7 us
    ppermute x6, starting transfers between devices, column_gather(): lax.ppermute(value, 'dp', [(item, (item + shift) % count) for item in ran...  13.1 us
    all_to_all x1, blocking collectives, plane_local(): attended = lax.all_to_all(attended, 'seq', 0, 0, tiled=True)  11 us
    dot_general x4, matrix products, dot(): return jnp.dot(left, right, preferred_element_type=jnp.float32)  10.8 us
    dot_general x1, matrix products, attend_back(): jnp.einsum('hqk,qhd->khd', probs.astype(jnp.bfloat16), d_out, preferred_e...  9.15 us
  transfers between devices with their start and end apart: 43, of which 21 were waited for; matrix products, arithmetic and copies ran while one was open for 38% of the time, Pallas kernels for 0%

profile of v1, /device:TPU:0, one launch (start us, length us, event | category | flops | bytes accessed | tf_op | source)
XLA Modules:
  0.0 348.4 jit_solution(13003685317384684668)
XLA Ops:
  9.0 3.0 collective-permute-start.3
  13.1 1.6 collective-permute-start.6
  27.2 3.5 all-to-all-start
  30.6 1.9 collective-permute-start.8
  33.4 1.5 collective-permute-start.4
  35.6 7.6 %collective-permute-done.8 = bf16[128,768]{1,0:T(8,128)(2,1)S(1)} collective-permute-done((bf16[128,768]{1,0:T(8,128)(2,1)S(1)}, bf16[128,768]{1,0:T(8,128)(2,1)S(1)}, u32[]{:S(2)}, u32[]{:S(2)}) %collective-permute-start.8) | collective-permute-done | bytes 196640 | tf_op jit(solution)/shard_map/ppermute | solution.py:247
  44.0 2.7 collective-permute-start.1
  46.7 1.6 collective-permute-start
  48.3 2.4 collective-permute-start.2
  50.8 1.6 pad_maximum_fusion.22
  52.4 11.7 %collective-permute-done.1 = bf16[192,599]{1,0:T(8,128)(2,1)S(1)} collective-permute-done((bf16[192,599]{1,0:T(8,128)(2,1)S(1)}, bf16[192,599]{1,0:T(8,128)(2,1)S(1)}, u32[]{:S(2)}, u32[]{:S(2)}) %collective-permute-start.1) | collective-permute-done | bytes 230048 | tf_op jit(solution)/shard_map/ppermute | solution.py:284
  64.2 1.6 collective-permute-start.9
  71.3 3.8 %collective-permute-done.9 = bf16[2,128,768]{2,1,0:T(8,128)(2,1)} collective-permute-done((bf16[2,128,768]{2,1,0:T(8,128)(2,1)}, bf16[2,128,768]{2,1,0:T(8,128)(2,1)}, u32[]{:S(2)}, u32[]{:S(2)}) %collective-permute-start.9) | collective-permute-done | bytes 393248 | tf_op jit(solution)/shard_map/ppermute | solution.py:247
  76.2 1.9 fusion.87
  82.5 2.2 select_reduce_fusion
  84.8 4.3 %fusion = f32[3,1024]{1,0:T(4,128)S(1)} fusion(f32[3,1024,1024]{1,2,0:T(8,128)S(1)} %get-tuple-element.124, f32[3,1024]{1,0:T(4,128)S(1)} %get-tuple-element.123, pred[1024,1024]{0,1:T(8,128)(4,1)} %copy-done.4), kind=kLoop, calls=%fused_computation.3 | loop fusion | flops 9434112 | bytes 13656064 | tf_op jit(solution)/shard_map/reduce_sum | solution.py:344
  89.3 5.3 %fusion.101 = (bf16[1024,3,64]{0,2,1:T(8,128)(2,1)S(1)}, f32[1024,3,64]{0,2,1:T(8,128)}) fusion(f32[1024,3]{0,1:T(4,128)S(1)} %bitcast.434, bf16[1024,3,64]{0,2,1:T(8,128)(2,1)S(1)} %bitcast.427, f32[3,1024,1024]{1,2,0:T(8,128)S(1)} %get-tuple-element.124, f32[3,1024]{1,0:T(4,128)S(1)} %get-tuple-element.123, pred[1024,1024]{0,1:T(8,128)(4,1)} %copy-done.4), kind=kOutput, calls=%fused_computation.259 | convolution fusion | flops 412483584 | bytes 15228928 | tf_op jit(solution)/shard_map/hqk,khd->hqd/dot_general | solution.py:345
  94.8 3.4 pad_maximum_fusion
  98.3 11.0 %all_to_all.20 = bf16[8,128,192]{1,2,0:T(8,128)(2,1)S(1)} all-to-all(bf16[8,128,192]{1,2,0:T(8,128)(2,1)S(1)} %copy.167), channel_id=1, replica_groups=mesh['dp'=4,'seq'=8] {'seq'}, dimensions={0} | all-to-all | bytes 786432 | tf_op jit(solution)/shard_map/all_to_all | solution.py:473
  109.7 2.0 fusion.102
  114.0 5.3 %collective-permute-done.16 = bf16[128,768]{1,0:T(8,128)(2,1)S(1)} collective-permute-done((bf16[128,768]{1,0:T(8,128)(2,1)S(1)}, bf16[128,768]{1,0:T(8,128)(2,1)S(1)}, u32[]{:S(2)}, u32[]{:S(2)}) %collective-permute-start.16) | collective-permute-done | bytes 196640 | tf_op jit(solution)/shard_map/ppermute | solution.py:247
  122.7 3.7 %collective-permute-start.12 = (bf16[192,768]{1,0:T(8,128)(2,1)}, bf16[192,768]{1,0:T(8,128)(2,1)}, u32[]{:S(2)}, u32[]{:S(2)}) collective-permute-start(bf16[192,768]{1,0:T(8,128)(2,1)} %pad_maximum_fusion.22), channel_id=1, source_target_pairs={{0,16},{8,24},{16,0},{24,8},{1,17},{9,25},{17,1},{25,9},{2,18},{10... | collective-permute-start | bytes 884744 | tf_op jit(solution)/shard_map/ppermute | solution.py:284
  126.4 2.0 collective-permute-start.11
  134.2 16.8 %collective-permute-done.12 = bf16[192,768]{1,0:T(8,128)(2,1)} collective-permute-done((bf16[192,768]{1,0:T(8,128)(2,1)}, bf16[192,768]{1,0:T(8,128)(2,1)}, u32[]{:S(2)}, u32[]{:S(2)}) %collective-permute-start.12) | collective-permute-done | bytes 294944 | tf_op jit(solution)/shard_map/ppermute | solution.py:284
  154.4 1.8 fusion.103
  156.2 1.7 pad_maximum_fusion.1
  157.9 3.8 %convert_reduce_fusion = (f32[384]{0:T(512)S(1)}, bf16[2048,384]{1,0:T(8,128)(2,1)S(1)}, f32[2048,384]{1,0:T(8,128)S(1)}) fusion(f32[2048,384]{1,0:T(8,128)S(1)} %fusion.103, f32[384]{0:T(512)S(1)} %reshape.675, bf16[2048,768]{1,0:T(8,128)(2,1)S(1)} %bitcast.364, bf16[768,384]{1,0:T(8,128)(2,1)S(1)} %bitcast.418), kind=kOutput, calls=%fused_computation.28 | convolution fusion | flops 1226047104 | bytes 11602944 | tf_op jit(solution)/shard_map/dot_general | solution.py:317
  161.7 1.8 convolution_convert_fusion.5
  163.5 1.8 convolution_convert_fusion.1
  166.8 1.6 convolution_convert_fusion.4
  170.7 3.8 %collective-permute-start.37 = (bf16[192,768]{1,0:T(8,128)(2,1)}, bf16[192,768]{1,0:T(8,128)(2,1)}, u32[]{:S(2)}, u32[]{:S(2)}) collective-permute-start(bf16[192,768]{1,0:T(8,128)(2,1)} %get-tuple-element.67), channel_id=1, source_target_pairs={{0,24},{8,0},{16,8},{24,16},{1,25},{9,1},{17,9},{25,17},{2,26},{10... | collective-permute-start | bytes 884744 | tf_op jit(solution)/shard_map/ppermute | solution.py:295
  174.5 4.0 %convolution_convert_fusion = bf16[2048,768]{1,0:T(8,128)(2,1)} fusion(bf16[384,768]{1,0:T(8,128)(2,1)S(1)} %bitcast.417, f32[2048,384]{1,0:T(8,128)S(1)} %get-tuple-element.129), kind=kOutput, calls=%fused_computation.15 | convolution fusion | flops 1216610304 | bytes 6881280 | tf_op jit(solution)/shard_map/dot_general | solution.py:317
  179.5 1.8 add.337
  183.9 5.5 %collective-permute-done.37 = bf16[192,768]{1,0:T(8,128)(2,1)} collective-permute-done((bf16[192,768]{1,0:T(8,128)(2,1)}, bf16[192,768]{1,0:T(8,128)(2,1)}, u32[]{:S(2)}, u32[]{:S(2)}) %collective-permute-start.37) | collective-permute-done | bytes 294944 | tf_op jit(solution)/shard_map/ppermute | solution.py:295
  189.4 9.3 %collective-permute-done.36 = bf16[192,768]{1,0:T(8,128)(2,1)} collective-permute-done((bf16[192,768]{1,0:T(8,128)(2,1)}, bf16[192,768]{1,0:T(8,128)(2,1)}, u32[]{:S(2)}, u32[]{:S(2)}) %collective-permute-start.36) | collective-permute-done | bytes 294944 | tf_op jit(solution)/shard_map/ppermute | solution.py:295
  198.7 2.2 fusion.92
  203.7 3.7 %collective-permute-done.23 = bf16[128,768]{1,0:T(8,128)(2,1)S(1)} collective-permute-done((bf16[128,768]{1,0:T(8,128)(2,1)S(1)}, bf16[128,768]{1,0:T(8,128)(2,1)S(1)}, u32[]{:S(2)}, u32[]{:S(2)}) %collective-permute-start.23) | collective-permute-done | bytes 196640 | tf_op jit(solution)/shard_map/ppermute | solution.py:247
  211.1 4.1 %all-to-all-start.2 = ((bf16[8,128,192]{1,2,0:T(8,128)(2,1)}), bf16[8,128,192]{1,2,0:T(8,128)(2,1)}, u32[]{:S(2)}, u32[]{:S(2)}) async-start(bf16[8,128,192]{1,2,0:T(8,128)(2,1)} %bitcast.87), calls=%async_computation.2 | async-start | bytes 786432 | tf_op jit(solution)/shard_map/all_to_all | solution.py:515
  217.0 1.5 convolution_convert_fusion.2
  218.5 5.0 %all-to-all-done.2 = bf16[8,128,192]{1,2,0:T(8,128)(2,1)} async-done(((bf16[8,128,192]{1,2,0:T(8,128)(2,1)}), bf16[8,128,192]{1,2,0:T(8,128)(2,1)}, u32[]{:S(2)}, u32[]{:S(2)}) %all-to-all-start.2) | async-done | bytes 393248 | tf_op jit(solution)/shard_map/all_to_all | solution.py:515
  227.1 9.2 %convert_reduce_fusion.3 = (f32[3,64]{1,0:T(4,128)}, bf16[3,64,1024]{2,1,0:T(8,128)(2,1)}) fusion(bf16[1024,3,64]{0,2,1:T(8,128)(2,1)} %reshape.655, f32[3,1024,1024]{1,2,0:T(8,128)} %copy-done, f32[3,1024]{1,0:T(4,128)} %log_add_fusion, pred[1024,1024]{0,1:T(8,128)(4,1)S(1)} %copy-done.5), kind=kOutput, calls=%fused_computation.100 | convolution fusion | flops 412680000 | bytes 14430976 | tf_op jit(solution)/shard_map/hqk,qhd->khd/dot_general | solution.py:357
  236.2 7.2 %multiply_convert_fusion = bf16[3,1024,1024]{1,2,0:T(8,128)(2,1)S(1)} fusion(f32[3,1024,1024]{1,2,0:T(8,128)} %copy-done, f32[3,1024]{1,0:T(4,128)S(1)} %bitcast.435, f32[3,1024]{1,0:T(4,128)S(1)} %copy-done.41, pred[1024,1024]{0,1:T(8,128)(4,1)S(1)} %copy-done.5, bf16[1024,3,64]{0,2,1:T(8,128)(2,1)S(1)} %copy-done.19, bf16[1024,3,64]{0,2,1:T(8,128)(2,1)S(1)} %bitcast.428), kind=kOutput, calls=%fused_computation | convolution fusion | flops 418381824 | bytes 20733952 | tf_op jit(solution)/shard_map/qhd,khd->hqk/dot_general | solution.py:355
  243.4 2.0 convolution_convert_fusion.6
  247.8 3.1 fusion.89
  253.8 1.5 copy.179
  255.5 4.0 %collective-permute-start.34 = (bf16[192,600]{1,0:T(8,128)(2,1)S(1)}, bf16[192,600]{1,0:T(8,128)(2,1)S(1)}, u32[]{:S(2)}, u32[]{:S(2)}) collective-permute-start(bf16[192,600]{1,0:T(8,128)(2,1)S(1)} %get-tuple-element.76), channel_id=1, source_target_pairs={{0,24},{8,0},{16,8},{24,16},{1,25},{9,1},{17,9},{25,17},{2,26},{10... | collective-permute-start | bytes 691208 | tf_op jit(solution)/shard_map/ppermute | solution.py:295
  259.5 2.1 dynamic-slice_bitcast_fusion
  261.5 2.7 slice_bitcast_fusion
  266.2 2.1 collective-permute-done.34
  268.2 11.6 %collective-permute-done.33 = bf16[192,600]{1,0:T(8,128)(2,1)S(1)} collective-permute-done((bf16[192,600]{1,0:T(8,128)(2,1)S(1)}, bf16[192,600]{1,0:T(8,128)(2,1)S(1)}, u32[]{:S(2)}, u32[]{:S(2)}) %collective-permute-start.33) | collective-permute-done | bytes 230432 | tf_op jit(solution)/shard_map/ppermute | solution.py:295
  281.1 3.7 %all-to-all-start.3 = ((bf16[8,24,1008]{2,1,0:T(8,128)(2,1)}), bf16[8,24,1008]{2,1,0:T(8,128)(2,1)S(1)}, u32[]{:S(2)}, u32[]{:S(2)}) async-start(bf16[8,24,1008]{2,1,0:T(8,128)(2,1)} %pad_maximum_fusion.21), calls=%async_computation.3 | async-start | bytes 786432 | tf_op jit(solution)/shard_map/all_to_all | solution.py:559
  284.8 1.5 bitcast_add_fusion.1
  287.0 2.1 collective-permute-start.30
  289.1 1.7 slice.384
  290.8 3.2 all-to-all-done.3
  297.1 1.9 reshape.666
  299.9 2.2 reshape.664
  302.1 1.4 reduce_sum.237
  311.9 7.6 %reduce-scatter.2.cloned.1.call-done = bf16[24,768]{1,0:T(8,128)(2,1)} async-done(((bf16[768,768]{1,0:T(8,128)(2,1)}), bf16[24,768]{1,0:T(8,128)(2,1)}) %reduce-scatter.2.cloned.1.call-update) | async-done | bytes 36880 | tf_op jit(solution)/shard_map/reduce_scatter | solution.py:506
  321.3 2.0 bitcast_add_fusion
  323.5 1.5 collective-permute-start.25
  327.6 5.1 %collective-permute-done.25 = bf16[2,128,768]{2,1,0:T(8,128)(2,1)S(1)} collective-permute-done((bf16[2,128,768]{2,1,0:T(8,128)(2,1)S(1)}, bf16[2,128,768]{2,1,0:T(8,128)(2,1)S(1)}, u32[]{:S(2)}, u32[]{:S(2)}) %collective-permute-start.25) | collective-permute-done | bytes 393248 | tf_op jit(solution)/shard_map/ppermute | solution.py:247
  334.6 1.5 collective-permute-start.26
  336.2 3.6 %collective-permute-done.28 = bf16[128,768]{1,0:T(8,128)(2,1)S(1)} collective-permute-done((bf16[128,768]{1,0:T(8,128)(2,1)S(1)}, bf16[128,768]{1,0:T(8,128)(2,1)S(1)}, u32[]{:S(2)}, u32[]{:S(2)}) %collective-permute-start.28) | collective-permute-done | bytes 196640 | tf_op jit(solution)/shard_map/ppermute | solution.py:247
  (346 shorter events, 92.2 us)
Async XLA Ops:
  7.2 18.5 %copy-start.25 = (bf16[24,3072]{1,0:T(8,128)(2,1)S(1)}, bf16[24,3072]{1,0:T(8,128)(2,1)}, u32[]{:S(2)}) copy-start(bf16[24,3072]{1,0:T(8,128)(2,1)} %param.25) | copy-start | bytes 442372
  7.2 102.5 %all-gather.2.cloned.1.call-start = ((), (), s32[]{:S(2)}) async-start(), calls=%async_computation.5 | async-start | bytes 1216512 | tf_op jit(solution)/shard_map/all_gather | solution.py:442
  9.0 23.5 %collective-permute-start.3 = (bf16[128,768]{1,0:T(8,128)(2,1)S(1)}, bf16[128,768]{1,0:T(8,128)(2,1)S(1)}, u32[]{:S(2)}, u32[]{:S(2)}) collective-permute-start(bf16[128,768]{1,0:T(8,128)(2,1)S(1)} %get-tuple-element.102), channel_id=1, source_target_pairs={{0,4},{1,5},{2,6},{3,7},{4,0},{5,1},{6,2},{7,3},{8,12},{9,13},{10,... | collective-permute-start | bytes 589832 | tf_op jit(solution)/shard_map/ppermute | solution.py:247
  13.1 21.7 %collective-permute-start.6 = (bf16[128,768]{1,0:T(8,128)(2,1)S(1)}, bf16[128,768]{1,0:T(8,128)(2,1)S(1)}, u32[]{:S(2)}, u32[]{:S(2)}) collective-permute-start(bf16[128,768]{1,0:T(8,128)(2,1)S(1)} %get-tuple-element.98), channel_id=1, source_target_pairs={{0,2},{1,3},{2,0},{3,1},{4,6},{5,7},{6,4},{7,5},{8,10},{9,11},{10,... | collective-permute-start | bytes 589832 | tf_op jit(solution)/shard_map/ppermute | solution.py:247
  27.2 16.8 %all-to-all-start = ((bf16[8,24,983]{2,1,0:T(8,128)(2,1)}), bf16[8,24,983]{2,1,0:T(8,128)(2,1)S(1)}, u32[]{:S(2)}, u32[]{:S(2)}) async-start(bf16[8,24,983]{2,1,0:T(8,128)(2,1)} %pad_maximum_fusion.14), calls=%async_computation | async-start | bytes 786432 | tf_op jit(solution)/shard_map/all_to_all | solution.py:429
  30.6 12.6 %collective-permute-start.8 = (bf16[128,768]{1,0:T(8,128)(2,1)S(1)}, bf16[128,768]{1,0:T(8,128)(2,1)S(1)}, u32[]{:S(2)}, u32[]{:S(2)}) collective-permute-start(bf16[128,768]{1,0:T(8,128)(2,1)S(1)} %get-tuple-element.99), channel_id=1, source_target_pairs={{0,4},{1,5},{2,6},{3,7},{4,0},{5,1},{6,2},{7,3},{8,12},{9,13},{10,... | collective-permute-start | bytes 589832 | tf_op jit(solution)/shard_map/ppermute | solution.py:247
  33.4 35.1 %collective-permute-start.4 = (bf16[2,128,768]{2,1,0:T(8,128)(2,1)}, bf16[2,128,768]{2,1,0:T(8,128)(2,1)S(1)}, u32[]{:S(2)}, u32[]{:S(2)}) collective-permute-start(bf16[2,128,768]{2,1,0:T(8,128)(2,1)} %maximum_select_fusion.4), channel_id=1, source_target_pairs={{0,2},{1,3},{2,0},{3,1},{4,6},{5,7},{6,4},{7,5},{8,10},{9,11},{10,... | collective-permute-start | bytes 1179656 | tf_op jit(solution)/shard_map/ppermute | solution.py:247
  34.9 35.3 %collective-permute-start.7 = (bf16[2,128,768]{2,1,0:T(8,128)(2,1)S(1)}, bf16[2,128,768]{2,1,0:T(8,128)(2,1)}, u32[]{:S(2)}, u32[]{:S(2)}) collective-permute-start(bf16[2,128,768]{2,1,0:T(8,128)(2,1)S(1)} %pad_maximum_fusion.15), channel_id=1, source_target_pairs={{0,4},{1,5},{2,6},{3,7},{4,0},{5,1},{6,2},{7,3},{8,12},{9,13},{10,... | collective-permute-start | bytes 1179656 | tf_op jit(solution)/shard_map/ppermute | solution.py:247
  44.0 20.1 %collective-permute-start.1 = (bf16[192,599]{1,0:T(8,128)(2,1)S(1)}, bf16[192,599]{1,0:T(8,128)(2,1)S(1)}, u32[]{:S(2)}, u32[]{:S(2)}) collective-permute-start(bf16[192,599]{1,0:T(8,128)(2,1)S(1)} %get-tuple-element.106), channel_id=1, source_target_pairs={{0,16},{8,24},{16,0},{24,8},{1,17},{9,25},{17,1},{25,9},{2,18},{10... | collective-permute-start | bytes 690056 | tf_op jit(solution)/shard_map/ppermute | solution.py:284
  46.7 19.1 %collective-permute-start = (bf16[192,599]{1,0:T(8,128)(2,1)S(1)}, bf16[192,599]{1,0:T(8,128)(2,1)S(1)}, u32[]{:S(2)}, u32[]{:S(2)}) collective-permute-start(bf16[192,599]{1,0:T(8,128)(2,1)S(1)} %get-tuple-element.106), channel_id=1, source_target_pairs={{0,8},{8,16},{16,24},{24,0},{1,9},{9,17},{17,25},{25,1},{2,10},{10... | collective-permute-start | bytes 690056 | tf_op jit(solution)/shard_map/ppermute | solution.py:284
  48.3 17.5 %collective-permute-start.2 = (bf16[192,599]{1,0:T(8,128)(2,1)S(1)}, bf16[192,599]{1,0:T(8,128)(2,1)S(1)}, u32[]{:S(2)}, u32[]{:S(2)}) collective-permute-start(bf16[192,599]{1,0:T(8,128)(2,1)S(1)} %get-tuple-element.106), channel_id=1, source_target_pairs={{0,24},{8,0},{16,8},{24,16},{1,25},{9,1},{17,9},{25,17},{2,26},{10... | collective-permute-start | bytes 690056 | tf_op jit(solution)/shard_map/ppermute | solution.py:284
  64.2 11.0 %collective-permute-start.9 = (bf16[2,128,768]{2,1,0:T(8,128)(2,1)}, bf16[2,128,768]{2,1,0:T(8,128)(2,1)}, u32[]{:S(2)}, u32[]{:S(2)}) collective-permute-start(bf16[2,128,768]{2,1,0:T(8,128)(2,1)} %pad_maximum_fusion.16), channel_id=1, source_target_pairs={{0,2},{1,3},{2,0},{3,1},{4,6},{5,7},{6,4},{7,5},{8,10},{9,11},{10,... | collective-permute-start | bytes 1179656 | tf_op jit(solution)/shard_map/ppermute | solution.py:247
  66.2 14.9 %copy-start.6 = (bf16[768,599]{1,0:T(8,128)(2,1)}, bf16[768,599]{1,0:T(8,128)(2,1)S(1)}, u32[]{:S(2)}) copy-start(bf16[768,599]{1,0:T(8,128)(2,1)S(1)} %pad_maximum_fusion.9) | copy-start | bytes 2760196
  68.4 14.1 %copy-start.4 = (pred[1024,1024]{0,1:T(8,128)(4,1)}, pred[1024,1024]{0,1:T(8,128)(4,1)S(1)}, u32[]{:S(2)}) copy-start(pred[1024,1024]{0,1:T(8,128)(4,1)S(1)} %fusion.9) | copy-start | bytes 3145732
  68.6 9.7 %collective-permute-start.5 = (bf16[2,2,128,768]{3,2,0,1:T(8,128)(2,1)S(1)}, bf16[2,2,128,768]{3,2,0,1:T(8,128)(2,1)S(1)}, u32[]{:S(2)}, u32[]{:S(2)}) collective-permute-start(bf16[2,2,128,768]{3,2,0,1:T(8,128)(2,1)S(1)} %maximum_select_fusion.2), channel_id=1, source_target_pairs={{0,1},{1,0},{2,3},{3,2},{4,5},{5,4},{6,7},{7,6},{8,9},{9,8},{10,11... | collective-permute-start | bytes 2359304 | tf_op jit(solution)/shard_map/ppermute | solution.py:247
  70.2 10.0 %copy-start.28 = (f32[768]{0:T(1024)}, f32[768]{0:T(1024)S(1)}, u32[]{:S(2)}) copy-start(f32[768]{0:T(1024)S(1)} %get-tuple-element.38) | copy-start | bytes 9220
  78.1 16.6 %collective-permute-start.10 = (bf16[2,4,128,768]{3,2,1,0:T(8,128)(2,1)}, bf16[2,4,128,768]{3,2,1,0:T(8,128)(2,1)}, u32[]{:S(2)}, u32[]{:S(2)}) collective-permute-start(bf16[2,4,128,768]{3,2,1,0:T(8,128)(2,1)} %get-tuple-element.65), channel_id=1, source_target_pairs={{0,1},{1,0},{2,3},{3,2},{4,5},{5,4},{6,7},{7,6},{8,9},{9,8},{10,11... | collective-permute-start | bytes 4718600 | tf_op jit(solution)/shard_map/ppermute | solution.py:247
  94.7 15.0 %copy-start.3 = (bf16[2,128,768]{2,1,0:T(8,128)(2,1)S(1)}, bf16[2,128,768]{2,1,0:T(8,128)(2,1)}, u32[]{:S(2)}) copy-start(bf16[2,128,768]{2,1,0:T(8,128)(2,1)} %param.18) | copy-start | bytes 1179652
  94.8 15.0 %copy-start.50 = (f32[768]{0:T(1024)S(1)}, f32[768]{0:T(1024)}, u32[]{:S(2)}) copy-start(f32[768]{0:T(1024)} %get-tuple-element.36) | copy-start | bytes 9220
  98.2 14.3 %copy-start.26 = (f32[768]{0:T(1024)S(1)}, f32[768]{0:T(1024)}, u32[]{:S(2)}) copy-start(f32[768]{0:T(1024)} %get-tuple-element.35) | copy-start | bytes 9220
  98.2 14.3 %copy-start.36 = (f32[768]{0:T(1024)S(1)}, f32[768]{0:T(1024)}, u32[]{:S(2)}) copy-start(f32[768]{0:T(1024)} %get-tuple-element.34) | copy-start | bytes 9220
  109.7 9.7 %copy-start.17 = (bf16[2,128,4,192]{1,0,3,2:T(2,128)(2,1)}, bf16[2,128,4,192]{1,0,3,2:T(2,128)(2,1)S(1)}, u32[]{:S(2)}) copy-start(bf16[2,128,4,192]{1,0,3,2:T(2,128)(2,1)S(1)} %copy.168) | copy-start | bytes 1179652
  112.8 6.5 %collective-permute-start.16 = (bf16[128,768]{1,0:T(8,128)(2,1)S(1)}, bf16[128,768]{1,0:T(8,128)(2,1)S(1)}, u32[]{:S(2)}, u32[]{:S(2)}) collective-permute-start(bf16[128,768]{1,0:T(8,128)(2,1)S(1)} %get-tuple-element.95), channel_id=1, source_target_pairs={{0,4},{1,5},{2,6},{3,7},{4,0},{5,1},{6,2},{7,3},{8,12},{9,13},{10,... | collective-permute-start | bytes 589832 | tf_op jit(solution)/shard_map/ppermute | solution.py:247
  113.4 6.7 %collective-permute-start.14 = (bf16[128,768]{1,0:T(8,128)(2,1)S(1)}, bf16[128,768]{1,0:T(8,128)(2,1)S(1)}, u32[]{:S(2)}, u32[]{:S(2)}) collective-permute-start(bf16[128,768]{1,0:T(8,128)(2,1)S(1)} %get-tuple-element.96), channel_id=1, source_target_pairs={{0,2},{1,3},{2,0},{3,1},{4,6},{5,7},{6,4},{7,5},{8,10},{9,11},{10,... | collective-permute-start | bytes 589832 | tf_op jit(solution)/shard_map/ppermute | solution.py:247
  119.4 9.8 %collective-permute-start.17 = (bf16[2,128,768]{2,1,0:T(8,128)(2,1)S(1)}, bf16[2,128,768]{2,1,0:T(8,128)(2,1)S(1)}, u32[]{:S(2)}, u32[]{:S(2)}) collective-permute-start(bf16[2,128,768]{2,1,0:T(8,128)(2,1)S(1)} %pad_maximum_fusion.18), channel_id=1, source_target_pairs={{0,2},{1,3},{2,0},{3,1},{4,6},{5,7},{6,4},{7,5},{8,10},{9,11},{10,... | collective-permute-start | bytes 1179656 | tf_op jit(solution)/shard_map/ppermute | solution.py:247
  120.2 9.7 %collective-permute-start.15 = (bf16[2,128,768]{2,1,0:T(8,128)(2,1)S(1)}, bf16[2,128,768]{2,1,0:T(8,128)(2,1)S(1)}, u32[]{:S(2)}, u32[]{:S(2)}) collective-permute-start(bf16[2,128,768]{2,1,0:T(8,128)(2,1)S(1)} %pad_maximum_fusion.17), channel_id=1, source_target_pairs={{0,4},{1,5},{2,6},{3,7},{4,0},{5,1},{6,2},{7,3},{8,12},{9,13},{10,... | collective-permute-start | bytes 1179656 | tf_op jit(solution)/shard_map/ppermute | solution.py:247
  121.9 12.3 %collective-permute-start.13 = (bf16[192,768]{1,0:T(8,128)(2,1)}, bf16[192,768]{1,0:T(8,128)(2,1)}, u32[]{:S(2)}, u32[]{:S(2)}) collective-permute-start(bf16[192,768]{1,0:T(8,128)(2,1)} %pad_maximum_fusion.22), channel_id=1, source_target_pairs={{0,24},{8,0},{16,8},{24,16},{1,25},{9,1},{17,9},{25,17},{2,26},{10... | collective-permute-start | bytes 884744 | tf_op jit(solution)/shard_map/ppermute | solution.py:284
  122.7 28.3 %collective-permute-start.12 = (bf16[192,768]{1,0:T(8,128)(2,1)}, bf16[192,768]{1,0:T(8,128)(2,1)}, u32[]{:S(2)}, u32[]{:S(2)}) collective-permute-start(bf16[192,768]{1,0:T(8,128)(2,1)} %pad_maximum_fusion.22), channel_id=1, source_target_pairs={{0,16},{8,24},{16,0},{24,8},{1,17},{9,25},{17,1},{25,9},{2,18},{10... | collective-permute-start | bytes 884744 | tf_op jit(solution)/shard_map/ppermute | solution.py:284
  126.4 24.6 %collective-permute-start.11 = (bf16[192,768]{1,0:T(8,128)(2,1)}, bf16[192,768]{1,0:T(8,128)(2,1)}, u32[]{:S(2)}, u32[]{:S(2)}) collective-permute-start(bf16[192,768]{1,0:T(8,128)(2,1)} %pad_maximum_fusion.22), channel_id=1, source_target_pairs={{0,8},{8,16},{16,24},{24,0},{1,9},{9,17},{17,25},{25,1},{2,10},{10... | collective-permute-start | bytes 884744 | tf_op jit(solution)/shard_map/ppermute | solution.py:284
  131.3 24.9 %collective-permute-start.18 = (bf16[2,4,128,768]{3,2,1,0:T(8,128)(2,1)}, bf16[2,4,128,768]{3,2,1,0:T(8,128)(2,1)}, u32[]{:S(2)}, u32[]{:S(2)}) collective-permute-start(bf16[2,4,128,768]{3,2,1,0:T(8,128)(2,1)} %get-tuple-element.63), channel_id=1, source_target_pairs={{0,1},{1,0},{2,3},{3,2},{4,5},{5,4},{6,7},{7,6},{8,9},{9,8},{10,11... | collective-permute-start | bytes 4718600 | tf_op jit(solution)/shard_map/ppermute | solution.py:247
  166.7 12.8 %collective-permute-start.19 = (bf16[2,4,128,768]{3,2,1,0:T(8,128)(2,1)}, bf16[2,4,128,768]{3,2,1,0:T(8,128)(2,1)}, u32[]{:S(2)}, u32[]{:S(2)}) collective-permute-start(bf16[2,4,128,768]{3,2,1,0:T(8,128)(2,1)} %bitcast.73), channel_id=1, source_target_pairs={{0,1},{1,0},{2,3},{3,2},{4,5},{5,4},{6,7},{7,6},{8,9},{9,8},{10,11... | collective-permute-start | bytes 4718600 | tf_op jit(solution)/shard_map/ppermute | solution.py:247
  170.5 13.4 %collective-permute-start.35 = (bf16[192,768]{1,0:T(8,128)(2,1)}, bf16[192,768]{1,0:T(8,128)(2,1)}, u32[]{:S(2)}, u32[]{:S(2)}) collective-permute-start(bf16[192,768]{1,0:T(8,128)(2,1)} %get-tuple-element.66), channel_id=1, source_target_pairs={{0,8},{8,16},{16,24},{24,0},{1,9},{9,17},{17,25},{25,1},{2,10},{10... | collective-permute-start | bytes 884744 | tf_op jit(solution)/shard_map/ppermute | solution.py:295
  170.7 18.7 %collective-permute-start.37 = (bf16[192,768]{1,0:T(8,128)(2,1)}, bf16[192,768]{1,0:T(8,128)(2,1)}, u32[]{:S(2)}, u32[]{:S(2)}) collective-permute-start(bf16[192,768]{1,0:T(8,128)(2,1)} %get-tuple-element.67), channel_id=1, source_target_pairs={{0,24},{8,0},{16,8},{24,16},{1,25},{9,1},{17,9},{25,17},{2,26},{10... | collective-permute-start | bytes 884744 | tf_op jit(solution)/shard_map/ppermute | solution.py:295
  174.5 24.2 %collective-permute-start.36 = (bf16[192,768]{1,0:T(8,128)(2,1)}, bf16[192,768]{1,0:T(8,128)(2,1)}, u32[]{:S(2)}, u32[]{:S(2)}) collective-permute-start(bf16[192,768]{1,0:T(8,128)(2,1)} %get-tuple-element.68), channel_id=1, source_target_pairs={{0,16},{8,24},{16,0},{24,8},{1,17},{9,25},{17,1},{25,9},{2,18},{10... | collective-permute-start | bytes 884744 | tf_op jit(solution)/shard_map/ppermute | solution.py:295
  181.4 19.6 %collective-permute-start.20 = (bf16[2,128,768]{2,1,0:T(8,128)(2,1)S(1)}, bf16[2,128,768]{2,1,0:T(8,128)(2,1)S(1)}, u32[]{:S(2)}, u32[]{:S(2)}) collective-permute-start(bf16[2,128,768]{2,1,0:T(8,128)(2,1)S(1)} %get-tuple-element.60), channel_id=1, source_target_pairs={{0,4},{1,5},{2,6},{3,7},{4,0},{5,1},{6,2},{7,3},{8,12},{9,13},{10,... | collective-permute-start | bytes 1179656 | tf_op jit(solution)/shard_map/ppermute | solution.py:247
  182.7 25.8 %copy-start.27 = (f32[768]{0:T(1024)S(1)}, f32[768]{0:T(1024)}, u32[]{:S(2)}) copy-start(f32[768]{0:T(1024)} %get-tuple-element.35) | copy-start | bytes 9220
  182.7 26.0 %copy-start.34 = (f32[256]{0:T(256)S(1)}, f32[256]{0:T(256)}, u32[]{:S(2)}) copy-start(f32[256]{0:T(256)} %copy-done.33) | copy-start | bytes 3076
  182.7 26.0 %copy-start.43 = (f32[256]{0:T(256)S(1)}, f32[256]{0:T(256)}, u32[]{:S(2)}) copy-start(f32[256]{0:T(256)} %copy-done.42) | copy-start | bytes 3076
  182.7 18.3 %collective-permute-start.22 = (bf16[2,128,768]{2,1,0:T(8,128)(2,1)S(1)}, bf16[2,128,768]{2,1,0:T(8,128)(2,1)S(1)}, u32[]{:S(2)}, u32[]{:S(2)}) collective-permute-start(bf16[2,128,768]{2,1,0:T(8,128)(2,1)S(1)} %get-tuple-element.61), channel_id=1, source_target_pairs={{0,2},{1,3},{2,0},{3,1},{4,6},{5,7},{6,4},{7,5},{8,10},{9,11},{10,... | collective-permute-start | bytes 1179656 | tf_op jit(solution)/shard_map/ppermute | solution.py:247
  201.1 8.4 %copy-start.22 = (bf16[768,768]{1,0:T(8,128)(2,1)S(1)}, bf16[768,768]{1,0:T(8,128)(2,1)}, u32[]{:S(2)}) copy-start(bf16[768,768]{1,0:T(8,128)(2,1)} %all-gather.2.cloned.1.call-done) | copy-start | bytes 3538948
  201.1 6.3 %collective-permute-start.23 = (bf16[128,768]{1,0:T(8,128)(2,1)S(1)}, bf16[128,768]{1,0:T(8,128)(2,1)S(1)}, u32[]{:S(2)}, u32[]{:S(2)}) collective-permute-start(bf16[128,768]{1,0:T(8,128)(2,1)S(1)} %slice_bitcast_fusion.15), channel_id=1, source_target_pairs={{0,4},{1,5},{2,6},{3,7},{4,0},{5,1},{6,2},{7,3},{8,12},{9,13},{10,... | collective-permute-start | bytes 589832 | tf_op jit(solution)/shard_map/ppermute | solution.py:247
  202.4 6.0 %collective-permute-start.21 = (bf16[128,768]{1,0:T(8,128)(2,1)S(1)}, bf16[128,768]{1,0:T(8,128)(2,1)S(1)}, u32[]{:S(2)}, u32[]{:S(2)}) collective-permute-start(bf16[128,768]{1,0:T(8,128)(2,1)S(1)} %slice_bitcast_fusion.17), channel_id=1, source_target_pairs={{0,2},{1,3},{2,0},{3,1},{4,6},{5,7},{6,4},{7,5},{8,10},{9,11},{10,... | collective-permute-start | bytes 589832 | tf_op jit(solution)/shard_map/ppermute | solution.py:247
  211.1 12.5 %all-to-all-start.2 = ((bf16[8,128,192]{1,2,0:T(8,128)(2,1)}), bf16[8,128,192]{1,2,0:T(8,128)(2,1)}, u32[]{:S(2)}, u32[]{:S(2)}) async-start(bf16[8,128,192]{1,2,0:T(8,128)(2,1)} %bitcast.87), calls=%async_computation.2 | async-start | bytes 786432 | tf_op jit(solution)/shard_map/all_to_all | solution.py:515
  215.2 104.3 %reduce-scatter.2.cloned.1.call-start = ((), (), s32[]{:S(2)}) async-start(), calls=%async_computation.6 | async-start | bytes 1216512 | tf_op jit(solution)/shard_map/reduce_scatter | solution.py:506
  217.0 10.1 %copy-start.5 = (pred[1024,1024]{0,1:T(8,128)(4,1)S(1)}, pred[1024,1024]{0,1:T(8,128)(4,1)}, u32[]{:S(2)}) copy-start(pred[1024,1024]{0,1:T(8,128)(4,1)} %copy-done.4) | copy-start | bytes 3145732
  227.0 9.2 %copy-start.19 = (bf16[1024,3,64]{0,2,1:T(8,128)(2,1)S(1)}, bf16[1024,3,64]{0,2,1:T(8,128)(2,1)}, u32[]{:S(2)}) copy-start(bf16[1024,3,64]{0,2,1:T(8,128)(2,1)} %reshape.655) | copy-start | bytes 1179652
  227.1 9.2 %copy-start.24 = (bf16[1024,192]{0,1:T(8,128)(2,1)S(1)}, bf16[1024,192]{0,1:T(8,128)(2,1)}, u32[]{:S(2)}) copy-start(bf16[1024,192]{0,1:T(8,128)(2,1)} %copy-done.23) | copy-start | bytes 1179652
  227.1 9.2 %copy-start.41 = (f32[3,1024]{1,0:T(4,128)S(1)}, f32[3,1024]{1,0:T(4,128)}, u32[]{:S(2)}) copy-start(f32[3,1024]{1,0:T(4,128)} %log_add_fusion) | copy-start | bytes 36868
  255.4 10.7 %collective-permute-start.32 = (bf16[192,600]{1,0:T(8,128)(2,1)S(1)}, bf16[192,600]{1,0:T(8,128)(2,1)S(1)}, u32[]{:S(2)}, u32[]{:S(2)}) collective-permute-start(bf16[192,600]{1,0:T(8,128)(2,1)S(1)} %get-tuple-element.75), channel_id=1, source_target_pairs={{0,8},{8,16},{16,24},{24,0},{1,9},{9,17},{17,25},{25,1},{2,10},{10... | collective-permute-start | bytes 691208 | tf_op jit(solution)/shard_map/ppermute | solution.py:295
  255.5 12.7 %collective-permute-start.34 = (bf16[192,600]{1,0:T(8,128)(2,1)S(1)}, bf16[192,600]{1,0:T(8,128)(2,1)S(1)}, u32[]{:S(2)}, u32[]{:S(2)}) collective-permute-start(bf16[192,600]{1,0:T(8,128)(2,1)S(1)} %get-tuple-element.76), channel_id=1, source_target_pairs={{0,24},{8,0},{16,8},{24,16},{1,25},{9,1},{17,9},{25,17},{2,26},{10... | collective-permute-start | bytes 691208 | tf_op jit(solution)/shard_map/ppermute | solution.py:295
  259.5 20.4 %collective-permute-start.33 = (bf16[192,600]{1,0:T(8,128)(2,1)S(1)}, bf16[192,600]{1,0:T(8,128)(2,1)S(1)}, u32[]{:S(2)}, u32[]{:S(2)}) collective-permute-start(bf16[192,600]{1,0:T(8,128)(2,1)S(1)} %get-tuple-element.77), channel_id=1, source_target_pairs={{0,16},{8,24},{16,0},{24,8},{1,17},{9,25},{17,1},{25,9},{2,18},{10... | collective-permute-start | bytes 691208 | tf_op jit(solution)/shard_map/ppermute | solution.py:295
  261.5 23.2 %collective-permute-start.29 = (bf16[2,2,128,768]{3,2,1,0:T(8,128)(2,1)}, bf16[2,2,128,768]{3,2,1,0:T(8,128)(2,1)}, u32[]{:S(2)}, u32[]{:S(2)}) collective-permute-start(bf16[2,2,128,768]{3,2,1,0:T(8,128)(2,1)} %dynamic-slice_bitcast_fusion), channel_id=1, source_target_pairs={{0,1},{1,0},{2,3},{3,2},{4,5},{5,4},{6,7},{7,6},{8,9},{9,8},{10,11... | collective-permute-start | bytes 2359304 | tf_op jit(solution)/shard_map/ppermute | solution.py:247
  264.2 24.9 %copy-start.52 = (f32[2,128]{1,0:T(2,128)S(1)}, f32[2,128]{1,0:T(2,128)}, u32[]{:S(2)}) copy-start(f32[2,128]{1,0:T(2,128)} %multiply_reduce_fusion.4) | copy-start | bytes 3076
  264.2 57.1 %collective-permute-start.24 = (bf16[2,4,128,768]{3,2,1,0:T(8,128)(2,1)}, bf16[2,4,128,768]{3,2,1,0:T(8,128)(2,1)}, u32[]{:S(2)}, u32[]{:S(2)}) collective-permute-start(bf16[2,4,128,768]{3,2,1,0:T(8,128)(2,1)} %slice_bitcast_fusion), channel_id=1, source_target_pairs={{0,1},{1,0},{2,3},{3,2},{4,5},{5,4},{6,7},{7,6},{8,9},{9,8},{10,11... | collective-permute-start | bytes 4718600 | tf_op jit(solution)/shard_map/ppermute | solution.py:247
  281.1 13.0 %all-to-all-start.3 = ((bf16[8,24,1008]{2,1,0:T(8,128)(2,1)}), bf16[8,24,1008]{2,1,0:T(8,128)(2,1)S(1)}, u32[]{:S(2)}, u32[]{:S(2)}) async-start(bf16[8,24,1008]{2,1,0:T(8,128)(2,1)} %pad_maximum_fusion.21), calls=%async_computation.3 | async-start | bytes 786432 | tf_op jit(solution)/shard_map/all_to_all | solution.py:559
  287.0 22.6 %collective-permute-start.30 = (bf16[2,128,768]{2,1,0:T(8,128)(2,1)}, bf16[2,128,768]{2,1,0:T(8,128)(2,1)}, u32[]{:S(2)}, u32[]{:S(2)}) collective-permute-start(bf16[2,128,768]{2,1,0:T(8,128)(2,1)} %dynamic-slice_bitcast_fusion.1), channel_id=1, source_target_pairs={{0,2},{1,3},{2,0},{3,1},{4,6},{5,7},{6,4},{7,5},{8,10},{9,11},{10,... | collective-permute-start | bytes 1179656 | tf_op jit(solution)/shard_map/ppermute | solution.py:247
  302.1 18.8 %copy-start.29 = (f32[768]{0:T(1024)S(1)}, f32[768]{0:T(1024)}, u32[]{:S(2)}) copy-start(f32[768]{0:T(1024)} %copy-done.28) | copy-start | bytes 9220
  302.1 18.8 %copy-start.49 = (f32[2,128]{1,0:T(2,128)S(1)}, f32[2,128]{1,0:T(2,128)}, u32[]{:S(2)}) copy-start(f32[2,128]{1,0:T(2,128)} %get-tuple-element.122) | copy-start | bytes 3076
  310.6 10.3 %collective-permute-start.31 = (bf16[128,768]{1,0:T(8,128)(2,1)S(1)}, bf16[128,768]{1,0:T(8,128)(2,1)S(1)}, u32[]{:S(2)}, u32[]{:S(2)}) collective-permute-start(bf16[128,768]{1,0:T(8,128)(2,1)S(1)} %get-tuple-element.91), channel_id=1, source_target_pairs={{0,4},{1,5},{2,6},{3,7},{4,0},{5,1},{6,2},{7,3},{8,12},{9,13},{10,... | collective-permute-start | bytes 589832 | tf_op jit(solution)/shard_map/ppermute | solution.py:247
  323.5 9.2 %collective-permute-start.25 = (bf16[2,128,768]{2,1,0:T(8,128)(2,1)S(1)}, bf16[2,128,768]{2,1,0:T(8,128)(2,1)S(1)}, u32[]{:S(2)}, u32[]{:S(2)}) collective-permute-start(bf16[2,128,768]{2,1,0:T(8,128)(2,1)S(1)} %get-tuple-element.56), channel_id=1, source_target_pairs={{0,4},{1,5},{2,6},{3,7},{4,0},{5,1},{6,2},{7,3},{8,12},{9,13},{10,... | collective-permute-start | bytes 1179656 | tf_op jit(solution)/shard_map/ppermute | solution.py:247
  324.9 9.0 %collective-permute-start.27 = (bf16[2,128,768]{2,1,0:T(8,128)(2,1)S(1)}, bf16[2,128,768]{2,1,0:T(8,128)(2,1)S(1)}, u32[]{:S(2)}, u32[]{:S(2)}) collective-permute-start(bf16[2,128,768]{2,1,0:T(8,128)(2,1)S(1)} %get-tuple-element.57), channel_id=1, source_target_pairs={{0,2},{1,3},{2,0},{3,1},{4,6},{5,7},{6,4},{7,5},{8,10},{9,11},{10,... | collective-permute-start | bytes 1179656 | tf_op jit(solution)/shard_map/ppermute | solution.py:247
  327.6 12.9 %copy-start.35 = (f32[768]{0:T(1024)S(1)}, f32[768]{0:T(1024)}, u32[]{:S(2)}) copy-start(f32[768]{0:T(1024)} %get-tuple-element.33) | copy-start | bytes 9220
  334.0 5.7 %collective-permute-start.28 = (bf16[128,768]{1,0:T(8,128)(2,1)S(1)}, bf16[128,768]{1,0:T(8,128)(2,1)S(1)}, u32[]{:S(2)}, u32[]{:S(2)}) collective-permute-start(bf16[128,768]{1,0:T(8,128)(2,1)S(1)} %slice_bitcast_fusion.11), channel_id=1, source_target_pairs={{0,4},{1,5},{2,6},{3,7},{4,0},{5,1},{6,2},{7,3},{8,12},{9,13},{10,... | collective-permute-start | bytes 589832 | tf_op jit(solution)/shard_map/ppermute | solution.py:247
  334.6 5.7 %collective-permute-start.26 = (bf16[128,768]{1,0:T(8,128)(2,1)S(1)}, bf16[128,768]{1,0:T(8,128)(2,1)S(1)}, u32[]{:S(2)}, u32[]{:S(2)}) collective-permute-start(bf16[128,768]{1,0:T(8,128)(2,1)S(1)} %slice_bitcast_fusion.13), channel_id=1, source_target_pairs={{0,2},{1,3},{2,0},{3,1},{4,6},{5,7},{6,4},{7,5},{8,10},{9,11},{10,... | collective-permute-start | bytes 589832 | tf_op jit(solution)/shard_map/ppermute | solution.py:247
  (34 other events, 95.0 us)
Sparse Core Ops, SparseCore 0:
  10.9 66.4 all-gather.1
  221.1 98.3 reduce-scatter.1

commit v2 on v0

--- a/solution.py
+++ b/solution.py
@@ -1,6 +1,8 @@
 import jax
 import jax.numpy as jnp
 from jax import lax
+from jax.experimental import pallas as pl
+from jax.experimental.pallas import tpu as pltpu
 from jax.sharding import PartitionSpec as P
 
 HEADS = 12
@@ -30,7 +32,7 @@
     return jnp.sum(value.astype(jnp.float32), axis=(0, 1))
 
 
-def local(
+def wide_local(
     hidden_in,
     cotangent,
     segment_ids,
@@ -155,24 +157,6 @@
         act_low = act_full.astype(jnp.bfloat16)
         output_rows = middle + project(act_low, wd) + bd
         outs_rows.append(output_rows.astype(jnp.bfloat16))
-        back_weights = (
-            lax.all_gather(params[0], ("dp", "seq"), axis=0, tiled=True),
-            lax.all_gather(params[1], ("dp", "seq"), axis=0, tiled=True),
-            lax.all_gather(params[2], ("dp", "seq"), axis=0, tiled=True),
-            lax.all_gather(params[3], ("dp", "seq"), axis=0, tiled=True),
-            lax.all_gather(params[4], ("dp", "seq"), axis=0, tiled=True),
-            lax.all_gather(params[5], ("dp", "seq"), axis=0, tiled=True),
-            lax.all_gather(params[6], ("dp", "seq"), axis=0, tiled=True),
-            lax.all_gather(params[7], ("dp", "seq"), axis=0, tiled=True),
-            lax.all_gather(params[8], ("dp", "seq"), axis=0, tiled=True),
-            lax.all_gather(params[9], ("dp", "seq"), axis=0, tiled=True),
-            lax.all_gather(params[10], ("dp", "seq"), axis=0, tiled=True),
-            lax.all_gather(params[11], ("dp", "seq"), axis=0, tiled=True),
-            lax.all_gather(params[12], ("dp", "seq"), axis=0, tiled=True),
-            lax.all_gather(params[13], ("dp", "seq"), axis=0, tiled=True),
-            lax.all_gather(params[14], ("dp", "seq"), axis=0, tiled=True),
-        )
-        wq, wk, wv, wo, wu, wd = back_weights[:6]
         grad_out = cotangent[lower:upper_end].astype(jnp.float32)
         grad_low = grad_out.astype(jnp.bfloat16)
         d_act = project_back(grad_low, wd)
@@ -188,10 +172,7 @@
             .reshape(group_size, shard_rows, HEADS, HEAD_DIM)
         )
         row_dots = jnp.sum(d_attended.astype(jnp.float32) * attended_full, -1).transpose(0, 2, 1)
-        backward_pieces = (
-            lax.all_gather(key_rows, "seq", axis=1, tiled=True),
-            lax.all_gather(value_rows, "seq", axis=1, tiled=True),
-        )
+        backward_pieces = pieces
         backward_count_keys = backward_pieces[0].shape[1]
         backward_key_heads = backward_pieces[0].reshape(
             group_size, backward_count_keys, HEADS, HEAD_DIM
@@ -260,7 +241,705 @@
     return (jnp.concatenate(outs_rows, 0), jnp.concatenate(outs_grads, 0)) + tuple(grads)
 
 
+CORE, NEAR_X, NEAR_Y, ACROSS = 1, 2, 4, 6
+GROUPS = 4
+
+
+def tie(*values):
+    return lax.optimization_barrier(values)
+
+
+def swap(value, mask):
+    return lax.ppermute(value, "seq", [(item, item ^ mask) for item in range(8)])
+
+
+def pick(value, index, axis=0):
+    return lax.dynamic_index_in_dim(value, index, axis, keepdims=False)
+
+
+def in_order(own, other, bit, axis):
+    return jnp.where(
+        bit == 0, jnp.stack([own, other], axis), jnp.stack([other, own], axis)
+    )
+
+
+def plus(left, right):
+    return (left.astype(jnp.float32) + right.astype(jnp.float32)).astype(jnp.bfloat16)
+
+
+def total_of(parts):
+    return sum(part.astype(jnp.float32) for part in parts)
+
+
+def chips(value):
+    return [value] + [swap(value, mask) for mask in (NEAR_X, NEAR_Y, ACROSS)]
+
+
+def chips_send(order):
+    got = [order(0)]
+    for item, mask in ((1, NEAR_X), (2, NEAR_Y), (3, ACROSS)):
+        got.append(swap(order(item), mask))
+    return got
+
+
+def chips_order(parts, chip):
+    parts = jnp.stack(parts)
+    return jnp.stack([pick(parts, chip ^ item) for item in range(GROUPS)])
+
+
+def column_parts(value, count):
+    parts = [value]
+    for shift in range(1, count):
+        perm = [(item, (item + shift) % count) for item in range(count)]
+        parts.append(lax.ppermute(value, "dp", perm))
+    return parts
+
+
+def column_order(parts, place):
+    count = len(parts)
+    parts = jnp.stack(parts)
+    return jnp.stack([pick(parts, (place - item) % count) for item in range(count)])
+
+
+def column_send(value, place, count):
+    parts = [pick(value, place)]
+    for shift in range(1, count):
+        sent = pick(value, (place + shift) % count)
+        perm = [(item, (item + shift) % count) for item in range(count)]
+        parts.append(lax.ppermute(sent, "dp", perm))
+    return parts
+
+
+def norm_parts(value):
+    center = value - jnp.mean(value, -1, keepdims=True)
+    spread_rows = jnp.mean(center * center, -1, keepdims=True)
+    scale = lax.rsqrt(spread_rows + 1e-05)
+    return center * scale, scale
+
+
+def norm_back(normal, scale, gain, grad):
+    through = grad * gain
+    kept = through - jnp.mean(through, -1, keepdims=True)
+    kept = kept - normal * jnp.mean(through * normal, -1, keepdims=True)
+    return scale * kept
+
+
+def dot(left, right):
+    return jnp.dot(left, right, preferred_element_type=jnp.float32)
+
+
+def dot_right(left, right):
+    return lax.dot_general(
+        left, right, (((1,), (1,)), ((), ())), preferred_element_type=jnp.float32
+    )
+
+
+def dot_left(left, right):
+    return lax.dot_general(
+        left, right, (((0,), (0,)), ((), ())), preferred_element_type=jnp.float32
+    )
+
+
+BLOCK = 256
+VMEM_BYTES = 60 * 1024 * 1024
+
+
+def head_mask(head, count):
+    lane = lax.broadcasted_iota(jnp.int32, (1, count), 1)
+    inside = (lane >= head * HEAD_DIM) & (lane < (head + 1) * HEAD_DIM)
+    return inside.astype(jnp.float32).astype(jnp.bfloat16)
+
+
+def head_rows(head):
+    return pl.ds(pl.multiple_of(head * HEAD_DIM, HEAD_DIM), HEAD_DIM)
+
+
+def flipped(value):
+    return value.astype(jnp.float32).T.astype(jnp.bfloat16)
+
+
+def attend_kernel(
+    normed_ref, w_ref, bias_ref, row_ref, column_ref,
+    q_ref, k_ref, v_ref, full_ref, out_ref, p_ref, v_flip, held,
+):
+    head = pl.program_id(0)
+    length, count = q_ref.shape
+
+    @pl.when(head == 0)
+    def first():
+        for start in range(0, length, BLOCK):
+            rows = pl.ds(start, BLOCK)
+            product = dot(normed_ref[rows], w_ref[...]) + bias_ref[...]
+            q_ref[rows] = (product[:, :count] * 0.125).astype(jnp.bfloat16)
+            k_ref[rows] = product[:, count : 2 * count].astype(jnp.bfloat16)
+            v_ref[rows] = product[:, 2 * count :].astype(jnp.bfloat16)
+        v_flip[...] = flipped(v_ref[...])
+
+    mask = head_mask(head, count)
+    for start in range(0, length, BLOCK):
+        stop = start + BLOCK
+        scores = dot_right(k_ref[:stop], q_ref[start:stop] * mask)
+        shape = (stop, BLOCK)
+        causal = lax.broadcasted_iota(jnp.int32, shape, 0) <= start + lax.broadcasted_iota(
+            jnp.int32, shape, 1
+        )
+        same = column_ref[:stop] == row_ref[:, start:stop]
+        scores = jnp.where(causal & same, scores, -1000000000.0)
+        expo = jnp.exp(scores - jnp.max(scores, 0, keepdims=True))
+        probs = (expo * (1.0 / jnp.sum(expo, 0, keepdims=True))).astype(jnp.bfloat16)
+        p_ref[0, :stop, start:stop] = probs
+        held[head_rows(head), start:stop] = dot(v_flip[head_rows(head), :stop], probs)
+
+    @pl.when(head == pl.num_programs(0) - 1)
+    def last():
+        full = held[...].T
+        full_ref[...] = full
+        out_ref[...] = full.astype(jnp.bfloat16)
+
+
+def attend_back_kernel(
+    chip_ref, q_ref, k_ref, v_ref, d_ref, full_ref, normed_ref, w_ref, normal_ref, p_ref,
+    grad_ref, first_ref, sums_ref, bias_ref, k_flip, dots, dq, dk, dv, d_all,
+):
+    head = pl.program_id(0)
+    length, count = q_ref.shape
+
+    @pl.when(head == 0)
+    def first():
+        k_flip[...] = flipped(k_ref[...])
+        dots[...] = (d_ref[...].astype(jnp.float32) * full_ref[...]).T
+        dk[...] = jnp.zeros_like(dk)
+        dv[...] = jnp.zeros_like(dv)
+
+    mask = head_mask(head, count)
+    for start in range(0, length, BLOCK):
+        stop = start + BLOCK
+        d_out = d_ref[start:stop] * mask
+        probs = p_ref[0, :stop, start:stop]
+        row_dots = jnp.sum(dots[head_rows(head), start:stop], 0, keepdims=True)
+        d_probs = dot_right(v_ref[:stop], d_out)
+        d_scores = (probs.astype(jnp.float32) * (d_probs - row_dots)).astype(jnp.bfloat16)
+        dv[:stop] += dot(probs, d_out)
+        dk[:stop] += dot(d_scores, q_ref[start:stop] * mask)
+        dq[head_rows(head), start:stop] = dot(k_flip[head_rows(head), :stop], d_scores)
+
+    @pl.when(head == pl.num_programs(0) - 1)
+    def last():
+        for start in range(0, length, BLOCK):
+            rows = pl.ds(start, BLOCK)
+            d_queries = dq[:, start : start + BLOCK].T.astype(jnp.bfloat16).astype(jnp.float32)
+            d_all[rows] = jnp.concatenate([d_queries * 0.125, dk[rows], dv[rows]], 1).astype(
+                jnp.bfloat16
+            )
+        bias_ref[...] = jnp.sum(d_all[...].astype(jnp.float32), 0, keepdims=True)
+        grad_ref[...] = dot_left(normed_ref[...], d_all[...]).astype(jnp.bfloat16)
+        sums_ref[...] = jnp.zeros_like(sums_ref)
+        for item in range(GROUPS):
+            size = length // GROUPS
+            rows = pl.ds(pl.multiple_of((chip_ref[0] ^ item) * size, size), size)
+            d_first = dot_right(d_all[rows], w_ref[...])
+            sums_ref[0:1] += jnp.sum(d_first * normal_ref[rows], 0, keepdims=True)
+            sums_ref[1:2] += jnp.sum(d_first, 0, keepdims=True)
+            first_ref[item] = d_first.astype(jnp.bfloat16)
+
+
+def whole(*shape):
+    return pl.BlockSpec(shape, lambda head: (0,) * len(shape))
+
+
+def kernel_params():
+    return pltpu.CompilerParams(
+        dimension_semantics=("arbitrary",), vmem_limit_bytes=VMEM_BYTES
+    )
+
+
+def attend(normed, weights, bias, segments):
+    length, width = normed.shape
+    count = weights.shape[1] // 3
+    heads = count // HEAD_DIM
+    shape = (length, count)
+    low = jax.ShapeDtypeStruct(shape, jnp.bfloat16)
+    probs = pl.BlockSpec((1, length, length), lambda head: (head, 0, 0))
+    queries, keys, values, full, out, probs = pl.pallas_call(
+        attend_kernel,
+        grid=(heads,),
+        in_specs=[
+            whole(length, width),
+            whole(width, 3 * count),
+            whole(1, 3 * count),
+            whole(1, length),
+            whole(length, 1),
+        ],
+        out_specs=[whole(*shape)] * 5 + [probs],
+        out_shape=[
+            low,
+            low,
+            low,
+            jax.ShapeDtypeStruct(shape, jnp.float32),
+            low,
+            jax.ShapeDtypeStruct((heads, length, length), jnp.bfloat16),
+        ],
+        scratch_shapes=[
+            pltpu.VMEM((count, length), jnp.bfloat16),
+            pltpu.VMEM((count, length), jnp.float32),
+        ],
+        compiler_params=kernel_params(),
+        cost_estimate=pl.CostEstimate(
+            flops=4 * length * length * count + 6 * length * width * count,
+            bytes_accessed=2 * heads * length * length,
+            transcendentals=heads * length * length,
+        ),
+    )(normed, weights, bias[None], segments[None], segments[:, None])
+    return out, (queries, keys, values), (full, probs)
+
+
+def attend_back(chip, projected, kept, d_out, normed, weights, normal):
+    length, width = normed.shape
+    count = d_out.shape[1]
+    heads = count // HEAD_DIM
+    shape = (length, count)
+    full, probs = kept
+    size = length // GROUPS
+    return pl.pallas_call(
+        attend_back_kernel,
+        grid=(heads,),
+        in_specs=[pl.BlockSpec(memory_space=pltpu.SMEM)]
+        + [whole(*shape)] * 5
+        + [
+            whole(length, width),
+            whole(width, 3 * count),
+            whole(length, width),
+            pl.BlockSpec((1, length, length), lambda head: (head, 0, 0)),
+        ],
+        out_specs=[
+            whole(width, 3 * count),
+            whole(GROUPS, size, width),
+            whole(8, width),
+            whole(1, 3 * count),
+        ],
+        out_shape=[
+            jax.ShapeDtypeStruct((width, 3 * count), jnp.bfloat16),
+            jax.ShapeDtypeStruct((GROUPS, size, width), jnp.bfloat16),
+            jax.ShapeDtypeStruct((8, width), jnp.float32),
+            jax.ShapeDtypeStruct((1, 3 * count), jnp.float32),
+        ],
+        scratch_shapes=[
+            pltpu.VMEM((count, length), jnp.bfloat16),
+            pltpu.VMEM((count, length), jnp.float32),
+            pltpu.VMEM((count, length), jnp.float32),
+            pltpu.VMEM(shape, jnp.float32),
+            pltpu.VMEM(shape, jnp.float32),
+            pltpu.VMEM((length, 3 * count), jnp.bfloat16),
+        ],
+        compiler_params=kernel_params(),
+        cost_estimate=pl.CostEstimate(
+            flops=10 * length * length * count + 12 * length * width * count,
+            bytes_accessed=2 * heads * length * length,
+            transcendentals=0,
+        ),
+    )(chip[None], *projected, d_out, full, normed, weights, normal, probs)
+
+
+def one(*shape):
+    return jax.ShapeDtypeStruct(shape, jnp.float32)
+
+
+def low(*shape):
+    return jax.ShapeDtypeStruct(shape, jnp.bfloat16)
+
+
+def run(body, given, outs, flops, scratch=(), scalars=()):
+    specs = [pl.BlockSpec(memory_space=pltpu.SMEM)] * len(scalars)
+    return pl.pallas_call(
+        body,
+        grid=(1,),
+        in_specs=specs + [whole(*item.shape) for item in given],
+        out_specs=[whole(*item.shape) for item in outs],
+        out_shape=list(outs),
+        scratch_shapes=list(scratch),
+        compiler_params=pltpu.CompilerParams(vmem_limit_bytes=VMEM_BYTES),
+        cost_estimate=pl.CostEstimate(flops=flops, bytes_accessed=0, transcendentals=0),
+    )(*[item[None] for item in scalars], *given)
+
+
+def second_kernel(attended_ref, w_ref, in_ref, vectors_ref, middle_ref, second_ref):
+    groups, seqs, rows, count = attended_ref.shape
+    for seq in range(seqs):
+        place = pl.ds(seq * rows, rows)
+        middle = in_ref[place].astype(jnp.float32) + vectors_ref[0:1]
+        for group in range(groups):
+            middle += dot(attended_ref[group, seq], w_ref[group * count : (group + 1) * count])
+        middle_ref[place] = middle
+        normal, _ = norm_parts(middle)
+        second_ref[place] = (normal * vectors_ref[1:2] + vectors_ref[2:3]).astype(jnp.bfloat16)
+
+
+def branch_kernel(
+    own_ref, x_ref, y_ref, across_ref, grad_ref, middle_ref, vectors_ref, w_ref,
+    d_middle_ref, d_branch_ref, d_attended_ref, sums_ref,
+):
+    groups, seqs, rows, count = d_attended_ref.shape
+    d_second = total_of([own_ref[0], x_ref[...], y_ref[...], across_ref[...]])
+    normal, scale = norm_parts(middle_ref[...])
+    d_middle = grad_ref[...].astype(jnp.float32) + norm_back(
+        normal, scale, vectors_ref[1:2], d_second
+    )
+    d_middle_ref[...] = d_middle
+    d_branch = d_middle.astype(jnp.bfloat16)
+    d_branch_ref[...] = d_branch
+    for group in range(groups):
+        part = dot_right(d_branch, w_ref[group * count : (group + 1) * count])
+        part = part.astype(jnp.bfloat16)
+        for seq in range(seqs):
+            d_attended_ref[group, seq] = part[seq * rows : (seq + 1) * rows]
+    sums_ref[...] = jnp.zeros_like(sums_ref)
+    sums_ref[0:1] = jnp.sum(d_branch.astype(jnp.float32), 0, keepdims=True)
+    sums_ref[1:2] = jnp.sum(grad_ref[...].astype(jnp.float32), 0, keepdims=True)
+    sums_ref[2:3] = jnp.sum(d_second * normal, 0, keepdims=True)
+    sums_ref[3:4] = jnp.sum(d_second, 0, keepdims=True)
+
+
+def hidden_kernel(*refs):
+    rows_refs, grad_refs = refs[:4], refs[4:8]
+    w_up, w_down, bias_ref, act_ref, d_upper_ref, d_rows_ref, sums_ref = refs[8:]
+    tokens = rows_refs[0].shape[0]
+    skip = (grad_refs[0].shape[0] - tokens) // 2
+    slope = 0.7978845608028654
+    sums_ref[...] = jnp.zeros_like(sums_ref)
+    for item in range(4):
+        place = pl.ds(item * tokens, tokens)
+        upper = dot(rows_refs[item][...], w_up[...]) + bias_ref[...]
+        square = upper * upper
+        bend = jnp.tanh(slope * (upper + 0.044715 * (square * upper)))
+        act_ref[place] = (0.5 * upper * (1.0 + bend)).astype(jnp.bfloat16)
+        rise = 0.5 * (1.0 + bend) + (0.5 * slope) * upper * (1.0 - bend * bend) * (
+            1.0 + (3.0 * 0.044715) * square
+        )
+        d_act = dot_right(grad_refs[item][skip : skip + tokens], w_down[...])
+        d_upper = (d_act * rise).astype(jnp.bfloat16)
+        d_upper_ref[place] = d_upper
+        sums_ref[0:1] += jnp.sum(d_upper.astype(jnp.float32), 0, keepdims=True)
+        d_rows_ref[item] = dot_right(d_upper, w_up[...]).astype(jnp.bfloat16)
+
+
+def hidden_weights_kernel(core_ref, *refs):
+    rows_refs, grad_refs = refs[:4], refs[4:8]
+    act_ref, d_upper_ref, w_down, down_ref, late_ref, up, down = refs[8:]
+    tokens = rows_refs[0].shape[0]
+    skip = (grad_refs[0].shape[0] - tokens) // 2
+    for item in range(4):
+        place = pl.ds(item * tokens, tokens)
+        down_ref[item] = dot(act_ref[place], w_down[...]).astype(jnp.bfloat16)
+        up_term = dot_left(rows_refs[item][...], d_upper_ref[place])
+        down_term = dot_left(act_ref[place], grad_refs[item][skip : skip + tokens])
+        if item == 0:
+            up[...] = up_term
+            down[...] = down_term
+        else:
+            up[...] += up_term
+            down[...] += down_term
+    _, columns, both, width = late_ref.shape
+    half, side = both // 2, width // 2
+    for order in range(2):
+        start = pl.multiple_of((core_ref[0] ^ order) * side, side)
+        for column in range(columns):
+            top = column * both
+            for part in range(2):
+                late_ref[order, column, :half, part * side : (part + 1) * side] = up[
+                    top + part * half : top + (part + 1) * half, pl.ds(start, side)
+                ].astype(jnp.bfloat16)
+            late_ref[order, column, half:] = down[
+                pl.ds(pl.multiple_of(start + column * half, 8), half)
+            ].astype(jnp.bfloat16)
+
+
+def out_weight_kernel(place_ref, attended_ref, d_ref, grad_ref, total):
+    groups, seqs, rows, count = attended_ref.shape
+    for group in range(groups):
+        total[group * count : (group + 1) * count] = sum(
+            dot_left(attended_ref[group, seq], d_ref[seq * rows : (seq + 1) * rows])
+            for seq in range(seqs)
+        )
+    cores, chips_count, columns, share, _ = grad_ref.shape
+    plane = cores * chips_count
+    for order in range(cores):
+        for item in range(chips_count):
+            owner = place_ref[0] ^ (2 * item + order)
+            for column in range(columns):
+                start = pl.multiple_of((column * plane + owner) * share, 8)
+                grad_ref[order, item, column] = total[pl.ds(start, share)].astype(jnp.bfloat16)
+
+
+def plane_local(
+    hidden_in,
+    cotangent,
+    segment_ids,
+    query_weight,
+    key_weight,
+    value_weight,
+    out_weight,
+    up_weight,
+    down_weight,
+    query_bias,
+    value_bias,
+    out_bias,
+    up_bias,
+    down_bias,
+    first_gain,
+    first_shift,
+    second_gain,
+    second_shift,
+):
+    seqs, rows, width = hidden_in.shape
+    plane = lax.axis_size("seq")
+    columns = lax.axis_size("dp")
+    owners = plane * columns
+    share = query_weight.shape[0]
+    ff_share = down_weight.shape[0]
+    hidden = up_weight.shape[1]
+    group_width = width // GROUPS
+    length = rows * plane
+    tokens = seqs * rows
+    half = plane * share // 2
+    column = lax.axis_index("dp")
+    place = lax.axis_index("seq")
+    core, chip = place % 2, place // 2
+
+    sent = jnp.stack([query_weight, key_weight, value_weight], 1)
+    sent = sent.reshape(share, 3, GROUPS, group_width).transpose(2, 0, 1, 3)
+    sent = jnp.repeat(sent.reshape(GROUPS, share, 3 * group_width), 2, axis=0)
+    sent_up = up_weight.reshape(share, columns, plane, ff_share).transpose(2, 0, 1, 3)
+    sent_up = sent_up.reshape(plane, share, columns * ff_share)
+    sent = jnp.concatenate([sent, sent_up], -1)
+
+    small = (
+        query_bias,
+        value_bias,
+        out_bias,
+        down_bias,
+        first_gain,
+        first_shift,
+        second_gain,
+        second_shift,
+        up_bias,
+        segment_ids,
+    )
+    sent, small, out_weight = tie(sent, small, out_weight)
+    got = lax.all_to_all(sent, "seq", 0, 0, tiled=True).reshape(plane * share, -1)
+    small = jnp.concatenate(small[:-1] + (small[-1].astype(jnp.bfloat16).reshape(-1),))
+    small_size = small.size
+    small = jnp.pad(small[None], ((0, 7), (0, width - small_size)))
+    small = column_parts(jnp.concatenate([out_weight, small]), columns)
+    mine = in_order(pick(hidden_in, core), swap(pick(hidden_in, 1 - core), CORE), core, 0)
+    got, small, mine = tie(got, small, mine)
+
+    got_up = got[:, 3 * group_width :]
+    later = [
+        got_up[:half],
+        got_up[half:],
+        down_weight,
+        pick(got[:, : 3 * group_width].reshape(2, half, -1), core),
+    ]
+    later = column_parts(jnp.concatenate(later, -1), columns)
+
+    small = column_order(small, column)
+    w_out = small[:, :share].reshape(columns * share, width)
+    small = jnp.pad(small[:, share], ((0, -columns % 8), (0, 0)))
+    small = in_order(small, swap(small, CORE), core, 0)
+    mine = chips(jnp.concatenate([mine, small], 1))
+    mine = chips_order(mine, chip).reshape(plane, -1, width)
+    small = mine[:, rows : rows + columns].transpose(1, 0, 2)
+    mine = mine[:, :rows].reshape(length, width)
+    vectors = small[:, :, : 8 * share].astype(jnp.float32).reshape(owners, 8, share)
+    vectors = vectors.transpose(1, 0, 2).reshape(8, width)
+    bq, bv, bo, bd, gain_one, shift_one, gain_two, shift_two = [vectors[i] for i in range(8)]
+    bu = small[:, :, 8 * share : 8 * share + ff_share].astype(jnp.float32)
+    bu = pick(bu.reshape(columns, GROUPS, 2, ff_share), chip, 1).transpose(1, 0, 2).reshape(-1)
+    segments = pick(small[:, :, 8 * share + ff_share : small_size], column)
+    segments = pick(segments.reshape(plane, seqs, rows), core, 1).reshape(length)
+    segments = segments.astype(jnp.int32)
+    normal_all, _ = norm_parts(mine.astype(jnp.float32))
+    normed = (normal_all * gain_one + shift_one).astype(jnp.bfloat16)
+    own_columns = lambda item: lax.dynamic_slice_in_dim(item, chip * group_width, group_width)
+    bias_here = jnp.concatenate([own_columns(bq), jnp.zeros((group_width,)), own_columns(bv)])
+
+    w_out = in_order(w_out, swap(w_out, CORE), core, 0)
+    mine, w_out, own_low = tie(mine, w_out, cotangent.reshape(tokens, width))
+    w_out = chips(w_out)
+    normed, bias_here, segments, later, w_out, own_low = tie(
+        normed, bias_here, segments, later, w_out, own_low
+    )
+    beside = chips(own_low)
+    w_qkv = column_order([item[:, 2 * width :] for item in later], column)
+    w_qkv = in_order(w_qkv, swap(w_qkv, CORE), core, 1).reshape(width, 3 * group_width)
+    attended, projected, kept = attend(normed, w_qkv, bias_here, segments)
+    attended, beside, later, w_out = tie(attended, beside, later, w_out)
+    later = column_order([item[:, : 2 * width] for item in later], column)
+    later_far = swap(later, CORE)
+    w_out = chips_order(w_out, chip).reshape(plane, columns, share, width)
+    w_out = w_out.transpose(1, 0, 2, 3).reshape(width, width)
+    attended = attended.reshape(plane, rows, group_width)
+    attended = lax.all_to_all(attended, "seq", 0, 0, tiled=True)
+    attended = attended.reshape(GROUPS, seqs, rows, group_width)
+    block_in = hidden_in.reshape(tokens, width)
+    norm_vectors = jnp.stack([bo, gain_two, shift_two] + [jnp.zeros_like(bo)] * 5)
+    middle, second = run(
+        second_kernel,
+        (attended, w_out, block_in, norm_vectors),
+        (one(tokens, width), low(tokens, width)),
+        2 * tokens * width * width,
+    )
+    second = chips(second)
+    later = in_order(later, later_far, core, 0)
+    w_down = later[..., width:].reshape(width, width)
+    w_up = jnp.concatenate(
+        [
+            later[item, ..., width // 2 * side : width // 2 * (side + 1)]
+            for side in range(2)
+            for item in range(2)
+        ],
+        -1,
+    )
+    w_up = w_up.reshape(columns, half, 2, width).transpose(0, 2, 1, 3).reshape(width, width)
+
+    many = GROUPS * tokens
+    act, d_upper, d_rows, d_bu = run(
+        hidden_kernel,
+        (*second, *beside, w_up, w_down, bu[None]),
+        (low(many, width), low(many, width), low(GROUPS, tokens, width), one(8, width)),
+        12 * many * width * width,
+    )
+    d_second = [swap(d_rows[i], mask) for i, mask in ((1, NEAR_X), (2, NEAR_Y), (3, ACROSS))]
+    act, d_rows = tie(act, d_rows)
+    down, late = run(
+        hidden_weights_kernel,
+        (*second, *beside, act, d_upper, w_down),
+        (low(GROUPS, tokens, width), low(2, columns, 2 * half, width)),
+        12 * many * width * width,
+        [pltpu.VMEM((width, width), jnp.float32)] * 2,
+        (core,),
+    )
+    d_second, late, down = tie(d_second, late, down)
+    late = plus(late[0], swap(late[1], CORE))
+    d_middle, d_branch, d_attended, sums = run(
+        branch_kernel,
+        (d_rows, *d_second, cotangent.reshape(tokens, width), middle, norm_vectors, w_out),
+        (
+            one(tokens, width),
+            low(tokens, width),
+            low(GROUPS, seqs, rows, group_width),
+            one(8, width),
+        ),
+        2 * tokens * width * width,
+    )
+    d_attended, d_branch, late = tie(d_attended, d_branch, late)
+    late = column_send(late, column, columns)
+    d_attended = d_attended.reshape(plane, rows, group_width)
+    d_attended = lax.all_to_all(d_attended, "seq", 0, 0, tiled=True)
+    (grad_out,) = run(
+        out_weight_kernel,
+        (attended, d_branch),
+        (low(2, GROUPS, columns, share, width),),
+        2 * tokens * width * width,
+        [pltpu.VMEM((width, width), jnp.float32)],
+        (place,),
+    )
+    grad_out = plus(grad_out[0], swap(grad_out[1], CORE))
+    d_attended, grad_out, down = tie(d_attended, grad_out, down)
+    grad_out = [grad_out[0]] + [
+        swap(grad_out[i], mask) for i, mask in ((1, NEAR_X), (2, NEAR_Y), (3, ACROSS))
+    ]
+    down = [down[0]] + [
+        swap(down[i], mask) for i, mask in ((1, NEAR_X), (2, NEAR_Y), (3, ACROSS))
+    ]
+    d_attended = d_attended.reshape(length, group_width)
+    grad_qkv, d_first, d_sums, d_bias = attend_back(
+        chip, projected, kept, d_attended, normed, w_qkv, normal_all
+    )
+    grad_qkv, d_first, grad_out, late = tie(grad_qkv, d_first, grad_out, late)
+    d_bias = d_bias.reshape(3, group_width)
+
+    grad_qkv = grad_qkv.reshape(columns, 2, half, -1)
+    grad_qkv = plus(pick(grad_qkv, core, 1), swap(pick(grad_qkv, 1 - core, 1), CORE))
+    grad_out = total_of(grad_out).astype(jnp.bfloat16).reshape(columns, -1, 3 * group_width)
+    last = column_send(jnp.concatenate([grad_qkv, grad_out], 1), column, columns)
+    d_first = [d_first[0]] + [
+        swap(d_first[item], mask) for item, mask in ((1, NEAR_X), (2, NEAR_Y), (3, ACROSS))
+    ]
+
+    def placed(item):
+        zeros = jnp.zeros((width,), jnp.float32)
+        return lax.dynamic_update_slice_in_dim(zeros, item, chip * group_width, 0)
+
+    d_bu = d_bu[0].reshape(2, columns, 1, ff_share).transpose(1, 2, 0, 3)
+    d_bu = lax.dynamic_update_slice_in_dim(
+        jnp.zeros((columns, GROUPS, 2, ff_share), jnp.float32), d_bu, chip, 1
+    )
+    terms = [
+        placed(d_bias[0]),
+        placed(d_bias[2]),
+        sums[0],
+        sums[1],
+        d_sums[0],
+        d_sums[1],
+        sums[2],
+        sums[3],
+    ]
+    terms = jnp.concatenate([jnp.stack(terms).T, d_bu.reshape(width, -1)], -1)
+
+    terms = column_send(terms.reshape(columns, plane * share, -1), column, columns)
+    last, late, terms, down = tie(last, late, terms, down)
+    last, late, terms = total_of(last), total_of(late), total_of(terms)
+    grad_up = jnp.concatenate([late[:half, : width // 2], late[:half, width // 2 :]])
+    grad_down = late[half:]
+    grad_out = last[half:].reshape(share, width)
+    last = last[:half].astype(jnp.bfloat16)
+    last = in_order(last, swap(last, CORE), core, 0).reshape(plane * share, -1)
+    coarse = lax.reduce_precision(terms, 8, 7)
+    terms = jnp.concatenate([coarse, terms - coarse], -1)
+    last = jnp.concatenate([last, terms.astype(jnp.bfloat16), grad_up.astype(jnp.bfloat16)], -1)
+    last = lax.all_to_all(last.reshape(plane, share, -1), "seq", 0, 0, tiled=True)
+    last = last.astype(jnp.float32)
+    grad_up = last[..., -columns * ff_share :].reshape(plane, share, columns, ff_share)
+    grad_up = grad_up.transpose(1, 2, 0, 3).reshape(share, hidden)
+    terms = jnp.sum(last[..., 3 * group_width : -columns * ff_share], 0)
+    terms = terms[:, : terms.shape[1] // 2] + terms[:, terms.shape[1] // 2 :]
+    g_bu = terms[:, 8:].reshape(-1)
+    terms = terms[:, :8].T
+    g_bq, g_bv, g_bo, g_bd, g_g1, g_s1, g_g2, g_s2 = [terms[i] for i in range(8)]
+    grad_qkv = last[::2, :, : 3 * group_width].reshape(GROUPS, share, 3, group_width)
+    grad_qkv = grad_qkv.transpose(2, 1, 0, 3).reshape(3, share, width)
+
+    d_first = total_of(d_first).astype(jnp.bfloat16).reshape(2, rows, width)
+    d_first = in_order(pick(d_first, core), swap(pick(d_first, 1 - core), CORE), core, 0)
+    d_first = d_first.reshape(tokens, width).astype(jnp.float32)
+    normal_one, scale_one = norm_parts(block_in.astype(jnp.float32))
+    grad_input = d_middle + norm_back(normal_one, scale_one, gain_one, d_first)
+    hidden_out = (middle + total_of(down) + bd).astype(jnp.bfloat16)
+    return (
+        hidden_out.reshape(seqs, rows, width),
+        grad_input.reshape(seqs, rows, width),
+        grad_qkv[0],
+        grad_qkv[1],
+        grad_qkv[2],
+        grad_out,
+        grad_up,
+        grad_down,
+        g_bq,
+        g_bv,
+        g_bo,
+        g_bu,
+        g_bd,
+        g_g1,
+        g_s1,
+        g_g2,
+        g_s2,
+    )
+
+
 def solution(mesh):
+    plane = mesh.shape["seq"] == 8 and HEADS % 4 == 0
+    body = plane_local if plane else wide_local
     placed = (
         P("dp", "seq", None),
         P("dp", "seq", None),
@@ -282,7 +961,7 @@
         P(("dp", "seq")),
     )
     return jax.shard_map(
-        local,
+        body,
         mesh=mesh,
         in_specs=placed,
         out_specs=(

time: 1390 us -> 293 us (0.21)
  waiting for transfers between devices: 1060 us -> 78.1 us
  matrix products: 108 us -> 0 us
  blocking collectives: 92 us -> 0 us
  starting transfers between devices: 1.21 us -> 69.7 us
  Pallas kernels: 0 us -> 57.7 us
  local copies, waits for them, and re-layouts: 84.4 us -> 52.1 us
    reduce_scatter x6 -> x0, waiting for transfers between devices: 610 us -> none  [local(): lax.psum_scatter(totals, ('dp', 'seq'), scatter_dimension=0, tiled=True)]
    all_gather x10 -> x0, waiting for transfers between devices: 358 us -> none  [the longest x1 58.7 us: local(): lax.all_gather(params[5], ('dp', 'seq'), axis=0, tiled=True)]
    dot_general x48 -> x0, matrix products: 108 us -> none  [the longest x12 26.1 us: weight_term(): jnp.einsum('spd,spe->de', left, right, preferred_element_type=jnp.float32)]
    unnamed x24 -> x0, waiting for transfers between devices: 86.6 us -> none
    unnamed x2 -> x0, blocking collectives: 83.2 us -> none
    unnamed x285 -> x106, local copies, waits for them, and re-layouts: 70.7 us -> 2.53 us
    ppermute x0 -> x49, waiting for transfers between devices: none -> 64.4 us  [the longest x34 58.2 us: swap(): lax.ppermute(value, 'seq', [(item, item ^ mask) for item in range(8)])]
    pallas_call x0 -> x7, Pallas kernels: none -> 57.7 us  [the longest x5 29.3 us: run(): pl.pallas_call(body, grid=(1,), in_specs=specs + [whole(*item.shape) for...]
  transfers between devices with their start and end apart: 20 -> 53, of which waited for: 19 -> 20; matrix products, arithmetic and copies ran while one was open for 13% -> 21% of each run, Pallas kernels for 0% -> 16%
where the time goes in v2:
time: 293 us; the launch traced here: 288 us
  waiting for transfers between devices  78.1 us (27%)
  starting transfers between devices  69.7 us (24%)
  Pallas kernels  57.7 us (20%)
  local copies, waits for them, and re-layouts  52.1 us (18%)
  other arithmetic  28.1 us (10%)
    ppermute x34, waiting for transfers between devices, swap(): lax.ppermute(value, 'seq', [(item, item ^ mask) for item in range(8)])  58.2 us
    ppermute x34, starting transfers between devices, swap(): lax.ppermute(value, 'seq', [(item, item ^ mask) for item in range(8)])  30 us
    pallas_call x5, Pallas kernels, run(): pl.pallas_call(body, grid=(1,), in_specs=specs + [whole(*item.shape) for...  29.3 us
    pallas_call x1, Pallas kernels, attend_back(): pl.pallas_call(attend_back_kernel, grid=(heads,), in_specs=[pl.BlockSpec(...  14.4 us
    pallas_call x1, Pallas kernels, attend(): pl.pallas_call(attend_kernel, grid=(heads,), in_specs=[whole(length, widt...  14.1 us
    ppermute x9, starting transfers between devices, column_send(): parts.append(lax.ppermute(sent, 'dp', perm))  13.1 us
    ppermute x6, starting transfers between devices, column_parts(): parts.append(lax.ppermute(value, 'dp', perm))  11.1 us
    all_to_all x1, waiting for transfers between devices, plane_local(): lax.all_to_all(last.reshape(plane, share, -1), 'seq', 0, 0, tiled=True)  5.96 us
  transfers between devices with their start and end apart: 53, of which 20 were waited for; matrix products, arithmetic and copies ran while one was open for 21% of the time, Pallas kernels for 16%

profile of v2, /device:TPU:0, one launch (start us, length us, event | category | flops | bytes accessed | tf_op | source)
XLA Modules:
  0.0 288.0 jit_solution(3439906938633778468)
XLA Ops:
  7.2 4.8 %all-to-all-start = ((bf16[8,24,960]{2,1,0:T(8,128)(2,1)}), bf16[8,24,960]{2,1,0:T(8,128)(2,1)S(1)}, u32[]{:S(2)}, u32[]{:S(2)}) async-start(bf16[8,24,960]{2,1,0:T(8,128)(2,1)} %pad_maximum_fusion.11), calls=%async_computation | async-start | bytes 786432 | tf_op jit(solution)/shard_map/all_to_all | solution.py:728
  12.3 1.6 collective-permute-start
  13.9 2.6 collective-permute-start.1
  16.5 1.3 collective-permute-start.2
  18.5 2.1 collective-permute-done.1
  22.7 2.0 collective-permute-start.5
  24.7 1.5 collective-permute-start.6
  26.3 3.2 %collective-permute-start.10 = (bf16[96,2112]{1,0:T(8,128)(2,1)S(1)}, bf16[96,2112]{1,0:T(8,128)(2,1)S(1)}, u32[]{:S(2)}, u32[]{:S(2)}) collective-permute-start(bf16[96,2112]{1,0:T(8,128)(2,1)S(1)} %pad_maximum_fusion.10), channel_id=1, source_target_pairs={{0,24},{8,0},{16,8},{24,16},{1,25},{9,1},{17,9},{25,17},{2,26},{10... | collective-permute-start | bytes 1216520 | tf_op jit(solution)/shard_map/ppermute | solution.py:294
  29.7 5.5 %collective-permute-done.5 = bf16[2,136,768]{2,1,0:T(8,128)(2,1)S(1)} collective-permute-done((bf16[2,136,768]{2,1,0:T(8,128)(2,1)S(1)}, bf16[2,136,768]{2,1,0:T(8,128)(2,1)S(1)}, u32[]{:S(2)}, u32[]{:S(2)}) %collective-permute-start.5) | collective-permute-done | bytes 417824 | tf_op jit(solution)/shard_map/ppermute | solution.py:253
  35.2 2.2 collective-permute-start.9
  37.4 7.9 %collective-permute-done.6 = bf16[2,136,768]{2,1,0:T(8,128)(2,1)S(1)} collective-permute-done((bf16[2,136,768]{2,1,0:T(8,128)(2,1)S(1)}, bf16[2,136,768]{2,1,0:T(8,128)(2,1)S(1)}, u32[]{:S(2)}, u32[]{:S(2)}) %collective-permute-start.6) | collective-permute-done | bytes 417824 | tf_op jit(solution)/shard_map/ppermute | solution.py:253
  45.3 2.0 collective-permute-start.13
  58.7 1.5 collective-permute-start.14
  60.3 2.8 subtract_multiply_fusion
  63.1 2.0 collective-permute-done.9
  65.0 2.1 collective-permute-done.14
  68.5 1.8 collective-permute-start.16
  70.7 1.4 collective-permute-start.18
  75.0 14.1 %shard_map.305 = (bf16[1024,192]{1,0:T(8,128)(2,1)}, bf16[1024,192]{1,0:T(8,128)(2,1)}, bf16[1024,192]{1,0:T(8,128)(2,1)}, f32[1024,192]{1,0:T(8,128)}, bf16[102...) custom-call(bf16[1024,768]{1,0:T(8,128)(2,1)} %get-tuple-element.143.normed_ref, bf16[768,576]{1,0:T(8,128)(2,1)} %bitcast.245, ...), custom_call_target="tpu_custom_call" | custom-call | flops 1711276032 | bytes 6291456 | tf_op jit(solution)/shard_map/pallas_call | solution.py:463
  89.1 1.2 collective-permute-done.17.refs_6_
  94.4 2.0 copy.137
  96.3 3.7 %all-to-all-start.1 = ((bf16[8,128,192]{1,2,0:T(8,128)(2,1)}), bf16[8,128,192]{1,2,0:T(8,128)(2,1)S(1)}, u32[]{:S(2)}, u32[]{:S(2)}) async-start(bf16[8,128,192]{1,2,0:T(8,128)(2,1)} %copy.137), calls=%async_computation.1 | async-start | bytes 786432 | tf_op jit(solution)/shard_map/all_to_all | solution.py:782
  100.0 1.2 pad_maximum_fusion.2
  101.5 1.1 copy.139
  102.6 5.5 %all-to-all-done.1 = bf16[8,128,192]{1,2,0:T(8,128)(2,1)S(1)} async-done(((bf16[8,128,192]{1,2,0:T(8,128)(2,1)}), bf16[8,128,192]{1,2,0:T(8,128)(2,1)S(1)}, u32[]{:S(2)}, u32[]{:S(2)}) %all-to-all-start.1) | async-done | bytes 393248 | tf_op jit(solution)/shard_map/all_to_all | solution.py:782
  109.1 3.1 %shard_map.306 = (f32[256,768]{1,0:T(8,128)}, bf16[256,768]{1,0:T(8,128)(2,1)}) custom-call(bf16[4,2,128,192]{3,2,1,0:T(8,128)(2,1)} %bitcast.241, bf16[768,768]{1,0:T(8,128)(2,1)} %bitcast.237, bf16[256,768]{1,0:T(8,128)(2,1)} %bitcast.236, f32[8,768]{1,0:T(8,128)} %stack.267.vectors_ref), custom_call_target="tpu_custom_call" | custom-call | flops 301989888 | tf_op jit(solution)/shard_map/pallas_call | solution.py:553
  113.3 2.4 collective-permute-start.21
  115.7 2.0 maximum_select_fusion
  117.9 1.1 slice.365
  119.1 1.1 copy.174
  120.2 4.2 %collective-permute-done.19.refs_1_ = bf16[256,768]{1,0:T(8,128)(2,1)S(1)} collective-permute-done((bf16[256,768]{1,0:T(8,128)(2,1)}, bf16[256,768]{1,0:T(8,128)(2,1)S(1)}, u32[]{:S(2)}, u32[]{:S(2)}) %collective-permute-start.19) | collective-permute-done | bytes 393248 | tf_op jit(solution)/shard_map/ppermute | solution.py:253
  124.4 7.7 %collective-permute-done.20.refs_2_ = bf16[256,768]{1,0:T(8,128)(2,1)S(1)} collective-permute-done((bf16[256,768]{1,0:T(8,128)(2,1)}, bf16[256,768]{1,0:T(8,128)(2,1)S(1)}, u32[]{:S(2)}, u32[]{:S(2)}) %collective-permute-start.20) | collective-permute-done | bytes 393248 | tf_op jit(solution)/shard_map/ppermute | solution.py:253
  133.1 9.4 %shard_map.307 = (bf16[1024,768]{1,0:T(8,128)(2,1)}, bf16[1024,768]{1,0:T(8,128)(2,1)}, bf16[4,256,768]{2,1,0:T(8,128)(2,1)}, f32[8,768]{1,0:T(8,128)}) custom-call(bf16[256,768]{1,0:T(8,128)(2,1)} %get-tuple-element.165.refs_0_, bf16[256,768]{1,0:T(8,128)(2,1)} %copy-done.46, bf16[256,768]{1,0:T(8,128)(2,1)} %copy-done.47, bf16[256,768]{1,0:T(8,128)(2,1)} %copy-done.48, ...), custom_call_target="tpu_custom_call" | custom-call | flops 7247757312 | tf_op jit(solution)/shard_map/pallas_call | solution.py:553
  142.5 1.3 slice_bitcast_fusion.10
  144.1 1.3 collective-permute-start.24
  145.5 1.9 collective-permute-start.25
  147.3 8.6 %shard_map.308 = (bf16[4,256,768]{2,1,0:T(8,128)(2,1)}, bf16[2,4,192,768]{3,2,1,0:T(8,128)(2,1)}) custom-call(s32[1]{0:T(128)} %bitcast.70.core_ref, bf16[256,768]{1,0:T(8,128)(2,1)} %get-tuple-element.165.refs_0_, bf16[256,768]{1,0:T(8,128)(2,1)} %copy-done.46, bf16[256,768]{1,0:T(8,128)(2,1)} %copy-done.47, bf16[256,768]{1,0:T(8,128)(2,1)} %copy-done.48, ...), custom_call_target="tpu_custom_call" | custom-call | flops 7247757312 | tf_op jit(solution)/shard_map/pallas_call | solution.py:553
  156.0 6.3 %collective-permute-done.24.y_ref = bf16[256,768]{1,0:T(8,128)(2,1)S(1)} collective-permute-done((bf16[256,768]{1,0:T(8,128)(2,1)S(1)}, bf16[256,768]{1,0:T(8,128)(2,1)S(1)}, u32[]{:S(2)}, u32[]{:S(2)}) %collective-permute-start.24) | collective-permute-done | bytes 393248 | tf_op jit(solution)/shard_map/ppermute | solution.py:253
  163.1 1.4 slice_bitcast_fusion
  167.6 5.0 %shard_map.309 = (f32[256,768]{1,0:T(8,128)}, bf16[256,768]{1,0:T(8,128)(2,1)}, bf16[4,2,128,192]{3,2,1,0:T(8,128)(2,1)}, f32[8,768]{1,0:T(8,128)}) custom-call(bf16[4,256,768]{2,1,0:T(8,128)(2,1)} %get-tuple-element.176.own_ref, bf16[256,768]{1,0:T(8,128)(2,1)} %copy-done.9, bf16[256,768]{1,0:T(8,128)(2,1)} %copy-done.10, bf16[256,768]{1,0:T(8,128)(2,1)} %copy-done.11, ...), custom_call_target="tpu_custom_call" | custom-call | flops 301989888 | tf_op jit(solution)/shard_map/pallas_call | solution.py:553
  172.7 1.5 fusion.2
  174.2 3.2 %shard_map.310 = bf16[2,4,4,24,768]{4,3,2,1,0:T(8,128)(2,1)} custom-call(s32[1]{0:T(128)} %bitcast.74.place_ref, bf16[4,2,128,192]{3,2,1,0:T(8,128)(2,1)} %bitcast.242, bf16[256,768]{1,0:T(8,128)(2,1)} %get-tuple-element.188.d_ref), custom_call_target="tpu_custom_call" | custom-call | flops 301989888 | tf_op jit(solution)/shard_map/pallas_call | solution.py:553
  177.4 1.9 slice_bitcast_fusion.1
  181.7 3.6 %all-to-all-start.2 = ((bf16[8,128,192]{1,2,0:T(8,128)(2,1)}), bf16[8,128,192]{1,2,0:T(8,128)(2,1)S(1)}, u32[]{:S(2)}, u32[]{:S(2)}) async-start(bf16[8,128,192]{1,2,0:T(8,128)(2,1)} %copy.142), calls=%async_computation.2 | async-start | bytes 786432 | tf_op jit(solution)/shard_map/all_to_all | solution.py:838
  187.1 2.6 collective-permute-start.32
  190.1 1.2 fusion.3
  191.3 2.3 all-to-all-done.2
  194.6 14.4 %shard_map.311 = (bf16[768,576]{1,0:T(8,128)(2,1)}, bf16[4,256,768]{2,1,0:T(8,128)(2,1)}, f32[8,768]{1,0:T(8,128)}, f32[1,576]{1,0:T(1,128)}) custom-call(s32[1]{0:T(128)} %bitcast.50.chip_ref, bf16[1024,192]{1,0:T(8,128)(2,1)} %get-tuple-element.162.q_ref, bf16[1024,192]{1,0:T(8,128)(2,1)} %get-tuple-element.163.k_ref, ...), custom_call_target="tpu_custom_call" | custom-call | flops 3825205248 | bytes 6291456 | tf_op jit(solution)/shard_map/pallas_call | solution.py:503
  213.0 2.3 collective-permute-start.30
  217.2 2.6 collective-permute-start.39
  224.1 1.8 collective-permute-start.46
  226.2 2.9 %collective-permute-start.40 = (f32[192,12]{0,1:T(8,128)S(1)}, f32[192,12]{0,1:T(8,128)S(1)}, u32[]{:S(2)}, u32[]{:S(2)}) collective-permute-start(f32[192,12]{0,1:T(8,128)S(1)} %bitcast.293), channel_id=1, source_target_pairs={{0,24},{8,0},{16,8},{24,16},{1,25},{9,1},{17,9},{25,17},{2,26},{10... | collective-permute-start | bytes 27656 | tf_op jit(solution)/shard_map/ppermute | solution.py:309
  229.3 1.3 collective-permute-done.40
  232.9 7.3 %collective-permute-done.44 = bf16[256,768]{1,0:T(8,128)(2,1)} collective-permute-done((bf16[256,768]{1,0:T(8,128)(2,1)}, bf16[256,768]{1,0:T(8,128)(2,1)}, u32[]{:S(2)}, u32[]{:S(2)}) %collective-permute-start.44) | collective-permute-done | bytes 393248 | tf_op jit(solution)/shard_map/ppermute | solution.py:253
  241.9 7.1 %collective-permute-done.46 = bf16[256,768]{1,0:T(8,128)(2,1)} collective-permute-done((bf16[256,768]{1,0:T(8,128)(2,1)}, bf16[256,768]{1,0:T(8,128)(2,1)}, u32[]{:S(2)}, u32[]{:S(2)}) %collective-permute-start.46) | collective-permute-done | bytes 393248 | tf_op jit(solution)/shard_map/ppermute | solution.py:253
  249.0 1.2 collective-permute-start.37
  250.2 1.5 fusion.12
  252.5 7.3 %collective-permute-done.42 = bf16[256,768]{1,0:T(8,128)(2,1)S(1)} collective-permute-done((bf16[256,768]{1,0:T(8,128)(2,1)}, bf16[256,768]{1,0:T(8,128)(2,1)S(1)}, u32[]{:S(2)}, u32[]{:S(2)}) %collective-permute-start.42) | collective-permute-done | bytes 393248 | tf_op jit(solution)/shard_map/ppermute | solution.py:253
  261.4 1.4 fusion.42
  264.3 2.1 add_convert_fusion.1
  266.5 1.5 multiply_reduce_fusion
  270.0 3.5 %all-to-all-start.3 = ((bf16[8,24,984]{2,1,0:T(8,128)(2,1)}), bf16[8,24,984]{2,1,0:T(8,128)(2,1)S(1)}, u32[]{:S(2)}, u32[]{:S(2)}) async-start(bf16[8,24,984]{2,1,0:T(8,128)(2,1)} %pad_maximum_fusion.12), calls=%async_computation.3 | async-start | bytes 786432 | tf_op jit(solution)/shard_map/all_to_all | solution.py:901
  273.5 2.3 fusion.16
  275.8 6.0 %all-to-all-done.3 = bf16[8,24,984]{2,1,0:T(8,128)(2,1)S(1)} async-done(((bf16[8,24,984]{2,1,0:T(8,128)(2,1)}), bf16[8,24,984]{2,1,0:T(8,128)(2,1)S(1)}, u32[]{:S(2)}, u32[]{:S(2)}) %all-to-all-start.3) | async-done | bytes 377888 | tf_op jit(solution)/shard_map/all_to_all | solution.py:901
  (329 shorter events, 69.2 us)
Async XLA Ops:
  1.8 16.1 %collective-permute-start.3 = (bf16[128,768]{1,0:T(8,128)(2,1)S(1)}, bf16[128,768]{1,0:T(8,128)(2,1)S(1)}, u32[]{:S(2)}, u32[]{:S(2)}) collective-permute-start(bf16[128,768]{1,0:T(8,128)(2,1)S(1)} %get-tuple-element.309), channel_id=1, source_target_pairs={{0,1},{1,0},{2,3},{3,2},{4,5},{5,4},{6,7},{7,6},{8,9},{9,8},{10,11... | collective-permute-start | bytes 589832 | tf_op jit(solution)/shard_map/ppermute | solution.py:253
  7.2 13.6 %all-to-all-start = ((bf16[8,24,960]{2,1,0:T(8,128)(2,1)}), bf16[8,24,960]{2,1,0:T(8,128)(2,1)S(1)}, u32[]{:S(2)}, u32[]{:S(2)}) async-start(bf16[8,24,960]{2,1,0:T(8,128)(2,1)} %pad_maximum_fusion.11), calls=%async_computation | async-start | bytes 786432 | tf_op jit(solution)/shard_map/all_to_all | solution.py:728
  12.3 6.1 %collective-permute-start = (bf16[32,768]{1,0:T(8,128)(2,1)S(1)}, bf16[32,768]{1,0:T(8,128)(2,1)S(1)}, u32[]{:S(2)}, u32[]{:S(2)}) collective-permute-start(bf16[32,768]{1,0:T(8,128)(2,1)S(1)} %fusion.26), channel_id=1, source_target_pairs={{0,8},{8,16},{16,24},{24,0},{1,9},{9,17},{17,25},{25,1},{2,10},{10... | collective-permute-start | bytes 147464 | tf_op jit(solution)/shard_map/ppermute | solution.py:294
  13.9 6.6 %collective-permute-start.1 = (bf16[32,768]{1,0:T(8,128)(2,1)S(1)}, bf16[32,768]{1,0:T(8,128)(2,1)S(1)}, u32[]{:S(2)}, u32[]{:S(2)}) collective-permute-start(bf16[32,768]{1,0:T(8,128)(2,1)S(1)} %fusion.26), channel_id=1, source_target_pairs={{0,16},{8,24},{16,0},{24,8},{1,17},{9,25},{17,1},{25,9},{2,18},{10... | collective-permute-start | bytes 147464 | tf_op jit(solution)/shard_map/ppermute | solution.py:294
  16.5 4.3 %collective-permute-start.2 = (bf16[32,768]{1,0:T(8,128)(2,1)S(1)}, bf16[32,768]{1,0:T(8,128)(2,1)S(1)}, u32[]{:S(2)}, u32[]{:S(2)}) collective-permute-start(bf16[32,768]{1,0:T(8,128)(2,1)S(1)} %fusion.26), channel_id=1, source_target_pairs={{0,24},{8,0},{16,8},{24,16},{1,25},{9,1},{17,9},{25,17},{2,26},{10... | collective-permute-start | bytes 147464 | tf_op jit(solution)/shard_map/ppermute | solution.py:294
  21.1 8.3 %collective-permute-start.11 = (bf16[96,768]{1,0:T(8,128)(2,1)S(1)}, bf16[96,768]{1,0:T(8,128)(2,1)S(1)}, u32[]{:S(2)}, u32[]{:S(2)}) collective-permute-start(bf16[96,768]{1,0:T(8,128)(2,1)S(1)} %bitcast.264), channel_id=1, source_target_pairs={{0,1},{1,0},{2,3},{3,2},{4,5},{5,4},{6,7},{7,6},{8,9},{9,8},{10,11... | collective-permute-start | bytes 442376 | tf_op jit(solution)/shard_map/ppermute | solution.py:253
  21.3 1.4 collective-permute-start.4
  22.7 12.5 %collective-permute-start.5 = (bf16[2,136,768]{2,1,0:T(8,128)(2,1)S(1)}, bf16[2,136,768]{2,1,0:T(8,128)(2,1)S(1)}, u32[]{:S(2)}, u32[]{:S(2)}) collective-permute-start(bf16[2,136,768]{2,1,0:T(8,128)(2,1)S(1)} %get-tuple-element.300), channel_id=1, source_target_pairs={{0,2},{1,3},{2,0},{3,1},{4,6},{5,7},{6,4},{7,5},{8,10},{9,11},{10,... | collective-permute-start | bytes 1253384 | tf_op jit(solution)/shard_map/ppermute | solution.py:253
  24.7 20.6 %collective-permute-start.6 = (bf16[2,136,768]{2,1,0:T(8,128)(2,1)S(1)}, bf16[2,136,768]{2,1,0:T(8,128)(2,1)S(1)}, u32[]{:S(2)}, u32[]{:S(2)}) collective-permute-start(bf16[2,136,768]{2,1,0:T(8,128)(2,1)S(1)} %get-tuple-element.300), channel_id=1, source_target_pairs={{0,4},{1,5},{2,6},{3,7},{4,0},{5,1},{6,2},{7,3},{8,12},{9,13},{10,... | collective-permute-start | bytes 1253384 | tf_op jit(solution)/shard_map/ppermute | solution.py:253
  26.2 19.1 %collective-permute-start.7 = (bf16[2,136,768]{2,1,0:T(8,128)(2,1)S(1)}, bf16[2,136,768]{2,1,0:T(8,128)(2,1)S(1)}, u32[]{:S(2)}, u32[]{:S(2)}) collective-permute-start(bf16[2,136,768]{2,1,0:T(8,128)(2,1)S(1)} %get-tuple-element.300), channel_id=1, source_target_pairs={{0,6},{1,7},{2,4},{3,5},{4,2},{5,3},{6,0},{7,1},{8,14},{9,15},{10,... | collective-permute-start | bytes 1253384 | tf_op jit(solution)/shard_map/ppermute | solution.py:253
  26.3 32.4 %collective-permute-start.10 = (bf16[96,2112]{1,0:T(8,128)(2,1)S(1)}, bf16[96,2112]{1,0:T(8,128)(2,1)S(1)}, u32[]{:S(2)}, u32[]{:S(2)}) collective-permute-start(bf16[96,2112]{1,0:T(8,128)(2,1)S(1)} %pad_maximum_fusion.10), channel_id=1, source_target_pairs={{0,24},{8,0},{16,8},{24,16},{1,25},{9,1},{17,9},{25,17},{2,26},{10... | collective-permute-start | bytes 1216520 | tf_op jit(solution)/shard_map/ppermute | solution.py:294
  29.5 33.6 %collective-permute-start.8 = (bf16[96,2112]{1,0:T(8,128)(2,1)S(1)}, bf16[96,2112]{1,0:T(8,128)(2,1)S(1)}, u32[]{:S(2)}, u32[]{:S(2)}) collective-permute-start(bf16[96,2112]{1,0:T(8,128)(2,1)S(1)} %pad_maximum_fusion.10), channel_id=1, source_target_pairs={{0,8},{8,16},{16,24},{24,0},{1,9},{9,17},{17,25},{25,1},{2,10},{10... | collective-permute-start | bytes 1216520 | tf_op jit(solution)/shard_map/ppermute | solution.py:294
  35.2 29.8 %collective-permute-start.9 = (bf16[96,2112]{1,0:T(8,128)(2,1)S(1)}, bf16[96,2112]{1,0:T(8,128)(2,1)}, u32[]{:S(2)}, u32[]{:S(2)}) collective-permute-start(bf16[96,2112]{1,0:T(8,128)(2,1)S(1)} %pad_maximum_fusion.10), channel_id=1, source_target_pairs={{0,16},{8,24},{16,0},{24,8},{1,17},{9,25},{17,1},{25,9},{2,18},{10... | collective-permute-start | bytes 1216520 | tf_op jit(solution)/shard_map/ppermute | solution.py:294
  45.3 19.8 %collective-permute-start.12 = (bf16[2,96,768]{2,1,0:T(8,128)(2,1)S(1)}, bf16[2,96,768]{2,1,0:T(8,128)(2,1)S(1)}, u32[]{:S(2)}, u32[]{:S(2)}) collective-permute-start(bf16[2,96,768]{2,1,0:T(8,128)(2,1)S(1)} %maximum_select_fusion.4), channel_id=1, source_target_pairs={{0,2},{1,3},{2,0},{3,1},{4,6},{5,7},{6,4},{7,5},{8,10},{9,11},{10,... | collective-permute-start | bytes 884744 | tf_op jit(solution)/shard_map/ppermute | solution.py:253
  45.3 19.8 %collective-permute-start.13 = (bf16[2,96,768]{2,1,0:T(8,128)(2,1)S(1)}, bf16[2,96,768]{2,1,0:T(8,128)(2,1)}, u32[]{:S(2)}, u32[]{:S(2)}) collective-permute-start(bf16[2,96,768]{2,1,0:T(8,128)(2,1)S(1)} %maximum_select_fusion.4), channel_id=1, source_target_pairs={{0,4},{1,5},{2,6},{3,7},{4,0},{5,1},{6,2},{7,3},{8,12},{9,13},{10,... | collective-permute-start | bytes 884744 | tf_op jit(solution)/shard_map/ppermute | solution.py:253
  56.3 15.8 %copy-start.29 = (s32[1024]{0:T(1024)}, s32[1024]{0:T(1024)S(1)}, u32[]{:S(2)}) copy-start(s32[1024]{0:T(1024)S(1)} %fusion.34) | copy-start | bytes 12292
  58.7 8.4 %collective-permute-start.14 = (bf16[2,96,768]{2,1,0:T(8,128)(2,1)S(1)}, bf16[2,96,768]{2,1,0:T(8,128)(2,1)S(1)}, u32[]{:S(2)}, u32[]{:S(2)}) collective-permute-start(bf16[2,96,768]{2,1,0:T(8,128)(2,1)S(1)} %maximum_select_fusion.4), channel_id=1, source_target_pairs={{0,6},{1,7},{2,4},{3,5},{4,2},{5,3},{6,0},{7,1},{8,14},{9,15},{10,... | collective-permute-start | bytes 884744 | tf_op jit(solution)/shard_map/ppermute | solution.py:253
  68.5 5.2 %collective-permute-start.15 = (bf16[4,96,576]{2,1,0:T(8,128)(2,1)S(1)}, bf16[4,96,576]{2,1,0:T(8,128)(2,1)S(1)}, u32[]{:S(2)}, u32[]{:S(2)}) collective-permute-start(bf16[4,96,576]{2,1,0:T(8,128)(2,1)S(1)} %get-tuple-element.294), channel_id=1, source_target_pairs={{0,1},{1,0},{2,3},{3,2},{4,5},{5,4},{6,7},{7,6},{8,9},{9,8},{10,11... | collective-permute-start | bytes 1327112 | tf_op jit(solution)/shard_map/ppermute | solution.py:253
  68.5 20.6 %collective-permute-start.16 = (bf16[256,768]{1,0:T(8,128)(2,1)}, bf16[256,768]{1,0:T(8,128)(2,1)}, u32[]{:S(2)}, u32[]{:S(2)}) collective-permute-start(bf16[256,768]{1,0:T(8,128)(2,1)} %bitcast.30.refs_4_.grad_ref), channel_id=1, source_target_pairs={{0,2},{1,3},{2,0},{3,1},{4,6},{5,7},{6,4},{7,5},{8,10},{9,11},{10,... | collective-permute-start | bytes 1179656 | tf_op jit(solution)/shard_map/ppermute | solution.py:253
  70.3 19.9 %collective-permute-start.17 = (bf16[256,768]{1,0:T(8,128)(2,1)}, bf16[256,768]{1,0:T(8,128)(2,1)}, u32[]{:S(2)}, u32[]{:S(2)}) collective-permute-start(bf16[256,768]{1,0:T(8,128)(2,1)} %bitcast.30.refs_4_.grad_ref), channel_id=1, source_target_pairs={{0,4},{1,5},{2,6},{3,7},{4,0},{5,1},{6,2},{7,3},{8,12},{9,13},{10,... | collective-permute-start | bytes 1179656 | tf_op jit(solution)/shard_map/ppermute | solution.py:253
  70.7 19.6 %collective-permute-start.18 = (bf16[256,768]{1,0:T(8,128)(2,1)}, bf16[256,768]{1,0:T(8,128)(2,1)}, u32[]{:S(2)}, u32[]{:S(2)}) collective-permute-start(bf16[256,768]{1,0:T(8,128)(2,1)} %bitcast.30.refs_4_.grad_ref), channel_id=1, source_target_pairs={{0,6},{1,7},{2,4},{3,5},{4,2},{5,3},{6,0},{7,1},{8,14},{9,15},{10,... | collective-permute-start | bytes 1179656 | tf_op jit(solution)/shard_map/ppermute | solution.py:253
  91.9 23.8 %collective-permute-start.22 = (bf16[4,96,1536]{2,1,0:T(8,128)(2,1)S(1)}, bf16[4,96,1536]{2,1,0:T(8,128)(2,1)}, u32[]{:S(2)}, u32[]{:S(2)}) collective-permute-start(bf16[4,96,1536]{2,1,0:T(8,128)(2,1)S(1)} %get-tuple-element.276), channel_id=1, source_target_pairs={{0,1},{1,0},{2,3},{3,2},{4,5},{5,4},{6,7},{7,6},{8,9},{9,8},{10,11... | collective-permute-start | bytes 3538952 | tf_op jit(solution)/shard_map/ppermute | solution.py:253
  96.3 11.7 %all-to-all-start.1 = ((bf16[8,128,192]{1,2,0:T(8,128)(2,1)}), bf16[8,128,192]{1,2,0:T(8,128)(2,1)S(1)}, u32[]{:S(2)}, u32[]{:S(2)}) async-start(bf16[8,128,192]{1,2,0:T(8,128)(2,1)} %copy.137), calls=%async_computation.1 | async-start | bytes 786432 | tf_op jit(solution)/shard_map/all_to_all | solution.py:782
  112.2 12.3 %collective-permute-start.19 = (bf16[256,768]{1,0:T(8,128)(2,1)}, bf16[256,768]{1,0:T(8,128)(2,1)S(1)}, u32[]{:S(2)}, u32[]{:S(2)}) collective-permute-start(bf16[256,768]{1,0:T(8,128)(2,1)} %get-tuple-element.165.refs_0_), channel_id=1, source_target_pairs={{0,2},{1,3},{2,0},{3,1},{4,6},{5,7},{6,4},{7,5},{8,10},{9,11},{10,... | collective-permute-start | bytes 1179656 | tf_op jit(solution)/shard_map/ppermute | solution.py:253
  112.7 19.4 %collective-permute-start.20 = (bf16[256,768]{1,0:T(8,128)(2,1)}, bf16[256,768]{1,0:T(8,128)(2,1)S(1)}, u32[]{:S(2)}, u32[]{:S(2)}) collective-permute-start(bf16[256,768]{1,0:T(8,128)(2,1)} %get-tuple-element.165.refs_0_), channel_id=1, source_target_pairs={{0,4},{1,5},{2,6},{3,7},{4,0},{5,1},{6,2},{7,3},{8,12},{9,13},{10,... | collective-permute-start | bytes 1179656 | tf_op jit(solution)/shard_map/ppermute | solution.py:253
  113.3 18.9 %collective-permute-start.21 = (bf16[256,768]{1,0:T(8,128)(2,1)}, bf16[256,768]{1,0:T(8,128)(2,1)S(1)}, u32[]{:S(2)}, u32[]{:S(2)}) collective-permute-start(bf16[256,768]{1,0:T(8,128)(2,1)} %get-tuple-element.165.refs_0_), channel_id=1, source_target_pairs={{0,6},{1,7},{2,4},{3,5},{4,2},{5,3},{6,0},{7,1},{8,14},{9,15},{10,... | collective-permute-start | bytes 1179656 | tf_op jit(solution)/shard_map/ppermute | solution.py:253
  124.4 7.8 %copy-start.46 = (bf16[256,768]{1,0:T(8,128)(2,1)}, bf16[256,768]{1,0:T(8,128)(2,1)S(1)}, u32[]{:S(2)}) copy-start(bf16[256,768]{1,0:T(8,128)(2,1)S(1)} %collective-permute-done.19.refs_1_) | copy-start | bytes 1179652
  143.8 12.2 %collective-permute-start.23 = (bf16[256,768]{1,0:T(8,128)(2,1)S(1)}, bf16[256,768]{1,0:T(8,128)(2,1)S(1)}, u32[]{:S(2)}, u32[]{:S(2)}) collective-permute-start(bf16[256,768]{1,0:T(8,128)(2,1)S(1)} %get-tuple-element.270), channel_id=1, source_target_pairs={{0,2},{1,3},{2,0},{3,1},{4,6},{5,7},{6,4},{7,5},{8,10},{9,11},{10,... | collective-permute-start | bytes 1179656 | tf_op jit(solution)/shard_map/ppermute | solution.py:253
  144.1 18.1 %collective-permute-start.24 = (bf16[256,768]{1,0:T(8,128)(2,1)S(1)}, bf16[256,768]{1,0:T(8,128)(2,1)S(1)}, u32[]{:S(2)}, u32[]{:S(2)}) collective-permute-start(bf16[256,768]{1,0:T(8,128)(2,1)S(1)} %get-tuple-element.269), channel_id=1, source_target_pairs={{0,4},{1,5},{2,6},{3,7},{4,0},{5,1},{6,2},{7,3},{8,12},{9,13},{10,... | collective-permute-start | bytes 1179656 | tf_op jit(solution)/shard_map/ppermute | solution.py:253
  145.5 16.8 %collective-permute-start.25 = (bf16[256,768]{1,0:T(8,128)(2,1)S(1)}, bf16[256,768]{1,0:T(8,128)(2,1)S(1)}, u32[]{:S(2)}, u32[]{:S(2)}) collective-permute-start(bf16[256,768]{1,0:T(8,128)(2,1)S(1)} %get-tuple-element.268), channel_id=1, source_target_pairs={{0,6},{1,7},{2,4},{3,5},{4,2},{5,3},{6,0},{7,1},{8,14},{9,15},{10,... | collective-permute-start | bytes 1179656 | tf_op jit(solution)/shard_map/ppermute | solution.py:253
  156.0 8.6 %copy-start = (bf16[2,128,768]{2,1,0:T(8,128)(2,1)S(1)}, bf16[2,128,768]{2,1,0:T(8,128)(2,1)}, u32[]{:S(2)}) copy-start(bf16[2,128,768]{2,1,0:T(8,128)(2,1)} %param.18) | copy-start | bytes 1179652
  156.0 9.6 %copy-start.9 = (bf16[256,768]{1,0:T(8,128)(2,1)}, bf16[256,768]{1,0:T(8,128)(2,1)S(1)}, u32[]{:S(2)}) copy-start(bf16[256,768]{1,0:T(8,128)(2,1)S(1)} %collective-permute-done.23.x_ref) | copy-start | bytes 1179652
  164.4 8.2 %collective-permute-start.26 = (bf16[4,192,768]{2,1,0:T(8,128)(2,1)S(1)}, bf16[4,192,768]{2,1,0:T(8,128)(2,1)S(1)}, u32[]{:S(2)}, u32[]{:S(2)}) collective-permute-start(bf16[4,192,768]{2,1,0:T(8,128)(2,1)S(1)} %slice_bitcast_fusion), channel_id=1, source_target_pairs={{0,1},{1,0},{2,3},{3,2},{4,5},{5,4},{6,7},{7,6},{8,9},{9,8},{10,11... | collective-permute-start | bytes 3538952 | tf_op jit(solution)/shard_map/ppermute | solution.py:253
  179.3 10.8 %collective-permute-start.27 = (bf16[4,4,24,768]{3,2,1,0:T(8,128)(2,1)}, bf16[4,4,24,768]{3,2,1,0:T(8,128)(2,1)}, u32[]{:S(2)}, u32[]{:S(2)}) collective-permute-start(bf16[4,4,24,768]{3,2,1,0:T(8,128)(2,1)} %slice_bitcast_fusion.1), channel_id=1, source_target_pairs={{0,1},{1,0},{2,3},{3,2},{4,5},{5,4},{6,7},{7,6},{8,9},{9,8},{10,11... | collective-permute-start | bytes 1769480 | tf_op jit(solution)/shard_map/ppermute | solution.py:253
  181.7 8.4 %copy-start.1 = (bf16[2,4,4,24,768]{4,3,2,1,0:T(8,128)(2,1)S(1)}, bf16[2,4,4,24,768]{4,3,2,1,0:T(8,128)(2,1)}, u32[]{:S(2)}) copy-start(bf16[2,4,4,24,768]{4,3,2,1,0:T(8,128)(2,1)} %shard_map.310) | copy-start | bytes 3538948
  181.7 11.9 %all-to-all-start.2 = ((bf16[8,128,192]{1,2,0:T(8,128)(2,1)}), bf16[8,128,192]{1,2,0:T(8,128)(2,1)S(1)}, u32[]{:S(2)}, u32[]{:S(2)}) async-start(bf16[8,128,192]{1,2,0:T(8,128)(2,1)} %copy.142), calls=%async_computation.2 | async-start | bytes 786432 | tf_op jit(solution)/shard_map/all_to_all | solution.py:838
  186.3 26.7 %collective-permute-start.31 = (bf16[192,768]{1,0:T(8,128)(2,1)}, bf16[192,768]{1,0:T(8,128)(2,1)S(1)}, u32[]{:S(2)}, u32[]{:S(2)}) collective-permute-start(bf16[192,768]{1,0:T(8,128)(2,1)} %get-tuple-element.273), channel_id=1, source_target_pairs={{0,8},{8,16},{16,24},{24,0},{1,9},{9,17},{17,25},{25,1},{2,10},{10... | collective-permute-start | bytes 884744 | tf_op jit(solution)/shard_map/ppermute | solution.py:309
  187.1 29.2 %collective-permute-start.32 = (bf16[192,768]{1,0:T(8,128)(2,1)}, bf16[192,768]{1,0:T(8,128)(2,1)}, u32[]{:S(2)}, u32[]{:S(2)}) collective-permute-start(bf16[192,768]{1,0:T(8,128)(2,1)} %get-tuple-element.272), channel_id=1, source_target_pairs={{0,16},{8,24},{16,0},{24,8},{1,17},{9,25},{17,1},{25,9},{2,18},{10... | collective-permute-start | bytes 884744 | tf_op jit(solution)/shard_map/ppermute | solution.py:309
  189.7 27.5 %collective-permute-start.33 = (bf16[192,768]{1,0:T(8,128)(2,1)}, bf16[192,768]{1,0:T(8,128)(2,1)}, u32[]{:S(2)}, u32[]{:S(2)}) collective-permute-start(bf16[192,768]{1,0:T(8,128)(2,1)} %get-tuple-element.271), channel_id=1, source_target_pairs={{0,24},{8,0},{16,8},{24,16},{1,25},{9,1},{17,9},{25,17},{2,26},{10... | collective-permute-start | bytes 884744 | tf_op jit(solution)/shard_map/ppermute | solution.py:309
  194.6 16.2 %copy-start.27 = (f32[2,768]{1,0:T(2,128)S(1)}, f32[2,768]{1,0:T(2,128)}, u32[]{:S(2)}) copy-start(f32[2,768]{1,0:T(2,128)} %get-tuple-element.320) | copy-start | bytes 18436
  194.6 16.2 %copy-start.28 = (f32[2,768]{1,0:T(2,128)S(1)}, f32[2,768]{1,0:T(2,128)}, u32[]{:S(2)}) copy-start(f32[2,768]{1,0:T(2,128)} %get-tuple-element.321) | copy-start | bytes 18436
  194.6 20.6 %copy-start.3 = (bf16[4,256,768]{2,1,0:T(8,128)(2,1)S(1)}, bf16[4,256,768]{2,1,0:T(8,128)(2,1)}, u32[]{:S(2)}) copy-start(bf16[4,256,768]{2,1,0:T(8,128)(2,1)} %get-tuple-element.210) | copy-start | bytes 4718596
  211.7 8.1 %collective-permute-start.28 = (bf16[4,24,768]{2,1,0:T(8,128)(2,1)S(1)}, bf16[4,24,768]{2,1,0:T(8,128)(2,1)S(1)}, u32[]{:S(2)}, u32[]{:S(2)}) collective-permute-start(bf16[4,24,768]{2,1,0:T(8,128)(2,1)S(1)} %get-tuple-element.291), channel_id=1, source_target_pairs={{0,2},{1,3},{2,0},{3,1},{4,6},{5,7},{6,4},{7,5},{8,10},{9,11},{10,... | collective-permute-start | bytes 442376 | tf_op jit(solution)/shard_map/ppermute | solution.py:253
  212.4 8.7 %collective-permute-start.29 = (bf16[4,24,768]{2,1,0:T(8,128)(2,1)S(1)}, bf16[4,24,768]{2,1,0:T(8,128)(2,1)S(1)}, u32[]{:S(2)}, u32[]{:S(2)}) collective-permute-start(bf16[4,24,768]{2,1,0:T(8,128)(2,1)S(1)} %get-tuple-element.290), channel_id=1, source_target_pairs={{0,4},{1,5},{2,6},{3,7},{4,0},{5,1},{6,2},{7,3},{8,12},{9,13},{10,... | collective-permute-start | bytes 442376 | tf_op jit(solution)/shard_map/ppermute | solution.py:253
  213.0 8.2 %copy-start.5 = (bf16[768,576]{1,0:T(8,128)(2,1)S(1)}, bf16[768,576]{1,0:T(8,128)(2,1)}, u32[]{:S(2)}) copy-start(bf16[768,576]{1,0:T(8,128)(2,1)} %get-tuple-element.197) | copy-start | bytes 2654212
  213.0 8.3 %copy-start.4 = (bf16[4,256,768]{2,1,0:T(8,128)(2,1)S(1)}, bf16[4,256,768]{2,1,0:T(8,128)(2,1)}, u32[]{:S(2)}) copy-start(bf16[4,256,768]{2,1,0:T(8,128)(2,1)} %get-tuple-element.216) | copy-start | bytes 4718596
  213.0 8.2 %collective-permute-start.30 = (bf16[4,24,768]{2,1,0:T(8,128)(2,1)S(1)}, bf16[4,24,768]{2,1,0:T(8,128)(2,1)S(1)}, u32[]{:S(2)}, u32[]{:S(2)}) collective-permute-start(bf16[4,24,768]{2,1,0:T(8,128)(2,1)S(1)} %get-tuple-element.289), channel_id=1, source_target_pairs={{0,6},{1,7},{2,4},{3,5},{4,2},{5,3},{6,0},{7,1},{8,14},{9,15},{10,... | collective-permute-start | bytes 442376 | tf_op jit(solution)/shard_map/ppermute | solution.py:253
  216.3 6.8 %collective-permute-start.38 = (f32[192,12]{0,1:T(8,128)S(1)}, f32[192,12]{0,1:T(8,128)S(1)}, u32[]{:S(2)}, u32[]{:S(2)}) collective-permute-start(f32[192,12]{0,1:T(8,128)S(1)} %bitcast.295), channel_id=1, source_target_pairs={{0,8},{8,16},{16,24},{24,0},{1,9},{9,17},{17,25},{25,1},{2,10},{10... | collective-permute-start | bytes 27656 | tf_op jit(solution)/shard_map/ppermute | solution.py:309
  217.2 6.9 %collective-permute-start.39 = (f32[192,12]{0,1:T(8,128)S(1)}, f32[192,12]{0,1:T(8,128)S(1)}, u32[]{:S(2)}, u32[]{:S(2)}) collective-permute-start(f32[192,12]{0,1:T(8,128)S(1)} %bitcast.294), channel_id=1, source_target_pairs={{0,16},{8,24},{16,0},{24,8},{1,17},{9,25},{17,1},{25,9},{2,18},{10... | collective-permute-start | bytes 27656 | tf_op jit(solution)/shard_map/ppermute | solution.py:309
  219.8 12.0 %collective-permute-start.41 = (bf16[256,768]{1,0:T(8,128)(2,1)}, bf16[256,768]{1,0:T(8,128)(2,1)}, u32[]{:S(2)}, u32[]{:S(2)}) collective-permute-start(bf16[256,768]{1,0:T(8,128)(2,1)} %get-tuple-element.266), channel_id=1, source_target_pairs={{0,2},{1,3},{2,0},{3,1},{4,6},{5,7},{6,4},{7,5},{8,10},{9,11},{10,... | collective-permute-start | bytes 1179656 | tf_op jit(solution)/shard_map/ppermute | solution.py:253
  221.2 8.0 %copy-start.6 = (bf16[768,576]{1,0:T(8,128)(2,1)S(1)}, bf16[768,576]{1,0:T(8,128)(2,1)}, u32[]{:S(2)}) copy-start(bf16[768,576]{1,0:T(8,128)(2,1)} %get-tuple-element.197) | copy-start | bytes 2654212
  221.2 5.0 %collective-permute-start.34 = (bf16[4,96,576]{2,1,0:T(8,128)(2,1)S(1)}, bf16[4,96,576]{2,1,0:T(8,128)(2,1)S(1)}, u32[]{:S(2)}, u32[]{:S(2)}) collective-permute-start(bf16[4,96,576]{2,1,0:T(8,128)(2,1)S(1)} %dynamic-slice_bitcast_fusion), channel_id=1, source_target_pairs={{0,1},{1,0},{2,3},{3,2},{4,5},{5,4},{6,7},{7,6},{8,9},{9,8},{10,11... | collective-permute-start | bytes 1327112 | tf_op jit(solution)/shard_map/ppermute | solution.py:253
  222.4 17.8 %collective-permute-start.44 = (bf16[256,768]{1,0:T(8,128)(2,1)}, bf16[256,768]{1,0:T(8,128)(2,1)}, u32[]{:S(2)}, u32[]{:S(2)}) collective-permute-start(bf16[256,768]{1,0:T(8,128)(2,1)} %get-tuple-element.261), channel_id=1, source_target_pairs={{0,2},{1,3},{2,0},{3,1},{4,6},{5,7},{6,4},{7,5},{8,10},{9,11},{10,... | collective-permute-start | bytes 1179656 | tf_op jit(solution)/shard_map/ppermute | solution.py:253
  223.1 18.1 %collective-permute-start.45 = (bf16[256,768]{1,0:T(8,128)(2,1)}, bf16[256,768]{1,0:T(8,128)(2,1)}, u32[]{:S(2)}, u32[]{:S(2)}) collective-permute-start(bf16[256,768]{1,0:T(8,128)(2,1)} %get-tuple-element.263), channel_id=1, source_target_pairs={{0,4},{1,5},{2,6},{3,7},{4,0},{5,1},{6,2},{7,3},{8,12},{9,13},{10,... | collective-permute-start | bytes 1179656 | tf_op jit(solution)/shard_map/ppermute | solution.py:253
  224.1 24.9 %collective-permute-start.46 = (bf16[256,768]{1,0:T(8,128)(2,1)}, bf16[256,768]{1,0:T(8,128)(2,1)}, u32[]{:S(2)}, u32[]{:S(2)}) collective-permute-start(bf16[256,768]{1,0:T(8,128)(2,1)} %get-tuple-element.262), channel_id=1, source_target_pairs={{0,6},{1,7},{2,4},{3,5},{4,2},{5,3},{6,0},{7,1},{8,14},{9,15},{10,... | collective-permute-start | bytes 1179656 | tf_op jit(solution)/shard_map/ppermute | solution.py:253
  226.2 4.4 %collective-permute-start.40 = (f32[192,12]{0,1:T(8,128)S(1)}, f32[192,12]{0,1:T(8,128)S(1)}, u32[]{:S(2)}, u32[]{:S(2)}) collective-permute-start(f32[192,12]{0,1:T(8,128)S(1)} %bitcast.293), channel_id=1, source_target_pairs={{0,24},{8,0},{16,8},{24,16},{1,25},{9,1},{17,9},{25,17},{2,26},{10... | collective-permute-start | bytes 27656 | tf_op jit(solution)/shard_map/ppermute | solution.py:309
  230.6 29.2 %collective-permute-start.42 = (bf16[256,768]{1,0:T(8,128)(2,1)}, bf16[256,768]{1,0:T(8,128)(2,1)S(1)}, u32[]{:S(2)}, u32[]{:S(2)}) collective-permute-start(bf16[256,768]{1,0:T(8,128)(2,1)} %get-tuple-element.265), channel_id=1, source_target_pairs={{0,4},{1,5},{2,6},{3,7},{4,0},{5,1},{6,2},{7,3},{8,12},{9,13},{10,... | collective-permute-start | bytes 1179656 | tf_op jit(solution)/shard_map/ppermute | solution.py:253
  231.8 28.0 %collective-permute-start.43 = (bf16[256,768]{1,0:T(8,128)(2,1)}, bf16[256,768]{1,0:T(8,128)(2,1)S(1)}, u32[]{:S(2)}, u32[]{:S(2)}) collective-permute-start(bf16[256,768]{1,0:T(8,128)(2,1)} %get-tuple-element.264), channel_id=1, source_target_pairs={{0,6},{1,7},{2,4},{3,5},{4,2},{5,3},{6,0},{7,1},{8,14},{9,15},{10,... | collective-permute-start | bytes 1179656 | tf_op jit(solution)/shard_map/ppermute | solution.py:253
  240.2 19.6 %collective-permute-start.35 = (bf16[128,576]{1,0:T(8,128)(2,1)S(1)}, bf16[128,576]{1,0:T(8,128)(2,1)S(1)}, u32[]{:S(2)}, u32[]{:S(2)}) collective-permute-start(bf16[128,576]{1,0:T(8,128)(2,1)S(1)} %get-tuple-element.287), channel_id=1, source_target_pairs={{0,8},{8,16},{16,24},{24,0},{1,9},{9,17},{17,25},{25,1},{2,10},{10... | collective-permute-start | bytes 442376 | tf_op jit(solution)/shard_map/ppermute | solution.py:309
  241.2 18.6 %collective-permute-start.36 = (bf16[128,576]{1,0:T(8,128)(2,1)S(1)}, bf16[128,576]{1,0:T(8,128)(2,1)S(1)}, u32[]{:S(2)}, u32[]{:S(2)}) collective-permute-start(bf16[128,576]{1,0:T(8,128)(2,1)S(1)} %get-tuple-element.288), channel_id=1, source_target_pairs={{0,16},{8,24},{16,0},{24,8},{1,17},{9,25},{17,1},{25,9},{2,18},{10... | collective-permute-start | bytes 442376 | tf_op jit(solution)/shard_map/ppermute | solution.py:309
  249.0 10.8 %collective-permute-start.37 = (bf16[128,576]{1,0:T(8,128)(2,1)S(1)}, bf16[128,576]{1,0:T(8,128)(2,1)S(1)}, u32[]{:S(2)}, u32[]{:S(2)}) collective-permute-start(bf16[128,576]{1,0:T(8,128)(2,1)S(1)} %get-tuple-element.285), channel_id=1, source_target_pairs={{0,24},{8,0},{16,8},{24,16},{1,25},{9,1},{17,9},{25,17},{2,26},{10... | collective-permute-start | bytes 442376 | tf_op jit(solution)/shard_map/ppermute | solution.py:309
  259.8 6.7 %collective-permute-start.47 = (bf16[128,768]{1,0:T(8,128)(2,1)}, bf16[128,768]{1,0:T(8,128)(2,1)}, u32[]{:S(2)}, u32[]{:S(2)}) collective-permute-start(bf16[128,768]{1,0:T(8,128)(2,1)} %get-tuple-element.304), channel_id=1, source_target_pairs={{0,1},{1,0},{2,3},{3,2},{4,5},{5,4},{6,7},{7,6},{8,9},{9,8},{10,11... | collective-permute-start | bytes 589832 | tf_op jit(solution)/shard_map/ppermute | solution.py:253
  260.7 7.3 %collective-permute-start.48 = (bf16[96,576]{1,0:T(8,128)(2,1)}, bf16[96,576]{1,0:T(8,128)(2,1)}, u32[]{:S(2)}, u32[]{:S(2)}) collective-permute-start(bf16[96,576]{1,0:T(8,128)(2,1)} %slice.448), channel_id=1, source_target_pairs={{0,1},{1,0},{2,3},{3,2},{4,5},{5,4},{6,7},{7,6},{8,9},{9,8},{10,11... | collective-permute-start | bytes 331784 | tf_op jit(solution)/shard_map/ppermute | solution.py:253
  270.0 11.7 %all-to-all-start.3 = ((bf16[8,24,984]{2,1,0:T(8,128)(2,1)}), bf16[8,24,984]{2,1,0:T(8,128)(2,1)S(1)}, u32[]{:S(2)}, u32[]{:S(2)}) async-start(bf16[8,24,984]{2,1,0:T(8,128)(2,1)} %pad_maximum_fusion.12), calls=%async_computation.3 | async-start | bytes 786432 | tf_op jit(solution)/shard_map/all_to_all | solution.py:901
  (39 other events, 156.8 us)

commit v3 on v2

--- a/solution.py
+++ b/solution.py
@@ -359,14 +359,30 @@
 
 
 def attend_kernel(
-    normed_ref, w_ref, bias_ref, row_ref, column_ref,
-    q_ref, k_ref, v_ref, full_ref, out_ref, p_ref, v_flip, held,
+    place_ref, own_ref, x_ref, y_ref, across_ref, w_near, w_far, vectors_ref, bias_ref, row_ref,
+    normal_ref, normed_ref, w_ref, q_ref, k_ref, v_ref, full_ref, out_ref, p_ref,
+    v_flip, held, column_ref,
 ):
     head = pl.program_id(0)
     length, count = q_ref.shape
 
     @pl.when(head == 0)
     def first():
+        chip, core, column = place_ref[0] // 2, place_ref[0] % 2, place_ref[1]
+        rows = out_ref.shape[2]
+        for item, mine in enumerate((own_ref, x_ref, y_ref, across_ref)):
+            for side in range(2):
+                place = pl.ds(pl.multiple_of((2 * (chip ^ item) + side) * rows, rows), rows)
+                normal, _ = norm_parts(mine[side, :rows].astype(jnp.float32))
+                normal_ref[place] = normal.astype(jnp.bfloat16)
+                normed = normal * vectors_ref[0:1] + vectors_ref[1:2]
+                normed_ref[place] = normed.astype(jnp.bfloat16)
+        columns, half, _ = w_near.shape
+        for shift in range(columns):
+            top = lax.rem(column - shift + columns, columns) * 2
+            w_ref[pl.ds(pl.multiple_of((top + core) * half, 16), half)] = w_near[shift]
+            w_ref[pl.ds(pl.multiple_of((top + 1 - core) * half, 16), half)] = w_far[shift]
+        column_ref[...] = jnp.broadcast_to(row_ref[...], (128, length)).T
         for start in range(0, length, BLOCK):
             rows = pl.ds(start, BLOCK)
             product = dot(normed_ref[rows], w_ref[...]) + bias_ref[...]
@@ -383,7 +399,7 @@
         causal = lax.broadcasted_iota(jnp.int32, shape, 0) <= start + lax.broadcasted_iota(
             jnp.int32, shape, 1
         )
-        same = column_ref[:stop] == row_ref[:, start:stop]
+        same = column_ref[:stop, 0:1] == row_ref[:, start:stop]
         scores = jnp.where(causal & same, scores, -1000000000.0)
         expo = jnp.exp(scores - jnp.max(scores, 0, keepdims=True))
         probs = (expo * (1.0 / jnp.sum(expo, 0, keepdims=True))).astype(jnp.bfloat16)
@@ -392,14 +408,16 @@
 
     @pl.when(head == pl.num_programs(0) - 1)
     def last():
-        full = held[...].T
-        full_ref[...] = full
-        out_ref[...] = full.astype(jnp.bfloat16)
+        full_ref[...] = held[...]
+        blocks, _, rows = out_ref.shape
+        for block in range(blocks):
+            out_ref[block] = held[:, block * rows : (block + 1) * rows].astype(jnp.bfloat16)
 
 
 def attend_back_kernel(
-    chip_ref, q_ref, k_ref, v_ref, d_ref, full_ref, normed_ref, w_ref, normal_ref, p_ref,
-    grad_ref, first_ref, sums_ref, bias_ref, k_flip, dots, dq, dk, dv, d_all,
+    chip_ref, q_ref, k_ref, v_ref, d_ref, full_ref, normed_ref, w_ref, normal_ref, terms_in, p_ref,
+    near_ref, far_ref, first_0, first_1, first_2, first_3, terms_ref,
+    k_flip, dots, dq, dk, dv, d_all, d_held, grad,
 ):
     head = pl.program_id(0)
     length, count = q_ref.shape
@@ -407,14 +425,19 @@
     @pl.when(head == 0)
     def first():
         k_flip[...] = flipped(k_ref[...])
-        dots[...] = (d_ref[...].astype(jnp.float32) * full_ref[...]).T
+        blocks, _, rows = d_ref.shape
+        for block in range(blocks):
+            place = pl.ds(block * rows, rows)
+            d_out = d_ref[block].astype(jnp.float32)
+            d_held[place] = d_out.T.astype(jnp.bfloat16)
+            dots[:, place] = d_out * full_ref[:, place]
         dk[...] = jnp.zeros_like(dk)
         dv[...] = jnp.zeros_like(dv)
 
     mask = head_mask(head, count)
     for start in range(0, length, BLOCK):
         stop = start + BLOCK
-        d_out = d_ref[start:stop] * mask
+        d_out = d_held[start:stop] * mask
         probs = p_ref[0, :stop, start:stop]
         row_dots = jnp.sum(dots[head_rows(head), start:stop], 0, keepdims=True)
         d_probs = dot_right(v_ref[:stop], d_out)
@@ -431,16 +454,41 @@
             d_all[rows] = jnp.concatenate([d_queries * 0.125, dk[rows], dv[rows]], 1).astype(
                 jnp.bfloat16
             )
-        bias_ref[...] = jnp.sum(d_all[...].astype(jnp.float32), 0, keepdims=True)
-        grad_ref[...] = dot_left(normed_ref[...], d_all[...]).astype(jnp.bfloat16)
-        sums_ref[...] = jnp.zeros_like(sums_ref)
+        width = normed_ref.shape[1]
+        lane = lax.broadcasted_iota(jnp.int32, (1, width), 1) - chip_ref[0] * count
+        inside = ((lane >= 0) & (lane < count)).astype(jnp.float32)
+        bias = jnp.sum(d_all[...].astype(jnp.float32), 0, keepdims=True)
+        bias = [
+            jnp.concatenate([bias[:, item * count : (item + 1) * count]] * GROUPS, 1) * inside
+            for item in (0, 2)
+        ]
+        grad[...] = dot_left(normed_ref[...], d_all[...])
+        columns, half, _ = near_ref.shape
+        for column in range(columns):
+            for order, part_ref in enumerate((near_ref, far_ref)):
+                start = pl.multiple_of((2 * column + (chip_ref[1] ^ order)) * half, half)
+                part_ref[column] = grad[pl.ds(start, half)].astype(jnp.bfloat16)
+        gain = shift = jnp.zeros((1, width), jnp.float32)
         for item in range(GROUPS):
             size = length // GROUPS
             rows = pl.ds(pl.multiple_of((chip_ref[0] ^ item) * size, size), size)
             d_first = dot_right(d_all[rows], w_ref[...])
-            sums_ref[0:1] += jnp.sum(d_first * normal_ref[rows], 0, keepdims=True)
-            sums_ref[1:2] += jnp.sum(d_first, 0, keepdims=True)
-            first_ref[item] = d_first.astype(jnp.bfloat16)
+            gain += jnp.sum(d_first * normal_ref[rows].astype(jnp.float32), 0, keepdims=True)
+            shift += jnp.sum(d_first, 0, keepdims=True)
+            (first_0, first_1, first_2, first_3)[item][...] = d_first.astype(jnp.bfloat16)
+        row = lax.broadcasted_iota(jnp.int32, (16, 1), 0)
+        terms = terms_in[...]
+        for item, value in ((0, bias[0]), (1, bias[1]), (4, gain), (5, shift)):
+            terms = jnp.where(row == item, value, terms)
+        coarse = terms.astype(jnp.bfloat16).astype(jnp.float32)
+        fine = terms - coarse
+        columns = terms_ref.shape[0]
+        size = width // columns
+        for column in range(columns):
+            part = slice(column * size, (column + 1) * size)
+            terms_ref[column] = jnp.concatenate(
+                [coarse[:, part], fine[:, part], jnp.zeros((16, count * 3 - 2 * size), jnp.float32)], 1
+            ).astype(jnp.bfloat16)
 
 
 def whole(*shape):
@@ -453,35 +501,41 @@
     )
 
 
-def attend(normed, weights, bias, segments):
-    length, width = normed.shape
-    count = weights.shape[1] // 3
+def attend(place, column, mine, near, far, vectors, bias, segments):
+    _, padded, width = mine[0].shape
+    columns, half, _ = near.shape
+    length = segments.shape[0]
+    count = near.shape[2] // 3
     heads = count // HEAD_DIM
     shape = (length, count)
-    low = jax.ShapeDtypeStruct(shape, jnp.bfloat16)
+    blocks = (2 * GROUPS, count, length // (2 * GROUPS))
     probs = pl.BlockSpec((1, length, length), lambda head: (head, 0, 0))
-    queries, keys, values, full, out, probs = pl.pallas_call(
+    normal, normed, weights, queries, keys, values, full, out, probs = pl.pallas_call(
         attend_kernel,
         grid=(heads,),
-        in_specs=[
-            whole(length, width),
-            whole(width, 3 * count),
-            whole(1, 3 * count),
-            whole(1, length),
-            whole(length, 1),
-        ],
-        out_specs=[whole(*shape)] * 5 + [probs],
+        in_specs=[pl.BlockSpec(memory_space=pltpu.SMEM)]
+        + [whole(2, padded, width)] * 4
+        + [whole(*near.shape)] * 2
+        + [whole(8, width), whole(1, 3 * count), whole(1, length)],
+        out_specs=[whole(length, width)] * 2
+        + [whole(width, 3 * count)]
+        + [whole(*shape)] * 3
+        + [whole(count, length), whole(*blocks), probs],
         out_shape=[
-            low,
-            low,
-            low,
-            jax.ShapeDtypeStruct(shape, jnp.float32),
-            low,
-            jax.ShapeDtypeStruct((heads, length, length), jnp.bfloat16),
+            low(length, width),
+            low(length, width),
+            low(width, 3 * count),
+            low(*shape),
+            low(*shape),
+            low(*shape),
+            one(count, length),
+            low(*blocks),
+            low(heads, length, length),
         ],
         scratch_shapes=[
             pltpu.VMEM((count, length), jnp.bfloat16),
             pltpu.VMEM((count, length), jnp.float32),
+            pltpu.VMEM((length, 128), jnp.float32),
         ],
         compiler_params=kernel_params(),
         cost_estimate=pl.CostEstimate(
@@ -489,11 +543,11 @@
             bytes_accessed=2 * heads * length * length,
             transcendentals=heads * length * length,
         ),
-    )(normed, weights, bias[None], segments[None], segments[:, None])
-    return out, (queries, keys, values), (full, probs)
-
-
-def attend_back(chip, projected, kept, d_out, normed, weights, normal):
+    )(jnp.stack([place, column]), *mine, near, far, vectors, bias[None], segments[None])
+    return out, (queries, keys, values), (full, probs), (normal, normed, weights)
+
+
+def attend_back(place, columns, projected, kept, d_out, normed, weights, normal, terms):
     length, width = normed.shape
     count = d_out.shape[1]
     heads = count // HEAD_DIM
@@ -504,24 +558,33 @@
         attend_back_kernel,
         grid=(heads,),
         in_specs=[pl.BlockSpec(memory_space=pltpu.SMEM)]
-        + [whole(*shape)] * 5
+        + [whole(*shape)] * 3
         + [
+            whole(*d_out.shape),
+            whole(count, length),
             whole(length, width),
             whole(width, 3 * count),
             whole(length, width),
+            whole(16, width),
             pl.BlockSpec((1, length, length), lambda head: (head, 0, 0)),
         ],
         out_specs=[
-            whole(width, 3 * count),
-            whole(GROUPS, size, width),
-            whole(8, width),
-            whole(1, 3 * count),
+            whole(columns, width // columns // 2, 3 * count),
+            whole(columns, width // columns // 2, 3 * count),
+            whole(size, width),
+            whole(size, width),
+            whole(size, width),
+            whole(size, width),
+            whole(columns, 16, 3 * count),
         ],
         out_shape=[
-            jax.ShapeDtypeStruct((width, 3 * count), jnp.bfloat16),
-            jax.ShapeDtypeStruct((GROUPS, size, width), jnp.bfloat16),
-            jax.ShapeDtypeStruct((8, width), jnp.float32),
-            jax.ShapeDtypeStruct((1, 3 * count), jnp.float32),
+            low(columns, width // columns // 2, 3 * count),
+            low(columns, width // columns // 2, 3 * count),
+            low(size, width),
+            low(size, width),
+            low(size, width),
+            low(size, width),
+            low(columns, 16, 3 * count),
         ],
         scratch_shapes=[
             pltpu.VMEM((count, length), jnp.bfloat16),
@@ -530,6 +593,8 @@
             pltpu.VMEM(shape, jnp.float32),
             pltpu.VMEM(shape, jnp.float32),
             pltpu.VMEM((length, 3 * count), jnp.bfloat16),
+            pltpu.VMEM(shape, jnp.bfloat16),
+            pltpu.VMEM((width, 3 * count), jnp.float32),
         ],
         compiler_params=kernel_params(),
         cost_estimate=pl.CostEstimate(
@@ -537,7 +602,7 @@
             bytes_accessed=2 * heads * length * length,
             transcendentals=0,
         ),
-    )(chip[None], *projected, d_out, full, normed, weights, normal, probs)
+    )(jnp.stack([place // 2, place % 2]), *projected, d_out, full, normed, weights, normal, terms, probs)
 
 
 def one(*shape):
@@ -563,35 +628,49 @@
 
 
 def second_kernel(attended_ref, w_ref, in_ref, vectors_ref, middle_ref, second_ref):
-    groups, seqs, rows, count = attended_ref.shape
+    blocks, count, rows = attended_ref.shape
+    groups, seqs = blocks // 2, 2
     for seq in range(seqs):
         place = pl.ds(seq * rows, rows)
         middle = in_ref[place].astype(jnp.float32) + vectors_ref[0:1]
         for group in range(groups):
-            middle += dot(attended_ref[group, seq], w_ref[group * count : (group + 1) * count])
+            middle += dot_left(
+                attended_ref[seqs * group + seq], w_ref[group * count : (group + 1) * count]
+            )
         middle_ref[place] = middle
         normal, _ = norm_parts(middle)
         second_ref[place] = (normal * vectors_ref[1:2] + vectors_ref[2:3]).astype(jnp.bfloat16)
 
 
 def branch_kernel(
-    own_ref, x_ref, y_ref, across_ref, grad_ref, middle_ref, vectors_ref, w_ref,
-    d_middle_ref, d_branch_ref, d_attended_ref, sums_ref,
+    place_ref, own_ref, x_ref, y_ref, across_ref, grad_ref, middle_ref, vectors_ref, w_ref,
+    attended_ref, d_middle_ref, d_attended_ref, sums_ref, near_ref, far_ref, total,
 ):
-    groups, seqs, rows, count = d_attended_ref.shape
-    d_second = total_of([own_ref[0], x_ref[...], y_ref[...], across_ref[...]])
+    blocks, count, rows = d_attended_ref.shape
+    groups, seqs = blocks // 2, 2
+    d_second = total_of([own_ref[...], x_ref[...], y_ref[...], across_ref[...]])
     normal, scale = norm_parts(middle_ref[...])
     d_middle = grad_ref[...].astype(jnp.float32) + norm_back(
         normal, scale, vectors_ref[1:2], d_second
     )
     d_middle_ref[...] = d_middle
     d_branch = d_middle.astype(jnp.bfloat16)
-    d_branch_ref[...] = d_branch
     for group in range(groups):
-        part = dot_right(d_branch, w_ref[group * count : (group + 1) * count])
+        part = dot_right(w_ref[group * count : (group + 1) * count], d_branch)
         part = part.astype(jnp.bfloat16)
         for seq in range(seqs):
-            d_attended_ref[group, seq] = part[seq * rows : (seq + 1) * rows]
+            d_attended_ref[seqs * group + seq] = part[:, seq * rows : (seq + 1) * rows]
+        total[group * count : (group + 1) * count] = sum(
+            dot(attended_ref[seqs * group + seq], d_branch[seq * rows : (seq + 1) * rows])
+            for seq in range(seqs)
+        )
+    chips_count, columns, share, _ = near_ref.shape
+    for order, grad_out_ref in enumerate((near_ref, far_ref)):
+        for item in range(chips_count):
+            owner = place_ref[0] ^ (2 * item + order)
+            for column in range(columns):
+                start = pl.multiple_of((column * blocks + owner) * share, 8)
+                grad_out_ref[item, column] = total[pl.ds(start, share)].astype(jnp.bfloat16)
     sums_ref[...] = jnp.zeros_like(sums_ref)
     sums_ref[0:1] = jnp.sum(d_branch.astype(jnp.float32), 0, keepdims=True)
     sums_ref[1:2] = jnp.sum(grad_ref[...].astype(jnp.float32), 0, keepdims=True)
@@ -601,7 +680,7 @@
 
 def hidden_kernel(*refs):
     rows_refs, grad_refs = refs[:4], refs[4:8]
-    w_up, w_down, bias_ref, act_ref, d_upper_ref, d_rows_ref, sums_ref = refs[8:]
+    w_up, w_down, bias_ref, act_ref, d_upper_ref, *d_rows_refs, sums_ref = refs[8:]
     tokens = rows_refs[0].shape[0]
     skip = (grad_refs[0].shape[0] - tokens) // 2
     slope = 0.7978845608028654
@@ -619,17 +698,17 @@
         d_upper = (d_act * rise).astype(jnp.bfloat16)
         d_upper_ref[place] = d_upper
         sums_ref[0:1] += jnp.sum(d_upper.astype(jnp.float32), 0, keepdims=True)
-        d_rows_ref[item] = dot_right(d_upper, w_up[...]).astype(jnp.bfloat16)
+        d_rows_refs[item][...] = dot_right(d_upper, w_up[...]).astype(jnp.bfloat16)
 
 
 def hidden_weights_kernel(core_ref, *refs):
     rows_refs, grad_refs = refs[:4], refs[4:8]
-    act_ref, d_upper_ref, w_down, down_ref, late_ref, up, down = refs[8:]
+    act_ref, d_upper_ref, w_down, *down_refs, late_near, late_far, up, down = refs[8:]
     tokens = rows_refs[0].shape[0]
     skip = (grad_refs[0].shape[0] - tokens) // 2
     for item in range(4):
         place = pl.ds(item * tokens, tokens)
-        down_ref[item] = dot(act_ref[place], w_down[...]).astype(jnp.bfloat16)
+        down_refs[item][...] = dot(act_ref[place], w_down[...]).astype(jnp.bfloat16)
         up_term = dot_left(rows_refs[item][...], d_upper_ref[place])
         down_term = dot_left(act_ref[place], grad_refs[item][skip : skip + tokens])
         if item == 0:
@@ -638,36 +717,20 @@
         else:
             up[...] += up_term
             down[...] += down_term
-    _, columns, both, width = late_ref.shape
+    columns, both, width = late_near.shape
     half, side = both // 2, width // 2
     for order in range(2):
+        late_ref = (late_near, late_far)[order]
         start = pl.multiple_of((core_ref[0] ^ order) * side, side)
         for column in range(columns):
             top = column * both
             for part in range(2):
-                late_ref[order, column, :half, part * side : (part + 1) * side] = up[
+                late_ref[column, :half, part * side : (part + 1) * side] = up[
                     top + part * half : top + (part + 1) * half, pl.ds(start, side)
                 ].astype(jnp.bfloat16)
-            late_ref[order, column, half:] = down[
+            late_ref[column, half:] = down[
                 pl.ds(pl.multiple_of(start + column * half, 8), half)
             ].astype(jnp.bfloat16)
-
-
-def out_weight_kernel(place_ref, attended_ref, d_ref, grad_ref, total):
-    groups, seqs, rows, count = attended_ref.shape
-    for group in range(groups):
-        total[group * count : (group + 1) * count] = sum(
-            dot_left(attended_ref[group, seq], d_ref[seq * rows : (seq + 1) * rows])
-            for seq in range(seqs)
-        )
-    cores, chips_count, columns, share, _ = grad_ref.shape
-    plane = cores * chips_count
-    for order in range(cores):
-        for item in range(chips_count):
-            owner = place_ref[0] ^ (2 * item + order)
-            for column in range(columns):
-                start = pl.multiple_of((column * plane + owner) * share, 8)
-                grad_ref[order, item, column] = total[pl.ds(start, share)].astype(jnp.bfloat16)
 
 
 def plane_local(
@@ -747,9 +810,8 @@
     small = jnp.pad(small[:, share], ((0, -columns % 8), (0, 0)))
     small = in_order(small, swap(small, CORE), core, 0)
     mine = chips(jnp.concatenate([mine, small], 1))
-    mine = chips_order(mine, chip).reshape(plane, -1, width)
-    small = mine[:, rows : rows + columns].transpose(1, 0, 2)
-    mine = mine[:, :rows].reshape(length, width)
+    small = chips_order([item[:, rows : rows + columns] for item in mine], chip)
+    small = small.reshape(plane, columns, width).transpose(1, 0, 2)
     vectors = small[:, :, : 8 * share].astype(jnp.float32).reshape(owners, 8, share)
     vectors = vectors.transpose(1, 0, 2).reshape(8, width)
     bq, bv, bo, bd, gain_one, shift_one, gain_two, shift_two = [vectors[i] for i in range(8)]
@@ -757,30 +819,28 @@
     bu = pick(bu.reshape(columns, GROUPS, 2, ff_share), chip, 1).transpose(1, 0, 2).reshape(-1)
     segments = pick(small[:, :, 8 * share + ff_share : small_size], column)
     segments = pick(segments.reshape(plane, seqs, rows), core, 1).reshape(length)
-    segments = segments.astype(jnp.int32)
-    normal_all, _ = norm_parts(mine.astype(jnp.float32))
-    normed = (normal_all * gain_one + shift_one).astype(jnp.bfloat16)
+    segments = segments.astype(jnp.float32)
+    first_vectors = jnp.stack([gain_one, shift_one] + [jnp.zeros_like(bo)] * 6)
     own_columns = lambda item: lax.dynamic_slice_in_dim(item, chip * group_width, group_width)
     bias_here = jnp.concatenate([own_columns(bq), jnp.zeros((group_width,)), own_columns(bv)])
 
     w_out = in_order(w_out, swap(w_out, CORE), core, 0)
     mine, w_out, own_low = tie(mine, w_out, cotangent.reshape(tokens, width))
     w_out = chips(w_out)
-    normed, bias_here, segments, later, w_out, own_low = tie(
-        normed, bias_here, segments, later, w_out, own_low
+    first_vectors, bias_here, segments, later, w_out, own_low = tie(
+        first_vectors, bias_here, segments, later, w_out, own_low
     )
     beside = chips(own_low)
-    w_qkv = column_order([item[:, 2 * width :] for item in later], column)
-    w_qkv = in_order(w_qkv, swap(w_qkv, CORE), core, 1).reshape(width, 3 * group_width)
-    attended, projected, kept = attend(normed, w_qkv, bias_here, segments)
+    w_qkv = jnp.stack([item[:, 2 * width :] for item in later])
+    attended, projected, kept, (normal_all, normed, w_qkv) = attend(
+        place, column, mine, w_qkv, swap(w_qkv, CORE), first_vectors, bias_here, segments
+    )
     attended, beside, later, w_out = tie(attended, beside, later, w_out)
     later = column_order([item[:, : 2 * width] for item in later], column)
     later_far = swap(later, CORE)
     w_out = chips_order(w_out, chip).reshape(plane, columns, share, width)
     w_out = w_out.transpose(1, 0, 2, 3).reshape(width, width)
-    attended = attended.reshape(plane, rows, group_width)
     attended = lax.all_to_all(attended, "seq", 0, 0, tiled=True)
-    attended = attended.reshape(GROUPS, seqs, rows, group_width)
     block_in = hidden_in.reshape(tokens, width)
     norm_vectors = jnp.stack([bo, gain_two, shift_two] + [jnp.zeros_like(bo)] * 5)
     middle, second = run(
@@ -803,96 +863,87 @@
     w_up = w_up.reshape(columns, half, 2, width).transpose(0, 2, 1, 3).reshape(width, width)
 
     many = GROUPS * tokens
-    act, d_upper, d_rows, d_bu = run(
+    act, d_upper, *d_rows, d_bu = run(
         hidden_kernel,
         (*second, *beside, w_up, w_down, bu[None]),
-        (low(many, width), low(many, width), low(GROUPS, tokens, width), one(8, width)),
+        (low(many, width), low(many, width), *[low(tokens, width)] * 4, one(8, width)),
         12 * many * width * width,
     )
     d_second = [swap(d_rows[i], mask) for i, mask in ((1, NEAR_X), (2, NEAR_Y), (3, ACROSS))]
     act, d_rows = tie(act, d_rows)
-    down, late = run(
+    *down, late, late_far = run(
         hidden_weights_kernel,
         (*second, *beside, act, d_upper, w_down),
-        (low(GROUPS, tokens, width), low(2, columns, 2 * half, width)),
+        (*[low(tokens, width)] * 4, *[low(columns, 2 * half, width)] * 2),
         12 * many * width * width,
         [pltpu.VMEM((width, width), jnp.float32)] * 2,
         (core,),
     )
-    d_second, late, down = tie(d_second, late, down)
-    late = plus(late[0], swap(late[1], CORE))
-    d_middle, d_branch, d_attended, sums = run(
+    d_second, late, late_far, down = tie(d_second, late, late_far, down)
+    late = plus(late, swap(late_far, CORE))
+    d_middle, d_attended, sums, grad_out, grad_far = run(
         branch_kernel,
-        (d_rows, *d_second, cotangent.reshape(tokens, width), middle, norm_vectors, w_out),
+        (
+            d_rows[0],
+            *d_second,
+            cotangent.reshape(tokens, width),
+            middle,
+            norm_vectors,
+            w_out,
+            attended,
+        ),
         (
             one(tokens, width),
-            low(tokens, width),
-            low(GROUPS, seqs, rows, group_width),
+            low(plane, group_width, rows),
             one(8, width),
+            *[low(GROUPS, columns, share, width)] * 2,
         ),
-        2 * tokens * width * width,
-    )
-    d_attended, d_branch, late = tie(d_attended, d_branch, late)
-    late = column_send(late, column, columns)
-    d_attended = d_attended.reshape(plane, rows, group_width)
-    d_attended = lax.all_to_all(d_attended, "seq", 0, 0, tiled=True)
-    (grad_out,) = run(
-        out_weight_kernel,
-        (attended, d_branch),
-        (low(2, GROUPS, columns, share, width),),
-        2 * tokens * width * width,
+        4 * tokens * width * width,
         [pltpu.VMEM((width, width), jnp.float32)],
         (place,),
     )
-    grad_out = plus(grad_out[0], swap(grad_out[1], CORE))
-    d_attended, grad_out, down = tie(d_attended, grad_out, down)
+    d_attended, late = tie(d_attended, late)
+    late = column_send(late, column, columns)
+    d_attended = lax.all_to_all(d_attended, "seq", 0, 0, tiled=True)
+    grad_out = plus(grad_out, swap(grad_far, CORE))
+    d_attended, down, late[1] = tie(d_attended, down, late[1])
     grad_out = [grad_out[0]] + [
         swap(grad_out[i], mask) for i, mask in ((1, NEAR_X), (2, NEAR_Y), (3, ACROSS))
     ]
     down = [down[0]] + [
         swap(down[i], mask) for i, mask in ((1, NEAR_X), (2, NEAR_Y), (3, ACROSS))
     ]
-    d_attended = d_attended.reshape(length, group_width)
-    grad_qkv, d_first, d_sums, d_bias = attend_back(
-        chip, projected, kept, d_attended, normed, w_qkv, normal_all
-    )
-    grad_qkv, d_first, grad_out, late = tie(grad_qkv, d_first, grad_out, late)
-    d_bias = d_bias.reshape(3, group_width)
-
-    grad_qkv = grad_qkv.reshape(columns, 2, half, -1)
-    grad_qkv = plus(pick(grad_qkv, core, 1), swap(pick(grad_qkv, 1 - core, 1), CORE))
+    d_bu = lax.dynamic_update_slice_in_dim(
+        jnp.zeros((columns, GROUPS, 2, ff_share), jnp.float32),
+        d_bu[0].reshape(2, columns, 1, ff_share).transpose(1, 2, 0, 3),
+        chip,
+        1,
+    )
+    d_bu = d_bu.reshape(owners, -1, share).transpose(1, 0, 2).reshape(-1, width)
+    blank = jnp.zeros((2, width), jnp.float32)
+    terms = jnp.concatenate([blank, sums[:2], blank, sums[2:4], d_bu, blank, blank])
+    grad_near, grad_far, *d_first, terms = attend_back(
+        place, columns, projected, kept, d_attended, normed, w_qkv, normal_all, terms
+    )
+    grad_near, grad_far, terms, grad_out, down, late = tie(
+        grad_near, grad_far, terms, grad_out, down, late
+    )
+
+    grad_qkv = plus(grad_near, swap(grad_far, CORE))
     grad_out = total_of(grad_out).astype(jnp.bfloat16).reshape(columns, -1, 3 * group_width)
-    last = column_send(jnp.concatenate([grad_qkv, grad_out], 1), column, columns)
+    last = jnp.concatenate([grad_qkv, grad_out, terms], 1)
+    last = lax.all_to_all(last, "dp", 0, 0, tiled=True)
     d_first = [d_first[0]] + [
         swap(d_first[item], mask) for item, mask in ((1, NEAR_X), (2, NEAR_Y), (3, ACROSS))
     ]
 
-    def placed(item):
-        zeros = jnp.zeros((width,), jnp.float32)
-        return lax.dynamic_update_slice_in_dim(zeros, item, chip * group_width, 0)
-
-    d_bu = d_bu[0].reshape(2, columns, 1, ff_share).transpose(1, 2, 0, 3)
-    d_bu = lax.dynamic_update_slice_in_dim(
-        jnp.zeros((columns, GROUPS, 2, ff_share), jnp.float32), d_bu, chip, 1
-    )
-    terms = [
-        placed(d_bias[0]),
-        placed(d_bias[2]),
-        sums[0],
-        sums[1],
-        d_sums[0],
-        d_sums[1],
-        sums[2],
-        sums[3],
-    ]
-    terms = jnp.concatenate([jnp.stack(terms).T, d_bu.reshape(width, -1)], -1)
-
-    terms = column_send(terms.reshape(columns, plane * share, -1), column, columns)
-    last, late, terms, down = tie(last, late, terms, down)
-    last, late, terms = total_of(last), total_of(late), total_of(terms)
+    last, late, d_first = tie(last, late, d_first)
+    last, late = jnp.sum(last.astype(jnp.float32), 0), total_of(late)
     grad_up = jnp.concatenate([late[:half, : width // 2], late[:half, width // 2 :]])
     grad_down = late[half:]
-    grad_out = last[half:].reshape(share, width)
+    grad_out = last[half:-16].reshape(share, width)
+    terms = last[-16:, :group_width] + last[-16:, group_width : 2 * group_width]
+    terms = terms[:12].T
     last = last[:half].astype(jnp.bfloat16)
     last = in_order(last, swap(last, CORE), core, 0).reshape(plane * share, -1)
     coarse = lax.reduce_precision(terms, 8, 7)
@@ -904,8 +955,8 @@
     grad_up = grad_up.transpose(1, 2, 0, 3).reshape(share, hidden)
     terms = jnp.sum(last[..., 3 * group_width : -columns * ff_share], 0)
     terms = terms[:, : terms.shape[1] // 2] + terms[:, terms.shape[1] // 2 :]
-    g_bu = terms[:, 8:].reshape(-1)
-    terms = terms[:, :8].T
+    terms = terms.T
+    g_bu = terms[8:].reshape(-1)
     g_bq, g_bv, g_bo, g_bd, g_g1, g_s1, g_g2, g_s2 = [terms[i] for i in range(8)]
     grad_qkv = last[::2, :, : 3 * group_width].reshape(GROUPS, share, 3, group_width)
     grad_qkv = grad_qkv.transpose(2, 1, 0, 3).reshape(3, share, width)

time: 293 us -> 263 us (0.90)
  local copies, waits for them, and re-layouts: 52.1 us -> 27.7 us
  waiting for transfers between devices: 78.1 us -> 89 us
  starting transfers between devices: 69.7 us -> 61.8 us
  other arithmetic: 28.1 us -> 20.7 us
    ppermute x9 -> x3, starting transfers between devices: 13.1 us -> 1.37 us  [column_send(): parts.append(lax.ppermute(sent, 'dp', perm))]
    ppermute x9 -> x3, waiting for transfers between devices: 1.33 us -> 11.9 us  [column_send(): parts.append(lax.ppermute(sent, 'dp', perm))]
    squeeze x5 -> x0, local copies, waits for them, and re-layouts: 6.73 us -> none  [the longest x1 1.94 us: plane_local(): grad_out = plus(grad_out[0], swap(grad_out[1], CORE))]
    ppermute x6, waiting for transfers between devices: 4.91 us -> 10.8 us  [column_parts(): parts.append(lax.ppermute(value, 'dp', perm))]
    all_to_all x0 -> x1, starting transfers between devices: none -> 4.3 us  [plane_local(): last = lax.all_to_all(last, 'dp', 0, 0, tiled=True)]
    ppermute x34, waiting for transfers between devices: 58.2 us -> 54.3 us  [swap(): lax.ppermute(value, 'seq', [(item, item ^ mask) for item in range(8)])]
    pallas_call x5 -> x4, Pallas kernels: 29.3 us -> 26.4 us  [run(): pl.pallas_call(body, grid=(1,), in_specs=specs + [whole(*item.shape) for...]
  transfers between devices with their start and end apart: 53 -> 48, of which waited for: 20 -> 22; matrix products, arithmetic and copies ran while one was open for 21% -> 10% of each run, Pallas kernels for 16% -> 18%
where the time goes in v3:
time: 263 us; the launch traced here: 258 us
  waiting for transfers between devices  89 us (34%)
  starting transfers between devices  61.8 us (23%)
  Pallas kernels  56.6 us (22%)
  local copies, waits for them, and re-layouts  27.7 us (11%)
  other arithmetic  20.7 us (8%)
    ppermute x34, waiting for transfers between devices, swap(): lax.ppermute(value, 'seq', [(item, item ^ mask) for item in range(8)])  54.3 us
    ppermute x34, starting transfers between devices, swap(): lax.ppermute(value, 'seq', [(item, item ^ mask) for item in range(8)])  31.6 us
    pallas_call x4, Pallas kernels, run(): pl.pallas_call(body, grid=(1,), in_specs=specs + [whole(*item.shape) for...  26.4 us
    pallas_call x1, Pallas kernels, attend(): pl.pallas_call(attend_kernel, grid=(heads,), in_specs=[pl.BlockSpec(memor...  16.4 us
    pallas_call x1, Pallas kernels, attend_back(): pl.pallas_call(attend_back_kernel, grid=(heads,), in_specs=[pl.BlockSpec(...  13.9 us
    ppermute x3, waiting for transfers between devices, column_send(): parts.append(lax.ppermute(sent, 'dp', perm))  11.9 us
    ppermute x6, waiting for transfers between devices, column_parts(): parts.append(lax.ppermute(value, 'dp', perm))  10.8 us
    ppermute x6, starting transfers between devices, column_parts(): parts.append(lax.ppermute(value, 'dp', perm))  8.54 us
  transfers between devices with their start and end apart: 48, of which 22 were waited for; matrix products, arithmetic and copies ran while one was open for 10% of the time, Pallas kernels for 18%

profile of v3, /device:TPU:0, one launch (start us, length us, event | category | flops | bytes accessed | tf_op | source)
XLA Modules:
  0.0 257.9 jit_solution(17387886840955231217)
XLA Ops:
  0.7 0.9 stack.218
  4.8 0.9 pad_maximum_fusion.9
  5.7 5.2 %all-to-all-start = ((bf16[8,24,960]{2,1,0:T(8,128)(2,1)}), bf16[8,24,960]{2,1,0:T(8,128)(2,1)S(1)}, u32[]{:S(2)}, u32[]{:S(2)}) async-start(bf16[8,24,960]{2,1,0:T(8,128)(2,1)} %pad_maximum_fusion.9), calls=%async_computation | async-start | bytes 786432 | tf_op jit(solution)/shard_map/all_to_all | solution.py:791
  11.7 3.7 %collective-permute-start.2 = (bf16[32,768]{1,0:T(8,128)(2,1)S(1)}, bf16[32,768]{1,0:T(8,128)(2,1)S(1)}, u32[]{:S(2)}, u32[]{:S(2)}) collective-permute-start(bf16[32,768]{1,0:T(8,128)(2,1)S(1)} %fusion.10), channel_id=1, source_target_pairs={{0,24},{8,0},{16,8},{24,16},{1,25},{9,1},{17,9},{25,17},{2,26},{10... | collective-permute-start | bytes 147464 | tf_op jit(solution)/shard_map/ppermute | solution.py:294
  15.3 1.0 collective-permute-start
  16.4 1.0 collective-permute-done.2
  17.4 3.1 %collective-permute-done.1 = bf16[32,768]{1,0:T(8,128)(2,1)S(1)} collective-permute-done((bf16[32,768]{1,0:T(8,128)(2,1)S(1)}, bf16[32,768]{1,0:T(8,128)(2,1)S(1)}, u32[]{:S(2)}, u32[]{:S(2)}) %collective-permute-start.1) | collective-permute-done | bytes 49184 | tf_op jit(solution)/shard_map/ppermute | solution.py:294
  22.8 1.6 collective-permute-start.11
  24.5 3.0 %collective-permute-start.7 = (bf16[2,136,768]{2,1,0:T(8,128)(2,1)S(1)}, bf16[2,136,768]{2,1,0:T(8,128)(2,1)S(1)}, u32[]{:S(2)}, u32[]{:S(2)}) collective-permute-start(bf16[2,136,768]{2,1,0:T(8,128)(2,1)S(1)} %pad_maximum_fusion.7.own_ref), channel_id=1, source_target_pairs={{0,6},{1,7},{2,4},{3,5},{4,2},{5,3},{6,0},{7,1},{8,14},{9,15},{10,... | collective-permute-start | bytes 1253384 | tf_op jit(solution)/shard_map/ppermute | solution.py:253
  29.3 2.2 collective-permute-start.9
  31.6 6.0 %collective-permute-done.7.across_ref = bf16[2,136,768]{2,1,0:T(8,128)(2,1)S(1)} collective-permute-done((bf16[2,136,768]{2,1,0:T(8,128)(2,1)S(1)}, bf16[2,136,768]{2,1,0:T(8,128)(2,1)S(1)}, u32[]{:S(2)}, u32[]{:S(2)}) %collective-permute-start.7) | collective-permute-done | bytes 417824 | tf_op jit(solution)/shard_map/ppermute | solution.py:253
  37.6 1.7 collective-permute-start.5
  39.3 7.1 %collective-permute-done.6.y_ref = bf16[2,136,768]{2,1,0:T(8,128)(2,1)S(1)} collective-permute-done((bf16[2,136,768]{2,1,0:T(8,128)(2,1)S(1)}, bf16[2,136,768]{2,1,0:T(8,128)(2,1)S(1)}, u32[]{:S(2)}, u32[]{:S(2)}) %collective-permute-start.6) | collective-permute-done | bytes 417824 | tf_op jit(solution)/shard_map/ppermute | solution.py:253
  46.5 2.3 collective-permute-done.5.x_ref
  49.1 2.3 collective-permute-start.14
  55.4 5.9 %collective-permute-done.10 = bf16[96,2112]{1,0:T(8,128)(2,1)S(1)} collective-permute-done((bf16[96,2112]{1,0:T(8,128)(2,1)S(1)}, bf16[96,2112]{1,0:T(8,128)(2,1)S(1)}, u32[]{:S(2)}, u32[]{:S(2)}) %collective-permute-start.10) | collective-permute-done | bytes 405536 | tf_op jit(solution)/shard_map/ppermute | solution.py:294
  61.3 2.7 %collective-permute-done.13 = bf16[2,96,768]{2,1,0:T(8,128)(2,1)} collective-permute-done((bf16[2,96,768]{2,1,0:T(8,128)(2,1)S(1)}, bf16[2,96,768]{2,1,0:T(8,128)(2,1)}, u32[]{:S(2)}, u32[]{:S(2)}) %collective-permute-start.13) | collective-permute-done | bytes 294944 | tf_op jit(solution)/shard_map/ppermute | solution.py:253
  64.3 1.9 collective-permute-start.18
  66.9 1.0 collective-permute-start.16
  69.9 16.4 %shard_map.305 = (bf16[1024,768]{1,0:T(8,128)(2,1)}, bf16[1024,768]{1,0:T(8,128)(2,1)}, bf16[768,576]{1,0:T(8,128)(2,1)}, bf16[1024,192]{1,0:T(8,128)(2,1)}, bf1...) custom-call(s32[2]{0:T(128)} %pad_add_fusion.place_ref, ...), custom_call_target="tpu_custom_call" | custom-call | flops 1711276032 | bytes 6291456 | tf_op jit(solution)/shard_map/pallas_call | solution.py:513
  88.6 3.6 %all-to-all-start.1 = ((bf16[8,192,128]{2,1,0:T(8,128)(2,1)}), bf16[8,192,128]{2,1,0:T(8,128)(2,1)S(1)}, u32[]{:S(2)}, u32[]{:S(2)}) async-start(bf16[8,192,128]{2,1,0:T(8,128)(2,1)} %get-tuple-element.182), calls=%async_computation.1 | async-start | bytes 786432 | tf_op jit(solution)/shard_map/all_to_all | solution.py:843
  92.3 1.2 pad_maximum_fusion
  93.7 1.1 copy.157
  94.8 5.5 %all-to-all-done.1.attended_ref = bf16[8,192,128]{2,1,0:T(8,128)(2,1)S(1)} async-done(((bf16[8,192,128]{2,1,0:T(8,128)(2,1)}), bf16[8,192,128]{2,1,0:T(8,128)(2,1)S(1)}, u32[]{:S(2)}, u32[]{:S(2)}) %all-to-all-start.1) | async-done | bytes 393248 | tf_op jit(solution)/shard_map/all_to_all | solution.py:843
  101.1 3.2 %shard_map.306 = (f32[256,768]{1,0:T(8,128)}, bf16[256,768]{1,0:T(8,128)(2,1)}) custom-call(bf16[8,192,128]{2,1,0:T(8,128)(2,1)} %copy-done.2, bf16[768,768]{1,0:T(8,128)(2,1)} %bitcast.167, bf16[256,768]{1,0:T(8,128)(2,1)} %bitcast.166, f32[8,768]{1,0:T(8,128)} %stack.256.vectors_ref), custom_call_target="tpu_custom_call" | custom-call | flops 301989888 | tf_op jit(solution)/shard_map/pallas_call | solution.py:618
  104.9 1.5 collective-permute-start.20
  106.3 1.5 collective-permute-start.19
  107.8 2.0 maximum_select_fusion
  109.9 1.1 slice.309
  111.2 1.1 copy.174
  112.3 5.2 %collective-permute-done.21.refs_3_ = bf16[256,768]{1,0:T(8,128)(2,1)S(1)} collective-permute-done((bf16[256,768]{1,0:T(8,128)(2,1)}, bf16[256,768]{1,0:T(8,128)(2,1)S(1)}, u32[]{:S(2)}, u32[]{:S(2)}) %collective-permute-start.21) | collective-permute-done | bytes 393248 | tf_op jit(solution)/shard_map/ppermute | solution.py:253
  117.5 5.6 %collective-permute-done.20.refs_2_ = bf16[256,768]{1,0:T(8,128)(2,1)S(1)} collective-permute-done((bf16[256,768]{1,0:T(8,128)(2,1)}, bf16[256,768]{1,0:T(8,128)(2,1)S(1)}, u32[]{:S(2)}, u32[]{:S(2)}) %collective-permute-start.20) | collective-permute-done | bytes 393248 | tf_op jit(solution)/shard_map/ppermute | solution.py:253
  124.0 9.2 %shard_map.307 = (bf16[1024,768]{1,0:T(8,128)(2,1)}, bf16[1024,768]{1,0:T(8,128)(2,1)}, bf16[256,768]{1,0:T(8,128)(2,1)}, bf16[256,768]{1,0:T(8,128)(2,1)}, bf16...) custom-call(bf16[256,768]{1,0:T(8,128)(2,1)} %get-tuple-element.191.refs_0_, ...), custom_call_target="tpu_custom_call" | custom-call | flops 7247757312 | tf_op jit(solution)/shard_map/pallas_call | solution.py:618
  133.1 1.5 collective-permute-start.23
  134.7 1.4 collective-permute-start.24
  136.6 8.5 %shard_map.308 = (bf16[256,768]{1,0:T(8,128)(2,1)}, bf16[256,768]{1,0:T(8,128)(2,1)}, bf16[256,768]{1,0:T(8,128)(2,1)}, bf16[256,768]{1,0:T(8,128)(2,1)}, bf16[4...) custom-call(s32[1]{0:T(128)} %bitcast.45.core_ref, bf16[256,768]{1,0:T(8,128)(2,1)} %get-tuple-element.191.refs_0_, ...), custom_call_target="tpu_custom_call" | custom-call | flops 7247757312 | tf_op jit(solution)/shard_map/pallas_call | solution.py:618
  145.3 7.0 %collective-permute-done.24.y_ref = bf16[256,768]{1,0:T(8,128)(2,1)S(1)} collective-permute-done((bf16[256,768]{1,0:T(8,128)(2,1)}, bf16[256,768]{1,0:T(8,128)(2,1)S(1)}, u32[]{:S(2)}, u32[]{:S(2)}) %collective-permute-start.24) | collective-permute-done | bytes 393248 | tf_op jit(solution)/shard_map/ppermute | solution.py:253
  152.3 1.2 collective-permute-done.25.across_ref
  154.2 5.5 %shard_map.309 = (f32[256,768]{1,0:T(8,128)}, bf16[8,192,128]{2,1,0:T(8,128)(2,1)}, f32[8,768]{1,0:T(8,128)}, bf16[4,4,24,768]{3,2,1,0:T(8,128)(2,1)}, bf16[4,4,24,768]{3,2,1,0:T(8,128)(2,1)}) custom-call(s32[1]{0:T(128)} %bitcast.place_ref, bf16[256,768]{1,0:T(8,128)(2,1)} %get-tuple-element.205.own_ref, bf16[256,768]{1,0:T(8,128)(2,1)} %copy-done.10, ...), custom_call_target="tpu_custom_call" | custom-call | flops 603979776 | tf_op jit(solution)/shard_map/pallas_call | solution.py:618
  162.0 1.2 add_convert_fusion.1
  163.2 1.5 add_convert_fusion
  164.8 3.5 %all-to-all-start.2 = ((bf16[8,192,128]{2,1,0:T(8,128)(2,1)}), bf16[8,192,128]{2,1,0:T(8,128)(2,1)S(1)}, u32[]{:S(2)}, u32[]{:S(2)}) async-start(bf16[8,192,128]{2,1,0:T(8,128)(2,1)} %get-tuple-element.220), calls=%async_computation.2 | async-start | bytes 786432 | tf_op jit(solution)/shard_map/all_to_all | solution.py:907
  168.2 0.9 dynamic-slice_bitcast_fusion
  170.0 2.9 %collective-permute-start.31 = (bf16[4,24,768]{2,1,0:T(8,128)(2,1)S(1)}, bf16[4,24,768]{2,1,0:T(8,128)(2,1)S(1)}, u32[]{:S(2)}, u32[]{:S(2)}) collective-permute-start(bf16[4,24,768]{2,1,0:T(8,128)(2,1)S(1)} %get-tuple-element.311), channel_id=1, source_target_pairs={{0,6},{1,7},{2,4},{3,5},{4,2},{5,3},{6,0},{7,1},{8,14},{9,15},{10,... | collective-permute-start | bytes 442376 | tf_op jit(solution)/shard_map/ppermute | solution.py:253
  173.9 6.3 %collective-permute-done.27 = bf16[192,768]{1,0:T(8,128)(2,1)S(1)} collective-permute-done((bf16[192,768]{1,0:T(8,128)(2,1)S(1)}, bf16[192,768]{1,0:T(8,128)(2,1)S(1)}, u32[]{:S(2)}, u32[]{:S(2)}) %collective-permute-start.27) | collective-permute-done | bytes 294944 | tf_op jit(solution)/shard_map/ppermute | solution.py:309
  180.2 1.7 collective-permute-start.32
  182.0 1.5 collective-permute-start.33
  183.8 1.3 concatenate.51.terms_in
  185.6 13.9 %shard_map.310 = (bf16[4,96,576]{2,1,0:T(8,128)(2,1)}, bf16[4,96,576]{2,1,0:T(8,128)(2,1)}, bf16[256,768]{1,0:T(8,128)(2,1)}, bf16[256,768]{1,0:T(8,128)(2,1)}, ...) custom-call(s32[2]{0:T(128)} %pad_add_fusion.1.chip_ref, ...), custom_call_target="tpu_custom_call" | custom-call | flops 3825205248 | bytes 6291456 | tf_op jit(solution)/shard_map/pallas_call | solution.py:557
  199.5 5.5 %collective-permute-done.35 = bf16[192,768]{1,0:T(8,128)(2,1)S(1)} collective-permute-done((bf16[192,768]{1,0:T(8,128)(2,1)}, bf16[192,768]{1,0:T(8,128)(2,1)S(1)}, u32[]{:S(2)}, u32[]{:S(2)}) %collective-permute-start.35) | collective-permute-done | bytes 294944 | tf_op jit(solution)/shard_map/ppermute | solution.py:309
  205.7 1.1 add_convert_fusion.5
  208.0 0.9 pad_maximum_fusion.5
  208.9 4.3 %all-to-all-start.3 = ((bf16[4,144,576]{2,1,0:T(8,128)(2,1)}), bf16[4,144,576]{2,1,0:T(8,128)(2,1)S(1)}, u32[]{:S(2)}, u32[]{:S(2)}) async-start(bf16[4,144,576]{2,1,0:T(8,128)(2,1)} %pad_maximum_fusion.5), calls=%async_computation.3 | async-start | bytes 1474560 | tf_op jit(solution)/shard_map/all_to_all | solution.py:935
  213.6 1.2 collective-permute-start.38
  214.8 1.5 collective-permute-start.39
  217.3 2.0 add_convert_fusion.4
  219.3 6.6 %collective-permute-done.38 = bf16[256,768]{1,0:T(8,128)(2,1)} collective-permute-done((bf16[256,768]{1,0:T(8,128)(2,1)}, bf16[256,768]{1,0:T(8,128)(2,1)}, u32[]{:S(2)}, u32[]{:S(2)}) %collective-permute-start.38) | collective-permute-done | bytes 393248 | tf_op jit(solution)/shard_map/ppermute | solution.py:253
  226.0 8.2 %collective-permute-done.39 = bf16[256,768]{1,0:T(8,128)(2,1)} collective-permute-done((bf16[256,768]{1,0:T(8,128)(2,1)}, bf16[256,768]{1,0:T(8,128)(2,1)}, u32[]{:S(2)}, u32[]{:S(2)}) %collective-permute-start.39) | collective-permute-done | bytes 393248 | tf_op jit(solution)/shard_map/ppermute | solution.py:253
  234.4 1.5 add_convert_fusion.3
  238.6 1.0 pad_maximum_fusion.10
  239.5 3.7 %all-to-all-start.4 = ((bf16[8,24,984]{2,1,0:T(8,128)(2,1)}), bf16[8,24,984]{2,1,0:T(8,128)(2,1)S(1)}, u32[]{:S(2)}, u32[]{:S(2)}) async-start(bf16[8,24,984]{2,1,0:T(8,128)(2,1)} %pad_maximum_fusion.10), calls=%async_computation.4 | async-start | bytes 786432 | tf_op jit(solution)/shard_map/all_to_all | solution.py:952
  243.7 1.2 fusion.8
  244.9 6.6 %all-to-all-done.4 = bf16[8,24,984]{2,1,0:T(8,128)(2,1)S(1)} async-done(((bf16[8,24,984]{2,1,0:T(8,128)(2,1)}), bf16[8,24,984]{2,1,0:T(8,128)(2,1)S(1)}, u32[]{:S(2)}, u32[]{:S(2)}) %all-to-all-start.4) | async-done | bytes 377888 | tf_op jit(solution)/shard_map/all_to_all | solution.py:952
  256.1 0.9 reshape.286
  (293 shorter events, 38.0 us)
Async XLA Ops:
  4.6 6.8 %copy-start.48 = (s32[2,128]{1,0:T(2,128)S(1)}, s32[2,128]{1,0:T(2,128)}, u32[]{:S(2)}) copy-start(s32[2,128]{1,0:T(2,128)} %param.20) | copy-start | bytes 3076
  4.7 6.8 %copy-start.32 = (bf16[24]{0:T(256)(128)(2,1)S(1)}, bf16[24]{0:T(256)(128)(2,1)}, u32[]{:S(2)}) copy-start(bf16[24]{0:T(256)(128)(2,1)} %param.27) | copy-start | bytes 148
  4.7 6.8 %copy-start.33 = (bf16[24]{0:T(256)(128)(2,1)S(1)}, bf16[24]{0:T(256)(128)(2,1)}, u32[]{:S(2)}) copy-start(bf16[24]{0:T(256)(128)(2,1)} %param.28) | copy-start | bytes 148
  4.8 6.9 %copy-start.30 = (bf16[24,768]{1,0:T(8,128)(2,1)S(1)}, bf16[24,768]{1,0:T(8,128)(2,1)}, u32[]{:S(2)}) copy-start(bf16[24,768]{1,0:T(8,128)(2,1)} %param.24) | copy-start | bytes 110596
  5.7 15.5 %all-to-all-start = ((bf16[8,24,960]{2,1,0:T(8,128)(2,1)}), bf16[8,24,960]{2,1,0:T(8,128)(2,1)S(1)}, u32[]{:S(2)}, u32[]{:S(2)}) async-start(bf16[8,24,960]{2,1,0:T(8,128)(2,1)} %pad_maximum_fusion.9), calls=%async_computation | async-start | bytes 786432 | tf_op jit(solution)/shard_map/all_to_all | solution.py:791
  10.9 5.5 %collective-permute-start.3 = (bf16[128,768]{1,0:T(8,128)(2,1)S(1)}, bf16[128,768]{1,0:T(8,128)(2,1)S(1)}, u32[]{:S(2)}, u32[]{:S(2)}) collective-permute-start(bf16[128,768]{1,0:T(8,128)(2,1)S(1)} %get-tuple-element.323), channel_id=1, source_target_pairs={{0,1},{1,0},{2,3},{3,2},{4,5},{5,4},{6,7},{7,6},{8,9},{9,8},{10,11... | collective-permute-start | bytes 589832 | tf_op jit(solution)/shard_map/ppermute | solution.py:253
  11.7 5.8 %collective-permute-start.2 = (bf16[32,768]{1,0:T(8,128)(2,1)S(1)}, bf16[32,768]{1,0:T(8,128)(2,1)S(1)}, u32[]{:S(2)}, u32[]{:S(2)}) collective-permute-start(bf16[32,768]{1,0:T(8,128)(2,1)S(1)} %fusion.10), channel_id=1, source_target_pairs={{0,24},{8,0},{16,8},{24,16},{1,25},{9,1},{17,9},{25,17},{2,26},{10... | collective-permute-start | bytes 147464 | tf_op jit(solution)/shard_map/ppermute | solution.py:294
  15.3 5.2 %collective-permute-start.1 = (bf16[32,768]{1,0:T(8,128)(2,1)S(1)}, bf16[32,768]{1,0:T(8,128)(2,1)S(1)}, u32[]{:S(2)}, u32[]{:S(2)}) collective-permute-start(bf16[32,768]{1,0:T(8,128)(2,1)S(1)} %fusion.10), channel_id=1, source_target_pairs={{0,16},{8,24},{16,0},{24,8},{1,17},{9,25},{17,1},{25,9},{2,18},{10... | collective-permute-start | bytes 147464 | tf_op jit(solution)/shard_map/ppermute | solution.py:294
  15.3 5.9 %collective-permute-start = (bf16[32,768]{1,0:T(8,128)(2,1)S(1)}, bf16[32,768]{1,0:T(8,128)(2,1)S(1)}, u32[]{:S(2)}, u32[]{:S(2)}) collective-permute-start(bf16[32,768]{1,0:T(8,128)(2,1)S(1)} %fusion.10), channel_id=1, source_target_pairs={{0,8},{8,16},{16,24},{24,0},{1,9},{9,17},{17,25},{25,1},{2,10},{10... | collective-permute-start | bytes 147464 | tf_op jit(solution)/shard_map/ppermute | solution.py:294
  22.7 1.8 collective-permute-start.4
  22.8 30.7 %collective-permute-start.11 = (bf16[96,2112]{1,0:T(8,128)(2,1)S(1)}, bf16[96,2112]{1,0:T(8,128)(2,1)S(1)}, u32[]{:S(2)}, u32[]{:S(2)}) collective-permute-start(bf16[96,2112]{1,0:T(8,128)(2,1)S(1)} %pad_maximum_fusion.8), channel_id=1, source_target_pairs={{0,24},{8,0},{16,8},{24,16},{1,25},{9,1},{17,9},{25,17},{2,26},{10... | collective-permute-start | bytes 1216520 | tf_op jit(solution)/shard_map/ppermute | solution.py:294
  24.4 36.9 %collective-permute-start.10 = (bf16[96,2112]{1,0:T(8,128)(2,1)S(1)}, bf16[96,2112]{1,0:T(8,128)(2,1)S(1)}, u32[]{:S(2)}, u32[]{:S(2)}) collective-permute-start(bf16[96,2112]{1,0:T(8,128)(2,1)S(1)} %pad_maximum_fusion.8), channel_id=1, source_target_pairs={{0,16},{8,24},{16,0},{24,8},{1,17},{9,25},{17,1},{25,9},{2,18},{10... | collective-permute-start | bytes 1216520 | tf_op jit(solution)/shard_map/ppermute | solution.py:294
  24.5 28.5 %copy-start.8 = (bf16[2,136,768]{2,1,0:T(8,128)(2,1)}, bf16[2,136,768]{2,1,0:T(8,128)(2,1)S(1)}, u32[]{:S(2)}) copy-start(bf16[2,136,768]{2,1,0:T(8,128)(2,1)S(1)} %pad_maximum_fusion.7.own_ref) | copy-start | bytes 1253380
  24.5 13.1 %collective-permute-start.7 = (bf16[2,136,768]{2,1,0:T(8,128)(2,1)S(1)}, bf16[2,136,768]{2,1,0:T(8,128)(2,1)S(1)}, u32[]{:S(2)}, u32[]{:S(2)}) collective-permute-start(bf16[2,136,768]{2,1,0:T(8,128)(2,1)S(1)} %pad_maximum_fusion.7.own_ref), channel_id=1, source_target_pairs={{0,6},{1,7},{2,4},{3,5},{4,2},{5,3},{6,0},{7,1},{8,14},{9,15},{10,... | collective-permute-start | bytes 1253384 | tf_op jit(solution)/shard_map/ppermute | solution.py:253
  27.9 1.4 collective-permute-start.8
  27.9 18.5 %collective-permute-start.6 = (bf16[2,136,768]{2,1,0:T(8,128)(2,1)S(1)}, bf16[2,136,768]{2,1,0:T(8,128)(2,1)S(1)}, u32[]{:S(2)}, u32[]{:S(2)}) collective-permute-start(bf16[2,136,768]{2,1,0:T(8,128)(2,1)S(1)} %pad_maximum_fusion.7.own_ref), channel_id=1, source_target_pairs={{0,4},{1,5},{2,6},{3,7},{4,0},{5,1},{6,2},{7,3},{8,12},{9,13},{10,... | collective-permute-start | bytes 1253384 | tf_op jit(solution)/shard_map/ppermute | solution.py:253
  29.3 32.0 %collective-permute-start.9 = (bf16[96,2112]{1,0:T(8,128)(2,1)S(1)}, bf16[96,2112]{1,0:T(8,128)(2,1)S(1)}, u32[]{:S(2)}, u32[]{:S(2)}) collective-permute-start(bf16[96,2112]{1,0:T(8,128)(2,1)S(1)} %pad_maximum_fusion.8), channel_id=1, source_target_pairs={{0,8},{8,16},{16,24},{24,0},{1,9},{9,17},{17,25},{25,1},{2,10},{10... | collective-permute-start | bytes 1216520 | tf_op jit(solution)/shard_map/ppermute | solution.py:294
  37.6 13.8 %copy-start.41 = (bf16[2,136,768]{2,1,0:T(8,128)(2,1)}, bf16[2,136,768]{2,1,0:T(8,128)(2,1)S(1)}, u32[]{:S(2)}) copy-start(bf16[2,136,768]{2,1,0:T(8,128)(2,1)S(1)} %collective-permute-done.7.across_ref) | copy-start | bytes 1253380
  37.6 11.2 %collective-permute-start.5 = (bf16[2,136,768]{2,1,0:T(8,128)(2,1)S(1)}, bf16[2,136,768]{2,1,0:T(8,128)(2,1)S(1)}, u32[]{:S(2)}, u32[]{:S(2)}) collective-permute-start(bf16[2,136,768]{2,1,0:T(8,128)(2,1)S(1)} %pad_maximum_fusion.7.own_ref), channel_id=1, source_target_pairs={{0,2},{1,3},{2,0},{3,1},{4,6},{5,7},{6,4},{7,5},{8,10},{9,11},{10,... | collective-permute-start | bytes 1253384 | tf_op jit(solution)/shard_map/ppermute | solution.py:253
  49.1 12.3 %collective-permute-start.14 = (bf16[2,96,768]{2,1,0:T(8,128)(2,1)S(1)}, bf16[2,96,768]{2,1,0:T(8,128)(2,1)S(1)}, u32[]{:S(2)}, u32[]{:S(2)}) collective-permute-start(bf16[2,96,768]{2,1,0:T(8,128)(2,1)S(1)} %maximum_select_fusion.3), channel_id=1, source_target_pairs={{0,6},{1,7},{2,4},{3,5},{4,2},{5,3},{6,0},{7,1},{8,14},{9,15},{10,... | collective-permute-start | bytes 884744 | tf_op jit(solution)/shard_map/ppermute | solution.py:253
  51.4 12.7 %collective-permute-start.13 = (bf16[2,96,768]{2,1,0:T(8,128)(2,1)S(1)}, bf16[2,96,768]{2,1,0:T(8,128)(2,1)}, u32[]{:S(2)}, u32[]{:S(2)}) collective-permute-start(bf16[2,96,768]{2,1,0:T(8,128)(2,1)S(1)} %maximum_select_fusion.3), channel_id=1, source_target_pairs={{0,4},{1,5},{2,6},{3,7},{4,0},{5,1},{6,2},{7,3},{8,12},{9,13},{10,... | collective-permute-start | bytes 884744 | tf_op jit(solution)/shard_map/ppermute | solution.py:253
  52.1 12.2 %copy-start.9 = (bf16[2,128,768]{2,1,0:T(8,128)(2,1)S(1)}, bf16[2,128,768]{2,1,0:T(8,128)(2,1)}, u32[]{:S(2)}) copy-start(bf16[2,128,768]{2,1,0:T(8,128)(2,1)} %param.19) | copy-start | bytes 1179652
  53.5 10.6 %collective-permute-start.12 = (bf16[2,96,768]{2,1,0:T(8,128)(2,1)S(1)}, bf16[2,96,768]{2,1,0:T(8,128)(2,1)S(1)}, u32[]{:S(2)}, u32[]{:S(2)}) collective-permute-start(bf16[2,96,768]{2,1,0:T(8,128)(2,1)S(1)} %maximum_select_fusion.3), channel_id=1, source_target_pairs={{0,2},{1,3},{2,0},{3,1},{4,6},{5,7},{6,4},{7,5},{8,10},{9,11},{10,... | collective-permute-start | bytes 884744 | tf_op jit(solution)/shard_map/ppermute | solution.py:253
  64.0 22.2 %copy-start.18 = (bf16[2,96,768]{2,1,0:T(8,128)(2,1)}, bf16[2,96,768]{2,1,0:T(8,128)(2,1)S(1)}, u32[]{:S(2)}) copy-start(bf16[2,96,768]{2,1,0:T(8,128)(2,1)S(1)} %collective-permute-done.12) | copy-start | bytes 884740
  64.2 4.8 %collective-permute-start.15 = (bf16[4,96,576]{2,1,0:T(8,128)(2,1)S(1)}, bf16[4,96,576]{2,1,0:T(8,128)(2,1)S(1)}, u32[]{:S(2)}, u32[]{:S(2)}) collective-permute-start(bf16[4,96,576]{2,1,0:T(8,128)(2,1)S(1)} %pad_maximum_fusion.6.w_near), channel_id=1, source_target_pairs={{0,1},{1,0},{2,3},{3,2},{4,5},{5,4},{6,7},{7,6},{8,9},{9,8},{10,11... | collective-permute-start | bytes 1327112 | tf_op jit(solution)/shard_map/ppermute | solution.py:253
  64.3 21.9 %collective-permute-start.18 = (bf16[256,768]{1,0:T(8,128)(2,1)S(1)}, bf16[256,768]{1,0:T(8,128)(2,1)}, u32[]{:S(2)}, u32[]{:S(2)}) collective-permute-start(bf16[256,768]{1,0:T(8,128)(2,1)S(1)} %bitcast.194), channel_id=1, source_target_pairs={{0,6},{1,7},{2,4},{3,5},{4,2},{5,3},{6,0},{7,1},{8,14},{9,15},{10,... | collective-permute-start | bytes 1179656 | tf_op jit(solution)/shard_map/ppermute | solution.py:253
  66.2 20.1 %collective-permute-start.17 = (bf16[256,768]{1,0:T(8,128)(2,1)S(1)}, bf16[256,768]{1,0:T(8,128)(2,1)}, u32[]{:S(2)}, u32[]{:S(2)}) collective-permute-start(bf16[256,768]{1,0:T(8,128)(2,1)S(1)} %bitcast.195), channel_id=1, source_target_pairs={{0,4},{1,5},{2,6},{3,7},{4,0},{5,1},{6,2},{7,3},{8,12},{9,13},{10,... | collective-permute-start | bytes 1179656 | tf_op jit(solution)/shard_map/ppermute | solution.py:253
  66.9 19.3 %collective-permute-start.16 = (bf16[256,768]{1,0:T(8,128)(2,1)S(1)}, bf16[256,768]{1,0:T(8,128)(2,1)}, u32[]{:S(2)}, u32[]{:S(2)}) collective-permute-start(bf16[256,768]{1,0:T(8,128)(2,1)S(1)} %bitcast.196), channel_id=1, source_target_pairs={{0,2},{1,3},{2,0},{3,1},{4,6},{5,7},{6,4},{7,5},{8,10},{9,11},{10,... | collective-permute-start | bytes 1179656 | tf_op jit(solution)/shard_map/ppermute | solution.py:253
  86.9 20.9 %collective-permute-start.22 = (bf16[4,96,1536]{2,1,0:T(8,128)(2,1)S(1)}, bf16[4,96,1536]{2,1,0:T(8,128)(2,1)}, u32[]{:S(2)}, u32[]{:S(2)}) collective-permute-start(bf16[4,96,1536]{2,1,0:T(8,128)(2,1)S(1)} %get-tuple-element.302), channel_id=1, source_target_pairs={{0,1},{1,0},{2,3},{3,2},{4,5},{5,4},{6,7},{7,6},{8,9},{9,8},{10,11... | collective-permute-start | bytes 3538952 | tf_op jit(solution)/shard_map/ppermute | solution.py:253
  88.6 11.7 %all-to-all-start.1 = ((bf16[8,192,128]{2,1,0:T(8,128)(2,1)}), bf16[8,192,128]{2,1,0:T(8,128)(2,1)S(1)}, u32[]{:S(2)}, u32[]{:S(2)}) async-start(bf16[8,192,128]{2,1,0:T(8,128)(2,1)} %get-tuple-element.182), calls=%async_computation.1 | async-start | bytes 786432 | tf_op jit(solution)/shard_map/all_to_all | solution.py:843
  104.3 13.2 %collective-permute-start.21 = (bf16[256,768]{1,0:T(8,128)(2,1)}, bf16[256,768]{1,0:T(8,128)(2,1)S(1)}, u32[]{:S(2)}, u32[]{:S(2)}) collective-permute-start(bf16[256,768]{1,0:T(8,128)(2,1)} %get-tuple-element.191.refs_0_), channel_id=1, source_target_pairs={{0,6},{1,7},{2,4},{3,5},{4,2},{5,3},{6,0},{7,1},{8,14},{9,15},{10,... | collective-permute-start | bytes 1179656 | tf_op jit(solution)/shard_map/ppermute | solution.py:253
  104.9 18.2 %collective-permute-start.20 = (bf16[256,768]{1,0:T(8,128)(2,1)}, bf16[256,768]{1,0:T(8,128)(2,1)S(1)}, u32[]{:S(2)}, u32[]{:S(2)}) collective-permute-start(bf16[256,768]{1,0:T(8,128)(2,1)} %get-tuple-element.191.refs_0_), channel_id=1, source_target_pairs={{0,4},{1,5},{2,6},{3,7},{4,0},{5,1},{6,2},{7,3},{8,12},{9,13},{10,... | collective-permute-start | bytes 1179656 | tf_op jit(solution)/shard_map/ppermute | solution.py:253
  106.3 16.7 %collective-permute-start.19 = (bf16[256,768]{1,0:T(8,128)(2,1)}, bf16[256,768]{1,0:T(8,128)(2,1)S(1)}, u32[]{:S(2)}, u32[]{:S(2)}) collective-permute-start(bf16[256,768]{1,0:T(8,128)(2,1)} %get-tuple-element.191.refs_0_), channel_id=1, source_target_pairs={{0,2},{1,3},{2,0},{3,1},{4,6},{5,7},{6,4},{7,5},{8,10},{9,11},{10,... | collective-permute-start | bytes 1179656 | tf_op jit(solution)/shard_map/ppermute | solution.py:253
  133.1 12.2 %collective-permute-start.23 = (bf16[256,768]{1,0:T(8,128)(2,1)}, bf16[256,768]{1,0:T(8,128)(2,1)S(1)}, u32[]{:S(2)}, u32[]{:S(2)}) collective-permute-start(bf16[256,768]{1,0:T(8,128)(2,1)} %get-tuple-element.202), channel_id=1, source_target_pairs={{0,2},{1,3},{2,0},{3,1},{4,6},{5,7},{6,4},{7,5},{8,10},{9,11},{10,... | collective-permute-start | bytes 1179656 | tf_op jit(solution)/shard_map/ppermute | solution.py:253
  134.7 17.6 %collective-permute-start.24 = (bf16[256,768]{1,0:T(8,128)(2,1)}, bf16[256,768]{1,0:T(8,128)(2,1)S(1)}, u32[]{:S(2)}, u32[]{:S(2)}) collective-permute-start(bf16[256,768]{1,0:T(8,128)(2,1)} %get-tuple-element.203), channel_id=1, source_target_pairs={{0,4},{1,5},{2,6},{3,7},{4,0},{5,1},{6,2},{7,3},{8,12},{9,13},{10,... | collective-permute-start | bytes 1179656 | tf_op jit(solution)/shard_map/ppermute | solution.py:253
  136.0 17.5 %collective-permute-start.25 = (bf16[256,768]{1,0:T(8,128)(2,1)}, bf16[256,768]{1,0:T(8,128)(2,1)S(1)}, u32[]{:S(2)}, u32[]{:S(2)}) collective-permute-start(bf16[256,768]{1,0:T(8,128)(2,1)} %get-tuple-element.204), channel_id=1, source_target_pairs={{0,6},{1,7},{2,4},{3,5},{4,2},{5,3},{6,0},{7,1},{8,14},{9,15},{10,... | collective-permute-start | bytes 1179656 | tf_op jit(solution)/shard_map/ppermute | solution.py:253
  145.3 8.2 %copy-start.10 = (bf16[256,768]{1,0:T(8,128)(2,1)}, bf16[256,768]{1,0:T(8,128)(2,1)S(1)}, u32[]{:S(2)}) copy-start(bf16[256,768]{1,0:T(8,128)(2,1)S(1)} %collective-permute-done.23.x_ref) | copy-start | bytes 1179652
  153.5 9.7 %collective-permute-start.26 = (bf16[4,192,768]{2,1,0:T(8,128)(2,1)}, bf16[4,192,768]{2,1,0:T(8,128)(2,1)}, u32[]{:S(2)}, u32[]{:S(2)}) collective-permute-start(bf16[4,192,768]{2,1,0:T(8,128)(2,1)} %get-tuple-element.219), channel_id=1, source_target_pairs={{0,1},{1,0},{2,3},{3,2},{4,5},{5,4},{6,7},{7,6},{8,9},{9,8},{10,11... | collective-permute-start | bytes 3538952 | tf_op jit(solution)/shard_map/ppermute | solution.py:253
  159.8 2.2 collective-permute-start.28
  164.8 15.5 %all-to-all-start.2 = ((bf16[8,192,128]{2,1,0:T(8,128)(2,1)}), bf16[8,192,128]{2,1,0:T(8,128)(2,1)S(1)}, u32[]{:S(2)}, u32[]{:S(2)}) async-start(bf16[8,192,128]{2,1,0:T(8,128)(2,1)} %get-tuple-element.220), calls=%async_computation.2 | async-start | bytes 786432 | tf_op jit(solution)/shard_map/all_to_all | solution.py:907
  169.1 14.7 %copy-start.31 = (f32[8,768]{1,0:T(8,128)S(1)}, f32[8,768]{1,0:T(8,128)}, u32[]{:S(2)}) copy-start(f32[8,768]{1,0:T(8,128)} %get-tuple-element.231) | copy-start | bytes 73732
  169.1 11.1 %collective-permute-start.27 = (bf16[192,768]{1,0:T(8,128)(2,1)S(1)}, bf16[192,768]{1,0:T(8,128)(2,1)S(1)}, u32[]{:S(2)}, u32[]{:S(2)}) collective-permute-start(bf16[192,768]{1,0:T(8,128)(2,1)S(1)} %get-tuple-element.300), channel_id=1, source_target_pairs={{0,8},{8,16},{16,24},{24,0},{1,9},{9,17},{17,25},{25,1},{2,10},{10... | collective-permute-start | bytes 884744 | tf_op jit(solution)/shard_map/ppermute | solution.py:309
  170.0 13.4 %collective-permute-start.31 = (bf16[4,24,768]{2,1,0:T(8,128)(2,1)S(1)}, bf16[4,24,768]{2,1,0:T(8,128)(2,1)S(1)}, u32[]{:S(2)}, u32[]{:S(2)}) collective-permute-start(bf16[4,24,768]{2,1,0:T(8,128)(2,1)S(1)} %get-tuple-element.311), channel_id=1, source_target_pairs={{0,6},{1,7},{2,4},{3,5},{4,2},{5,3},{6,0},{7,1},{8,14},{9,15},{10,... | collective-permute-start | bytes 442376 | tf_op jit(solution)/shard_map/ppermute | solution.py:253
  173.2 11.9 %collective-permute-start.30 = (bf16[4,24,768]{2,1,0:T(8,128)(2,1)S(1)}, bf16[4,24,768]{2,1,0:T(8,128)(2,1)}, u32[]{:S(2)}, u32[]{:S(2)}) collective-permute-start(bf16[4,24,768]{2,1,0:T(8,128)(2,1)S(1)} %get-tuple-element.312), channel_id=1, source_target_pairs={{0,4},{1,5},{2,6},{3,7},{4,0},{5,1},{6,2},{7,3},{8,12},{9,13},{10,... | collective-permute-start | bytes 442376 | tf_op jit(solution)/shard_map/ppermute | solution.py:253
  173.8 11.3 %collective-permute-start.29 = (bf16[4,24,768]{2,1,0:T(8,128)(2,1)S(1)}, bf16[4,24,768]{2,1,0:T(8,128)(2,1)}, u32[]{:S(2)}, u32[]{:S(2)}) collective-permute-start(bf16[4,24,768]{2,1,0:T(8,128)(2,1)S(1)} %get-tuple-element.313), channel_id=1, source_target_pairs={{0,2},{1,3},{2,0},{3,1},{4,6},{5,7},{6,4},{7,5},{8,10},{9,11},{10,... | collective-permute-start | bytes 442376 | tf_op jit(solution)/shard_map/ppermute | solution.py:253
  180.2 19.2 %copy-start.19 = (bf16[192,768]{1,0:T(8,128)(2,1)}, bf16[192,768]{1,0:T(8,128)(2,1)S(1)}, u32[]{:S(2)}) copy-start(bf16[192,768]{1,0:T(8,128)(2,1)S(1)} %collective-permute-done.27) | copy-start | bytes 884740
  180.2 24.8 %collective-permute-start.32 = (bf16[256,768]{1,0:T(8,128)(2,1)}, bf16[256,768]{1,0:T(8,128)(2,1)S(1)}, u32[]{:S(2)}, u32[]{:S(2)}) collective-permute-start(bf16[256,768]{1,0:T(8,128)(2,1)} %get-tuple-element.240), channel_id=1, source_target_pairs={{0,2},{1,3},{2,0},{3,1},{4,6},{5,7},{6,4},{7,5},{8,10},{9,11},{10,... | collective-permute-start | bytes 1179656 | tf_op jit(solution)/shard_map/ppermute | solution.py:253
  182.0 23.1 %collective-permute-start.33 = (bf16[256,768]{1,0:T(8,128)(2,1)}, bf16[256,768]{1,0:T(8,128)(2,1)S(1)}, u32[]{:S(2)}, u32[]{:S(2)}) collective-permute-start(bf16[256,768]{1,0:T(8,128)(2,1)} %get-tuple-element.241), channel_id=1, source_target_pairs={{0,4},{1,5},{2,6},{3,7},{4,0},{5,1},{6,2},{7,3},{8,12},{9,13},{10,... | collective-permute-start | bytes 1179656 | tf_op jit(solution)/shard_map/ppermute | solution.py:253
  183.5 21.6 %collective-permute-start.34 = (bf16[256,768]{1,0:T(8,128)(2,1)}, bf16[256,768]{1,0:T(8,128)(2,1)}, u32[]{:S(2)}, u32[]{:S(2)}) collective-permute-start(bf16[256,768]{1,0:T(8,128)(2,1)} %get-tuple-element.242), channel_id=1, source_target_pairs={{0,6},{1,7},{2,4},{3,5},{4,2},{5,3},{6,0},{7,1},{8,14},{9,15},{10,... | collective-permute-start | bytes 1179656 | tf_op jit(solution)/shard_map/ppermute | solution.py:253
  185.1 14.4 %collective-permute-start.36 = (bf16[192,768]{1,0:T(8,128)(2,1)}, bf16[192,768]{1,0:T(8,128)(2,1)S(1)}, u32[]{:S(2)}, u32[]{:S(2)}) collective-permute-start(bf16[192,768]{1,0:T(8,128)(2,1)} %get-tuple-element.297), channel_id=1, source_target_pairs={{0,24},{8,0},{16,8},{24,16},{1,25},{9,1},{17,9},{25,17},{2,26},{10... | collective-permute-start | bytes 884744 | tf_op jit(solution)/shard_map/ppermute | solution.py:309
  185.1 19.9 %collective-permute-start.35 = (bf16[192,768]{1,0:T(8,128)(2,1)}, bf16[192,768]{1,0:T(8,128)(2,1)S(1)}, u32[]{:S(2)}, u32[]{:S(2)}) collective-permute-start(bf16[192,768]{1,0:T(8,128)(2,1)} %get-tuple-element.298), channel_id=1, source_target_pairs={{0,16},{8,24},{16,0},{24,8},{1,17},{9,25},{17,1},{25,9},{2,18},{10... | collective-permute-start | bytes 884744 | tf_op jit(solution)/shard_map/ppermute | solution.py:309
  199.4 8.4 %copy-start.6 = (bf16[4,96,576]{2,1,0:T(8,128)(2,1)S(1)}, bf16[4,96,576]{2,1,0:T(8,128)(2,1)}, u32[]{:S(2)}) copy-start(bf16[4,96,576]{2,1,0:T(8,128)(2,1)} %get-tuple-element.249) | copy-start | bytes 1327108
  205.7 2.1 collective-permute-start.37
  208.9 8.3 %copy-start.28 = (f32[32,24]{1,0:T(8,128)S(1)}, f32[32,24]{1,0:T(8,128)}, u32[]{:S(2)}) copy-start(f32[32,24]{1,0:T(8,128)} %get-tuple-element.275) | copy-start | bytes 9220
  208.9 8.4 %copy-start.3 = (f32[256,768]{1,0:T(8,128)S(1)}, f32[256,768]{1,0:T(8,128)}, u32[]{:S(2)}) copy-start(f32[256,768]{1,0:T(8,128)} %get-tuple-element.187.middle_ref) | copy-start | bytes 2359300
  208.9 8.4 %copy-start.14 = (bf16[256,768]{1,0:T(8,128)(2,1)S(1)}, bf16[256,768]{1,0:T(8,128)(2,1)}, u32[]{:S(2)}) copy-start(bf16[256,768]{1,0:T(8,128)(2,1)} %get-tuple-element.244) | copy-start | bytes 1179652
  208.9 25.2 %all-to-all-start.3 = ((bf16[4,144,576]{2,1,0:T(8,128)(2,1)}), bf16[4,144,576]{2,1,0:T(8,128)(2,1)S(1)}, u32[]{:S(2)}, u32[]{:S(2)}) async-start(bf16[4,144,576]{2,1,0:T(8,128)(2,1)} %pad_maximum_fusion.5), calls=%async_computation.3 | async-start | bytes 1474560 | tf_op jit(solution)/shard_map/all_to_all | solution.py:935
  213.6 12.4 %collective-permute-start.38 = (bf16[256,768]{1,0:T(8,128)(2,1)}, bf16[256,768]{1,0:T(8,128)(2,1)}, u32[]{:S(2)}, u32[]{:S(2)}) collective-permute-start(bf16[256,768]{1,0:T(8,128)(2,1)} %get-tuple-element.261), channel_id=1, source_target_pairs={{0,2},{1,3},{2,0},{3,1},{4,6},{5,7},{6,4},{7,5},{8,10},{9,11},{10,... | collective-permute-start | bytes 1179656 | tf_op jit(solution)/shard_map/ppermute | solution.py:253
  214.8 19.3 %collective-permute-start.39 = (bf16[256,768]{1,0:T(8,128)(2,1)}, bf16[256,768]{1,0:T(8,128)(2,1)}, u32[]{:S(2)}, u32[]{:S(2)}) collective-permute-start(bf16[256,768]{1,0:T(8,128)(2,1)} %get-tuple-element.262), channel_id=1, source_target_pairs={{0,4},{1,5},{2,6},{3,7},{4,0},{5,1},{6,2},{7,3},{8,12},{9,13},{10,... | collective-permute-start | bytes 1179656 | tf_op jit(solution)/shard_map/ppermute | solution.py:253
  216.3 17.9 %collective-permute-start.40 = (bf16[256,768]{1,0:T(8,128)(2,1)}, bf16[256,768]{1,0:T(8,128)(2,1)}, u32[]{:S(2)}, u32[]{:S(2)}) collective-permute-start(bf16[256,768]{1,0:T(8,128)(2,1)} %get-tuple-element.263), channel_id=1, source_target_pairs={{0,6},{1,7},{2,4},{3,5},{4,2},{5,3},{6,0},{7,1},{8,14},{9,15},{10,... | collective-permute-start | bytes 1179656 | tf_op jit(solution)/shard_map/ppermute | solution.py:253
  219.3 15.0 %copy-start.15 = (bf16[256,768]{1,0:T(8,128)(2,1)S(1)}, bf16[256,768]{1,0:T(8,128)(2,1)}, u32[]{:S(2)}) copy-start(bf16[256,768]{1,0:T(8,128)(2,1)} %get-tuple-element.264) | copy-start | bytes 1179652
  236.0 7.3 %collective-permute-start.41 = (bf16[128,768]{1,0:T(8,128)(2,1)S(1)}, bf16[128,768]{1,0:T(8,128)(2,1)S(1)}, u32[]{:S(2)}, u32[]{:S(2)}) collective-permute-start(bf16[128,768]{1,0:T(8,128)(2,1)S(1)} %get-tuple-element.318), channel_id=1, source_target_pairs={{0,1},{1,0},{2,3},{3,2},{4,5},{5,4},{6,7},{7,6},{8,9},{9,8},{10,11... | collective-permute-start | bytes 589832 | tf_op jit(solution)/shard_map/ppermute | solution.py:253
  237.1 1.5 collective-permute-start.42
  239.5 12.0 %all-to-all-start.4 = ((bf16[8,24,984]{2,1,0:T(8,128)(2,1)}), bf16[8,24,984]{2,1,0:T(8,128)(2,1)S(1)}, u32[]{:S(2)}, u32[]{:S(2)}) async-start(bf16[8,24,984]{2,1,0:T(8,128)(2,1)} %pad_maximum_fusion.10), calls=%async_computation.4 | async-start | bytes 786432 | tf_op jit(solution)/shard_map/all_to_all | solution.py:952
  (33 other events, 128.8 us)

commit v4 on v3

--- a/solution.py
+++ b/solution.py
@@ -644,7 +644,7 @@
 
 def branch_kernel(
     place_ref, own_ref, x_ref, y_ref, across_ref, grad_ref, middle_ref, vectors_ref, w_ref,
-    attended_ref, d_middle_ref, d_attended_ref, sums_ref, near_ref, far_ref, total,
+    attended_ref, bias_ref, d_middle_ref, d_attended_ref, sums_ref, near_ref, far_ref, total,
 ):
     blocks, count, rows = d_attended_ref.shape
     groups, seqs = blocks // 2, 2
@@ -672,45 +672,42 @@
                 start = pl.multiple_of((column * blocks + owner) * share, 8)
                 grad_out_ref[item, column] = total[pl.ds(start, share)].astype(jnp.bfloat16)
     sums_ref[...] = jnp.zeros_like(sums_ref)
-    sums_ref[0:1] = jnp.sum(d_branch.astype(jnp.float32), 0, keepdims=True)
-    sums_ref[1:2] = jnp.sum(grad_ref[...].astype(jnp.float32), 0, keepdims=True)
-    sums_ref[2:3] = jnp.sum(d_second * normal, 0, keepdims=True)
-    sums_ref[3:4] = jnp.sum(d_second, 0, keepdims=True)
+    sums_ref[2:3] = jnp.sum(d_branch.astype(jnp.float32), 0, keepdims=True)
+    sums_ref[3:4] = jnp.sum(grad_ref[...].astype(jnp.float32), 0, keepdims=True)
+    sums_ref[6:7] = jnp.sum(d_second * normal, 0, keepdims=True)
+    sums_ref[7:8] = jnp.sum(d_second, 0, keepdims=True)
+    sums_ref[8:12] = bias_ref[...]
 
 
 def hidden_kernel(*refs):
-    rows_refs, grad_refs = refs[:4], refs[4:8]
-    w_up, w_down, bias_ref, act_ref, d_upper_ref, *d_rows_refs, sums_ref = refs[8:]
-    tokens = rows_refs[0].shape[0]
-    skip = (grad_refs[0].shape[0] - tokens) // 2
+    count = (len(refs) - 4) // 5
+    groups = [refs[count * item : count * (item + 1)] for item in range(2)]
+    w_up, w_down, bias_ref = refs[2 * count : 2 * count + 3]
+    groups += [refs[count * item + 3 : count * (item + 1) + 3] for item in range(2, 5)]
+    sums_ref = refs[-1]
     slope = 0.7978845608028654
     sums_ref[...] = jnp.zeros_like(sums_ref)
-    for item in range(4):
-        place = pl.ds(item * tokens, tokens)
-        upper = dot(rows_refs[item][...], w_up[...]) + bias_ref[...]
+    for row_ref, grad_ref, act_ref, d_upper_ref, d_rows_ref in zip(*groups):
+        upper = dot(row_ref[...], w_up[...]) + bias_ref[...]
         square = upper * upper
         bend = jnp.tanh(slope * (upper + 0.044715 * (square * upper)))
-        act_ref[place] = (0.5 * upper * (1.0 + bend)).astype(jnp.bfloat16)
+        act_ref[...] = (0.5 * upper * (1.0 + bend)).astype(jnp.bfloat16)
         rise = 0.5 * (1.0 + bend) + (0.5 * slope) * upper * (1.0 - bend * bend) * (
             1.0 + (3.0 * 0.044715) * square
         )
-        d_act = dot_right(grad_refs[item][skip : skip + tokens], w_down[...])
-        d_upper = (d_act * rise).astype(jnp.bfloat16)
-        d_upper_ref[place] = d_upper
+        d_upper = (dot_right(grad_ref[...], w_down[...]) * rise).astype(jnp.bfloat16)
+        d_upper_ref[...] = d_upper
         sums_ref[0:1] += jnp.sum(d_upper.astype(jnp.float32), 0, keepdims=True)
-        d_rows_refs[item][...] = dot_right(d_upper, w_up[...]).astype(jnp.bfloat16)
+        d_rows_ref[...] = dot_right(d_upper, w_up[...]).astype(jnp.bfloat16)
 
 
 def hidden_weights_kernel(core_ref, *refs):
-    rows_refs, grad_refs = refs[:4], refs[4:8]
-    act_ref, d_upper_ref, w_down, *down_refs, late_near, late_far, up, down = refs[8:]
-    tokens = rows_refs[0].shape[0]
-    skip = (grad_refs[0].shape[0] - tokens) // 2
-    for item in range(4):
-        place = pl.ds(item * tokens, tokens)
-        down_refs[item][...] = dot(act_ref[place], w_down[...]).astype(jnp.bfloat16)
-        up_term = dot_left(rows_refs[item][...], d_upper_ref[place])
-        down_term = dot_left(act_ref[place], grad_refs[item][skip : skip + tokens])
+    groups = [refs[4 * item : 4 * item + 4] for item in range(4)]
+    w_down, *down_refs, late_near, late_far, up, down = refs[16:]
+    for item, (row_ref, grad_ref, act_ref, d_upper_ref) in enumerate(zip(*groups)):
+        down_refs[item][...] = dot(act_ref[...], w_down[...]).astype(jnp.bfloat16)
+        up_term = dot_left(row_ref[...], d_upper_ref[...])
+        down_term = dot_left(act_ref[...], grad_ref[...])
         if item == 0:
             up[...] = up_term
             down[...] = down_term
@@ -794,16 +791,15 @@
     small = jnp.pad(small[None], ((0, 7), (0, width - small_size)))
     small = column_parts(jnp.concatenate([out_weight, small]), columns)
     mine = in_order(pick(hidden_in, core), swap(pick(hidden_in, 1 - core), CORE), core, 0)
-    got, small, mine = tie(got, small, mine)
+    beside = chips(cotangent.reshape(tokens, width))
+    got, small, mine, beside = tie(got, small, mine, beside)
 
     got_up = got[:, 3 * group_width :]
-    later = [
-        got_up[:half],
-        got_up[half:],
-        down_weight,
-        pick(got[:, : 3 * group_width].reshape(2, half, -1), core),
-    ]
-    later = column_parts(jnp.concatenate(later, -1), columns)
+    w_qkv = pick(got[:, : 3 * group_width].reshape(2, half, -1), core)
+    w_qkv = column_parts(w_qkv, columns)
+    later = jnp.concatenate([got_up[:half], got_up[half:], down_weight], -1)
+    later = jnp.broadcast_to(later, (columns,) + later.shape)
+    later = lax.all_to_all(later, "dp", 0, 0, tiled=True)
 
     small = column_order(small, column)
     w_out = small[:, :share].reshape(columns * share, width)
@@ -825,18 +821,14 @@
     bias_here = jnp.concatenate([own_columns(bq), jnp.zeros((group_width,)), own_columns(bv)])
 
     w_out = in_order(w_out, swap(w_out, CORE), core, 0)
-    mine, w_out, own_low = tie(mine, w_out, cotangent.reshape(tokens, width))
+    mine, w_out = tie(mine, w_out)
     w_out = chips(w_out)
-    first_vectors, bias_here, segments, later, w_out, own_low = tie(
-        first_vectors, bias_here, segments, later, w_out, own_low
-    )
-    beside = chips(own_low)
-    w_qkv = jnp.stack([item[:, 2 * width :] for item in later])
+    first_vectors, bias_here, segments, w_qkv = tie(first_vectors, bias_here, segments, w_qkv)
+    w_qkv = jnp.stack(w_qkv)
     attended, projected, kept, (normal_all, normed, w_qkv) = attend(
         place, column, mine, w_qkv, swap(w_qkv, CORE), first_vectors, bias_here, segments
     )
     attended, beside, later, w_out = tie(attended, beside, later, w_out)
-    later = column_order([item[:, : 2 * width] for item in later], column)
     later_far = swap(later, CORE)
     w_out = chips_order(w_out, chip).reshape(plane, columns, share, width)
     w_out = w_out.transpose(1, 0, 2, 3).reshape(width, width)
@@ -862,26 +854,39 @@
     )
     w_up = w_up.reshape(columns, half, 2, width).transpose(0, 2, 1, 3).reshape(width, width)
 
-    many = GROUPS * tokens
-    act, d_upper, *d_rows, d_bu = run(
-        hidden_kernel,
-        (*second, *beside, w_up, w_down, bu[None]),
-        (low(many, width), low(many, width), *[low(tokens, width)] * 4, one(8, width)),
-        12 * many * width * width,
-    )
+    acts, d_uppers, d_rows, d_bu = [], [], [], 0.0
+    for part in (slice(0, 1), slice(1, 4)):
+        count = len(second[part])
+        *outs, sums = run(
+            hidden_kernel,
+            (*second[part], *beside[part], w_up, w_down, bu[None]),
+            (*[low(tokens, width)] * (3 * count), one(8, width)),
+            12 * count * tokens * width * width,
+        )
+        acts += outs[:count]
+        d_uppers += outs[count : 2 * count]
+        d_rows += outs[2 * count :]
+        d_bu = d_bu + sums
     d_second = [swap(d_rows[i], mask) for i, mask in ((1, NEAR_X), (2, NEAR_Y), (3, ACROSS))]
-    act, d_rows = tie(act, d_rows)
+    acts, d_rows = tie(acts, d_rows)
     *down, late, late_far = run(
         hidden_weights_kernel,
-        (*second, *beside, act, d_upper, w_down),
+        (*second, *beside, *acts, *d_uppers, w_down),
         (*[low(tokens, width)] * 4, *[low(columns, 2 * half, width)] * 2),
-        12 * many * width * width,
+        24 * tokens * width * width,
         [pltpu.VMEM((width, width), jnp.float32)] * 2,
         (core,),
     )
     d_second, late, late_far, down = tie(d_second, late, late_far, down)
     late = plus(late, swap(late_far, CORE))
-    d_middle, d_attended, sums, grad_out, grad_far = run(
+    d_bu = lax.dynamic_update_slice_in_dim(
+        jnp.zeros((columns, GROUPS, 2, ff_share), jnp.float32),
+        d_bu[0].reshape(2, columns, 1, ff_share).transpose(1, 2, 0, 3),
+        chip,
+        1,
+    )
+    d_bu = d_bu.reshape(owners, -1, share).transpose(1, 0, 2).reshape(-1, width)
+    d_middle, d_attended, terms, grad_out, grad_far = run(
         branch_kernel,
         (
             d_rows[0],
@@ -891,18 +896,18 @@
             norm_vectors,
             w_out,
             attended,
+            d_bu,
         ),
         (
             one(tokens, width),
             low(plane, group_width, rows),
-            one(8, width),
+            one(16, width),
             *[low(GROUPS, columns, share, width)] * 2,
         ),
         4 * tokens * width * width,
         [pltpu.VMEM((width, width), jnp.float32)],
         (place,),
     )
-    d_attended, late = tie(d_attended, late)
     late = column_send(late, column, columns)
     d_attended = lax.all_to_all(d_attended, "seq", 0, 0, tiled=True)
     grad_out = plus(grad_out, swap(grad_far, CORE))
@@ -913,15 +918,6 @@
     down = [down[0]] + [
         swap(down[i], mask) for i, mask in ((1, NEAR_X), (2, NEAR_Y), (3, ACROSS))
     ]
-    d_bu = lax.dynamic_update_slice_in_dim(
-        jnp.zeros((columns, GROUPS, 2, ff_share), jnp.float32),
-        d_bu[0].reshape(2, columns, 1, ff_share).transpose(1, 2, 0, 3),
-        chip,
-        1,
-    )
-    d_bu = d_bu.reshape(owners, -1, share).transpose(1, 0, 2).reshape(-1, width)
-    blank = jnp.zeros((2, width), jnp.float32)
-    terms = jnp.concatenate([blank, sums[:2], blank, sums[2:4], d_bu, blank, blank])
     grad_near, grad_far, *d_first, terms = attend_back(
         place, columns, projected, kept, d_attended, normed, w_qkv, normal_all, terms
     )
@@ -937,7 +933,7 @@
         swap(d_first[item], mask) for item, mask in ((1, NEAR_X), (2, NEAR_Y), (3, ACROSS))
     ]
 
-    last, late, d_first = tie(last, late, d_first)
+    last, late = tie(last, late)
     last, late = jnp.sum(last.astype(jnp.float32), 0), total_of(late)
     grad_up = jnp.concatenate([late[:half, : width // 2], late[:half, width // 2 :]])
     grad_down = late[half:]

time: 263 us -> 255 us (0.970)
  waiting for transfers between devices: 89 us -> 71.9 us
  starting transfers between devices: 61.8 us -> 73.2 us
  other arithmetic: 20.7 us -> 17.2 us
    ppermute x34, waiting for transfers between devices: 54.3 us -> 40.7 us  [swap(): lax.ppermute(value, 'seq', [(item, item ^ mask) for item in range(8)])]
    ppermute x6, waiting for transfers between devices: 10.8 us -> 4.14 us  [column_parts(): parts.append(lax.ppermute(value, 'dp', perm))]
    all_to_all x1, waiting for transfers between devices: 0.01 us -> 5.42 us  [plane_local(): last = lax.all_to_all(last, 'dp', 0, 0, tiled=True)]
    all_to_all x0 -> x1, starting transfers between devices: none -> 4.74 us  [plane_local(): later = lax.all_to_all(later, 'dp', 0, 0, tiled=True)]
    ppermute x6, starting transfers between devices: 8.54 us -> 12 us  [column_parts(): parts.append(lax.ppermute(value, 'dp', perm))]
    ppermute x3, waiting for transfers between devices: 11.9 us -> 8.8 us  [column_send(): parts.append(lax.ppermute(sent, 'dp', perm))]
    pallas_call x4 -> x5, Pallas kernels: 26.4 us -> 28 us  [run(): pl.pallas_call(body, grid=(1,), in_specs=specs + [whole(*item.shape) for...]
  transfers between devices with their start and end apart: 48 -> 49, of which waited for: 22 -> 21; matrix products, arithmetic and copies ran while one was open for 10% -> 13% of each run, Pallas kernels for 18% -> 21%
where the time goes in v4:
time: 255 us; the launch traced here: 250 us
  starting transfers between devices  73.2 us (29%)
  waiting for transfers between devices  71.9 us (28%)
  Pallas kernels  58.3 us (23%)
  local copies, waits for them, and re-layouts  27.1 us (11%)
  other arithmetic  17.2 us (7%)
    ppermute x34, waiting for transfers between devices, swap(): lax.ppermute(value, 'seq', [(item, item ^ mask) for item in range(8)])  40.7 us
    ppermute x34, starting transfers between devices, swap(): lax.ppermute(value, 'seq', [(item, item ^ mask) for item in range(8)])  32.5 us
    pallas_call x5, Pallas kernels, run(): pl.pallas_call(body, grid=(1,), in_specs=specs + [whole(*item.shape) for...  28 us
    pallas_call x1, Pallas kernels, attend(): pl.pallas_call(attend_kernel, grid=(heads,), in_specs=[pl.BlockSpec(memor...  16.4 us
    pallas_call x1, Pallas kernels, attend_back(): pl.pallas_call(attend_back_kernel, grid=(heads,), in_specs=[pl.BlockSpec(...  13.8 us
    ppermute x6, starting transfers between devices, column_parts(): parts.append(lax.ppermute(value, 'dp', perm))  12 us
    ppermute x3, waiting for transfers between devices, column_send(): parts.append(lax.ppermute(sent, 'dp', perm))  8.8 us
    all_to_all x1, waiting for transfers between devices, plane_local(): attended = lax.all_to_all(attended, 'seq', 0, 0, tiled=True)  5.59 us
  transfers between devices with their start and end apart: 49, of which 21 were waited for; matrix products, arithmetic and copies ran while one was open for 13% of the time, Pallas kernels for 21%

profile of v4, /device:TPU:0, one launch (start us, length us, event | category | flops | bytes accessed | tf_op | source)
XLA Modules:
  0.0 250.0 jit_solution(4649145970622470917)
XLA Ops:
  0.7 4.0 %collective-permute-start.6 = (bf16[256,768]{1,0:T(8,128)(2,1)}, bf16[256,768]{1,0:T(8,128)(2,1)S(1)}, u32[]{:S(2)}, u32[]{:S(2)}) collective-permute-start(bf16[256,768]{1,0:T(8,128)(2,1)} %bitcast.184), channel_id=1, source_target_pairs={{0,6},{1,7},{2,4},{3,5},{4,2},{5,3},{6,0},{7,1},{8,14},{9,15},{10,... | collective-permute-start | bytes 1179656 | tf_op jit(solution)/shard_map/ppermute | solution.py:253
  10.2 4.1 %all-to-all-start = ((bf16[8,24,960]{2,1,0:T(8,128)(2,1)}), bf16[8,24,960]{2,1,0:T(8,128)(2,1)S(1)}, u32[]{:S(2)}, u32[]{:S(2)}) async-start(bf16[8,24,960]{2,1,0:T(8,128)(2,1)} %pad_maximum_fusion.6), calls=%async_computation | async-start | bytes 786432 | tf_op jit(solution)/shard_map/all_to_all | solution.py:788
  15.2 3.7 %collective-permute-start.2 = (bf16[32,768]{1,0:T(8,128)(2,1)S(1)}, bf16[32,768]{1,0:T(8,128)(2,1)S(1)}, u32[]{:S(2)}, u32[]{:S(2)}) collective-permute-start(bf16[32,768]{1,0:T(8,128)(2,1)S(1)} %fusion.10), channel_id=1, source_target_pairs={{0,24},{8,0},{16,8},{24,16},{1,25},{9,1},{17,9},{25,17},{2,26},{10... | collective-permute-start | bytes 147464 | tf_op jit(solution)/shard_map/ppermute | solution.py:294
  18.9 1.7 collective-permute-done.2
  20.6 1.3 collective-permute-start.1
  21.9 3.4 %collective-permute-start = (bf16[32,768]{1,0:T(8,128)(2,1)S(1)}, bf16[32,768]{1,0:T(8,128)(2,1)S(1)}, u32[]{:S(2)}, u32[]{:S(2)}) collective-permute-start(bf16[32,768]{1,0:T(8,128)(2,1)S(1)} %fusion.10), channel_id=1, source_target_pairs={{0,8},{8,16},{16,24},{24,0},{1,9},{9,17},{17,25},{25,1},{2,10},{10... | collective-permute-start | bytes 147464 | tf_op jit(solution)/shard_map/ppermute | solution.py:294
  26.1 1.7 collective-permute-done
  29.6 2.7 %collective-permute-start.14 = (bf16[96,576]{1,0:T(8,128)(2,1)S(1)}, bf16[96,576]{1,0:T(8,128)(2,1)S(1)}, u32[]{:S(2)}, u32[]{:S(2)}) collective-permute-start(bf16[96,576]{1,0:T(8,128)(2,1)S(1)} %dynamic-slice_bitcast_fusion.6), channel_id=1, source_target_pairs={{0,24},{8,0},{16,8},{24,16},{1,25},{9,1},{17,9},{25,17},{2,26},{10... | collective-permute-start | bytes 331784 | tf_op jit(solution)/shard_map/ppermute | solution.py:294
  33.4 2.6 %collective-permute-start.10 = (bf16[2,136,768]{2,1,0:T(8,128)(2,1)S(1)}, bf16[2,136,768]{2,1,0:T(8,128)(2,1)S(1)}, u32[]{:S(2)}, u32[]{:S(2)}) collective-permute-start(bf16[2,136,768]{2,1,0:T(8,128)(2,1)S(1)} %pad_maximum_fusion.5.own_ref), channel_id=1, source_target_pairs={{0,6},{1,7},{2,4},{3,5},{4,2},{5,3},{6,0},{7,1},{8,14},{9,15},{10,... | collective-permute-start | bytes 1253384 | tf_op jit(solution)/shard_map/ppermute | solution.py:253
  36.0 1.1 broadcast_in_dim.32
  37.1 4.7 %all-to-all-start.1 = ((bf16[4,96,1536]{2,1,0:T(8,128)(2,1)}), bf16[4,96,1536]{2,1,0:T(8,128)(2,1)S(1)}, u32[]{:S(2)}, u32[]{:S(2)}) async-start(bf16[4,96,1536]{2,1,0:T(8,128)(2,1)} %broadcast_in_dim.32), calls=%async_computation.1 | async-start | bytes 2359296 | tf_op jit(solution)/shard_map/all_to_all | solution.py:802
  42.5 3.2 %collective-permute-done.10.across_ref = bf16[2,136,768]{2,1,0:T(8,128)(2,1)S(1)} collective-permute-done((bf16[2,136,768]{2,1,0:T(8,128)(2,1)S(1)}, bf16[2,136,768]{2,1,0:T(8,128)(2,1)S(1)}, u32[]{:S(2)}, u32[]{:S(2)}) %collective-permute-start.10) | collective-permute-done | bytes 417824 | tf_op jit(solution)/shard_map/ppermute | solution.py:253
  45.7 1.6 collective-permute-start.8
  47.3 7.2 %collective-permute-done.9.y_ref = bf16[2,136,768]{2,1,0:T(8,128)(2,1)S(1)} collective-permute-done((bf16[2,136,768]{2,1,0:T(8,128)(2,1)S(1)}, bf16[2,136,768]{2,1,0:T(8,128)(2,1)S(1)}, u32[]{:S(2)}, u32[]{:S(2)}) %collective-permute-start.9) | collective-permute-done | bytes 417824 | tf_op jit(solution)/shard_map/ppermute | solution.py:253
  54.5 1.3 collective-permute-done.8.x_ref
  60.6 1.1 collective-permute-done.11
  61.7 2.6 %collective-permute-start.18 = (bf16[2,96,768]{2,1,0:T(8,128)(2,1)S(1)}, bf16[2,96,768]{2,1,0:T(8,128)(2,1)S(1)}, u32[]{:S(2)}, u32[]{:S(2)}) collective-permute-start(bf16[2,96,768]{2,1,0:T(8,128)(2,1)S(1)} %maximum_select_fusion.3), channel_id=1, source_target_pairs={{0,6},{1,7},{2,4},{3,5},{4,2},{5,3},{6,0},{7,1},{8,14},{9,15},{10,... | collective-permute-start | bytes 884744 | tf_op jit(solution)/shard_map/ppermute | solution.py:253
  67.2 16.4 %shard_map.305 = (bf16[1024,768]{1,0:T(8,128)(2,1)}, bf16[1024,768]{1,0:T(8,128)(2,1)}, bf16[768,576]{1,0:T(8,128)(2,1)}, bf16[1024,192]{1,0:T(8,128)(2,1)}, bf1...) custom-call(s32[2]{0:T(128)} %pad_add_fusion.place_ref, ...), custom_call_target="tpu_custom_call" | custom-call | flops 1711276032 | bytes 6291456 | tf_op jit(solution)/shard_map/pallas_call | solution.py:513
  85.5 4.1 %all-to-all-start.2 = ((bf16[8,192,128]{2,1,0:T(8,128)(2,1)}), bf16[8,192,128]{2,1,0:T(8,128)(2,1)S(1)}, u32[]{:S(2)}, u32[]{:S(2)}) async-start(bf16[8,192,128]{2,1,0:T(8,128)(2,1)} %get-tuple-element.179), calls=%async_computation.2 | async-start | bytes 786432 | tf_op jit(solution)/shard_map/all_to_all | solution.py:835
  89.6 1.2 pad_maximum_fusion
  91.0 1.1 copy.157
  92.1 5.6 %all-to-all-done.2.attended_ref = bf16[8,192,128]{2,1,0:T(8,128)(2,1)S(1)} async-done(((bf16[8,192,128]{2,1,0:T(8,128)(2,1)}), bf16[8,192,128]{2,1,0:T(8,128)(2,1)S(1)}, u32[]{:S(2)}, u32[]{:S(2)}) %all-to-all-start.2) | async-done | bytes 393248 | tf_op jit(solution)/shard_map/all_to_all | solution.py:835
  98.5 3.1 %shard_map.306 = (f32[256,768]{1,0:T(8,128)}, bf16[256,768]{1,0:T(8,128)(2,1)}) custom-call(bf16[8,192,128]{2,1,0:T(8,128)(2,1)} %copy-done.2, bf16[768,768]{1,0:T(8,128)(2,1)} %bitcast.154, bf16[256,768]{1,0:T(8,128)(2,1)} %bitcast.153, f32[8,768]{1,0:T(8,128)} %stack.238.vectors_ref), custom_call_target="tpu_custom_call" | custom-call | flops 301989888 | tf_op jit(solution)/shard_map/pallas_call | solution.py:618
  102.1 1.5 collective-permute-start.21
  103.6 1.5 collective-permute-start.20
  105.6 1.1 slice.269
  106.8 1.1 copy.174
  108.0 6.8 %collective-permute-done.22.refs_2_.refs_3_ = bf16[256,768]{1,0:T(8,128)(2,1)S(1)} collective-permute-done((bf16[256,768]{1,0:T(8,128)(2,1)}, bf16[256,768]{1,0:T(8,128)(2,1)S(1)}, u32[]{:S(2)}, u32[]{:S(2)}) %collective-permute-start.22) | collective-permute-done | bytes 393248 | tf_op jit(solution)/shard_map/ppermute | solution.py:253
  114.8 5.6 %collective-permute-done.21.refs_1_.refs_2_ = bf16[256,768]{1,0:T(8,128)(2,1)S(1)} collective-permute-done((bf16[256,768]{1,0:T(8,128)(2,1)}, bf16[256,768]{1,0:T(8,128)(2,1)S(1)}, u32[]{:S(2)}, u32[]{:S(2)}) %collective-permute-start.21) | collective-permute-done | bytes 393248 | tf_op jit(solution)/shard_map/ppermute | solution.py:253
  121.2 6.7 %shard_map.308 = (bf16[256,768]{1,0:T(8,128)(2,1)}, bf16[256,768]{1,0:T(8,128)(2,1)}, bf16[256,768]{1,0:T(8,128)(2,1)}, bf16[256,768]{1,0:T(8,128)(2,1)}, bf16[2...) custom-call(bf16[256,768]{1,0:T(8,128)(2,1)} %copy-done.46, ...), custom_call_target="tpu_custom_call" | custom-call | flops 5435817984 | tf_op jit(solution)/shard_map/pallas_call | solution.py:618
  128.0 1.5 collective-permute-start.23
  129.5 1.4 collective-permute-start.24
  131.5 3.9 %shard_map.307 = (bf16[256,768]{1,0:T(8,128)(2,1)}, bf16[256,768]{1,0:T(8,128)(2,1)}, bf16[256,768]{1,0:T(8,128)(2,1)}, f32[8,768]{1,0:T(8,128)}) custom-call(bf16[256,768]{1,0:T(8,128)(2,1)} %get-tuple-element.188.refs_0_, bf16[256,768]{1,0:T(8,128)(2,1)} %bitcast.187, bf16[768,768]{1,0:T(8,128)(2,1)} %bitcast.170, bf16[768,768]{1,0:T(8,128)(2,1)} %bitcast.167, ...), custom_call_target="tpu_custom_call" | custom-call | flops 1811939328 | tf_op jit(solution)/shard_map/pallas_call | solution.py:618
  135.3 8.7 %shard_map.309 = (bf16[256,768]{1,0:T(8,128)(2,1)}, bf16[256,768]{1,0:T(8,128)(2,1)}, bf16[256,768]{1,0:T(8,128)(2,1)}, bf16[256,768]{1,0:T(8,128)(2,1)}, bf16[4...) custom-call(s32[1]{0:T(128)} %bitcast.45.core_ref, bf16[256,768]{1,0:T(8,128)(2,1)} %get-tuple-element.188.refs_0_, ...), custom_call_target="tpu_custom_call" | custom-call | flops 3623878656 | tf_op jit(solution)/shard_map/pallas_call | solution.py:618
  144.0 3.1 %collective-permute-done.24.y_ref = bf16[256,768]{1,0:T(8,128)(2,1)S(1)} collective-permute-done((bf16[256,768]{1,0:T(8,128)(2,1)}, bf16[256,768]{1,0:T(8,128)(2,1)S(1)}, u32[]{:S(2)}, u32[]{:S(2)}) %collective-permute-start.24) | collective-permute-done | bytes 393248 | tf_op jit(solution)/shard_map/ppermute | solution.py:253
  147.1 1.2 collective-permute-done.25.across_ref
  150.1 5.6 %shard_map.310 = (f32[256,768]{1,0:T(8,128)}, bf16[8,192,128]{2,1,0:T(8,128)(2,1)}, f32[16,768]{1,0:T(8,128)}, bf16[4,4,24,768]{3,2,1,0:T(8,128)(2,1)}, bf16[4,4,24,768]{3,2,1,0:T(8,128)(2,1)}) custom-call(s32[1]{0:T(128)} %bitcast.place_ref, bf16[256,768]{1,0:T(8,128)(2,1)} %get-tuple-element.202.own_ref, bf16[256,768]{1,0:T(8,128)(2,1)} %copy-done.11, ...), custom_call_target="tpu_custom_call" | custom-call | flops 603979776 | tf_op jit(solution)/shard_map/pallas_call | solution.py:618
  156.2 4.2 %all-to-all-start.3 = ((bf16[8,192,128]{2,1,0:T(8,128)(2,1)}), bf16[8,192,128]{2,1,0:T(8,128)(2,1)}, u32[]{:S(2)}, u32[]{:S(2)}) async-start(bf16[8,192,128]{2,1,0:T(8,128)(2,1)} %get-tuple-element.222), calls=%async_computation.3 | async-start | bytes 786432 | tf_op jit(solution)/shard_map/all_to_all | solution.py:912
  160.9 0.9 dynamic-slice_bitcast_fusion
  161.8 1.9 collective-permute-start.27
  163.8 2.9 %collective-permute-start.31 = (bf16[4,24,768]{2,1,0:T(8,128)(2,1)S(1)}, bf16[4,24,768]{2,1,0:T(8,128)(2,1)S(1)}, u32[]{:S(2)}, u32[]{:S(2)}) collective-permute-start(bf16[4,24,768]{2,1,0:T(8,128)(2,1)S(1)} %get-tuple-element.303), channel_id=1, source_target_pairs={{0,6},{1,7},{2,4},{3,5},{4,2},{5,3},{6,0},{7,1},{8,14},{9,15},{10,... | collective-permute-start | bytes 442376 | tf_op jit(solution)/shard_map/ppermute | solution.py:253
  167.5 1.8 all-to-all-done.3.d_ref
  169.3 3.6 %collective-permute-done.27 = bf16[192,768]{1,0:T(8,128)(2,1)S(1)} collective-permute-done((bf16[192,768]{1,0:T(8,128)(2,1)S(1)}, bf16[192,768]{1,0:T(8,128)(2,1)S(1)}, u32[]{:S(2)}, u32[]{:S(2)}) %collective-permute-start.27) | collective-permute-done | bytes 294944 | tf_op jit(solution)/shard_map/ppermute | solution.py:309
  172.9 1.7 collective-permute-start.32
  174.6 1.5 collective-permute-start.33
  177.0 1.5 collective-permute-start.36
  178.7 13.8 %shard_map.311 = (bf16[4,96,576]{2,1,0:T(8,128)(2,1)}, bf16[4,96,576]{2,1,0:T(8,128)(2,1)}, bf16[256,768]{1,0:T(8,128)(2,1)}, bf16[256,768]{1,0:T(8,128)(2,1)}, ...) custom-call(s32[2]{0:T(128)} %pad_add_fusion.1.chip_ref, ...), custom_call_target="tpu_custom_call" | custom-call | flops 3825205248 | bytes 6291456 | tf_op jit(solution)/shard_map/pallas_call | solution.py:557
  192.5 5.2 %collective-permute-done.35 = bf16[192,768]{1,0:T(8,128)(2,1)S(1)} collective-permute-done((bf16[192,768]{1,0:T(8,128)(2,1)S(1)}, bf16[192,768]{1,0:T(8,128)(2,1)S(1)}, u32[]{:S(2)}, u32[]{:S(2)}) %collective-permute-start.35) | collective-permute-done | bytes 294944 | tf_op jit(solution)/shard_map/ppermute | solution.py:309
  198.7 1.1 collective-permute-start.37
  199.8 1.3 collective-permute-start.38
  201.1 1.1 collective-permute-start.39
  202.2 1.0 add_convert_fusion.5
  203.7 1.8 pad_maximum_fusion.3
  205.5 4.4 %all-to-all-start.4 = ((bf16[4,144,576]{2,1,0:T(8,128)(2,1)}), bf16[4,144,576]{2,1,0:T(8,128)(2,1)S(1)}, u32[]{:S(2)}, u32[]{:S(2)}) async-start(bf16[4,144,576]{2,1,0:T(8,128)(2,1)} %pad_maximum_fusion.3), calls=%async_computation.4 | async-start | bytes 1474560 | tf_op jit(solution)/shard_map/all_to_all | solution.py:931
  211.0 8.8 %collective-permute-done.38 = bf16[256,768]{1,0:T(8,128)(2,1)} collective-permute-done((bf16[256,768]{1,0:T(8,128)(2,1)}, bf16[256,768]{1,0:T(8,128)(2,1)}, u32[]{:S(2)}, u32[]{:S(2)}) %collective-permute-start.38) | collective-permute-done | bytes 393248 | tf_op jit(solution)/shard_map/ppermute | solution.py:253
  219.8 1.6 add_convert_fusion.3
  221.6 1.0 add_convert_fusion.4
  223.4 5.4 %all-to-all-done.4 = bf16[4,144,576]{2,1,0:T(8,128)(2,1)S(1)} async-done(((bf16[4,144,576]{2,1,0:T(8,128)(2,1)}), bf16[4,144,576]{2,1,0:T(8,128)(2,1)S(1)}, u32[]{:S(2)}, u32[]{:S(2)}) %all-to-all-start.4) | async-done | bytes 663584 | tf_op jit(solution)/shard_map/all_to_all | solution.py:931
  229.6 1.1 collective-permute-done.42
  230.8 0.9 pad_maximum_fusion.7
  231.7 3.5 %all-to-all-start.5 = ((bf16[8,24,984]{2,1,0:T(8,128)(2,1)}), bf16[8,24,984]{2,1,0:T(8,128)(2,1)S(1)}, u32[]{:S(2)}, u32[]{:S(2)}) async-start(bf16[8,24,984]{2,1,0:T(8,128)(2,1)} %pad_maximum_fusion.7), calls=%async_computation.5 | async-start | bytes 786432 | tf_op jit(solution)/shard_map/all_to_all | solution.py:948
  235.2 1.3 fusion.8
  237.9 5.5 %all-to-all-done.5 = bf16[8,24,984]{2,1,0:T(8,128)(2,1)S(1)} async-done(((bf16[8,24,984]{2,1,0:T(8,128)(2,1)}), bf16[8,24,984]{2,1,0:T(8,128)(2,1)S(1)}, u32[]{:S(2)}, u32[]{:S(2)}) %all-to-all-start.5) | async-done | bytes 377888 | tf_op jit(solution)/shard_map/all_to_all | solution.py:948
  248.0 0.9 reshape.286
  (284 shorter events, 38.7 us)
Async XLA Ops:
  0.7 8.1 %copy-start.22 = (bf16[24,3072]{1,0:T(8,128)(2,1)S(1)}, bf16[24,3072]{1,0:T(8,128)(2,1)}, u32[]{:S(2)}) copy-start(bf16[24,3072]{1,0:T(8,128)(2,1)} %param.25) | copy-start | bytes 442372
  0.7 27.1 %collective-permute-start.6 = (bf16[256,768]{1,0:T(8,128)(2,1)}, bf16[256,768]{1,0:T(8,128)(2,1)S(1)}, u32[]{:S(2)}, u32[]{:S(2)}) collective-permute-start(bf16[256,768]{1,0:T(8,128)(2,1)} %bitcast.184), channel_id=1, source_target_pairs={{0,6},{1,7},{2,4},{3,5},{4,2},{5,3},{6,0},{7,1},{8,14},{9,15},{10,... | collective-permute-start | bytes 1179656 | tf_op jit(solution)/shard_map/ppermute | solution.py:253
  4.6 23.2 %collective-permute-start.5 = (bf16[256,768]{1,0:T(8,128)(2,1)}, bf16[256,768]{1,0:T(8,128)(2,1)S(1)}, u32[]{:S(2)}, u32[]{:S(2)}) collective-permute-start(bf16[256,768]{1,0:T(8,128)(2,1)} %bitcast.185), channel_id=1, source_target_pairs={{0,4},{1,5},{2,6},{3,7},{4,0},{5,1},{6,2},{7,3},{8,12},{9,13},{10,... | collective-permute-start | bytes 1179656 | tf_op jit(solution)/shard_map/ppermute | solution.py:253
  5.1 22.7 %collective-permute-start.4 = (bf16[256,768]{1,0:T(8,128)(2,1)}, bf16[256,768]{1,0:T(8,128)(2,1)S(1)}, u32[]{:S(2)}, u32[]{:S(2)}) collective-permute-start(bf16[256,768]{1,0:T(8,128)(2,1)} %bitcast.186), channel_id=1, source_target_pairs={{0,2},{1,3},{2,0},{3,1},{4,6},{5,7},{6,4},{7,5},{8,10},{9,11},{10,... | collective-permute-start | bytes 1179656 | tf_op jit(solution)/shard_map/ppermute | solution.py:253
  9.3 5.8 %copy-start.27 = (bf16[24,768]{1,0:T(8,128)(2,1)S(1)}, bf16[24,768]{1,0:T(8,128)(2,1)}, u32[]{:S(2)}) copy-start(bf16[24,768]{1,0:T(8,128)(2,1)} %param.24) | copy-start | bytes 110596
  10.2 17.6 %all-to-all-start = ((bf16[8,24,960]{2,1,0:T(8,128)(2,1)}), bf16[8,24,960]{2,1,0:T(8,128)(2,1)S(1)}, u32[]{:S(2)}, u32[]{:S(2)}) async-start(bf16[8,24,960]{2,1,0:T(8,128)(2,1)} %pad_maximum_fusion.6), calls=%async_computation | async-start | bytes 786432 | tf_op jit(solution)/shard_map/all_to_all | solution.py:788
  14.4 7.5 %collective-permute-start.3 = (bf16[128,768]{1,0:T(8,128)(2,1)S(1)}, bf16[128,768]{1,0:T(8,128)(2,1)S(1)}, u32[]{:S(2)}, u32[]{:S(2)}) collective-permute-start(bf16[128,768]{1,0:T(8,128)(2,1)S(1)} %get-tuple-element.315), channel_id=1, source_target_pairs={{0,1},{1,0},{2,3},{3,2},{4,5},{5,4},{6,7},{7,6},{8,9},{9,8},{10,11... | collective-permute-start | bytes 589832 | tf_op jit(solution)/shard_map/ppermute | solution.py:253
  15.2 5.4 %collective-permute-start.2 = (bf16[32,768]{1,0:T(8,128)(2,1)S(1)}, bf16[32,768]{1,0:T(8,128)(2,1)S(1)}, u32[]{:S(2)}, u32[]{:S(2)}) collective-permute-start(bf16[32,768]{1,0:T(8,128)(2,1)S(1)} %fusion.10), channel_id=1, source_target_pairs={{0,24},{8,0},{16,8},{24,16},{1,25},{9,1},{17,9},{25,17},{2,26},{10... | collective-permute-start | bytes 147464 | tf_op jit(solution)/shard_map/ppermute | solution.py:294
  20.6 5.5 %collective-permute-start.1 = (bf16[32,768]{1,0:T(8,128)(2,1)S(1)}, bf16[32,768]{1,0:T(8,128)(2,1)S(1)}, u32[]{:S(2)}, u32[]{:S(2)}) collective-permute-start(bf16[32,768]{1,0:T(8,128)(2,1)S(1)} %fusion.10), channel_id=1, source_target_pairs={{0,16},{8,24},{16,0},{24,8},{1,17},{9,25},{17,1},{25,9},{2,18},{10... | collective-permute-start | bytes 147464 | tf_op jit(solution)/shard_map/ppermute | solution.py:294
  21.9 5.9 %collective-permute-start = (bf16[32,768]{1,0:T(8,128)(2,1)S(1)}, bf16[32,768]{1,0:T(8,128)(2,1)S(1)}, u32[]{:S(2)}, u32[]{:S(2)}) collective-permute-start(bf16[32,768]{1,0:T(8,128)(2,1)S(1)} %fusion.10), channel_id=1, source_target_pairs={{0,8},{8,16},{16,24},{24,0},{1,9},{9,17},{17,25},{25,1},{2,10},{10... | collective-permute-start | bytes 147464 | tf_op jit(solution)/shard_map/ppermute | solution.py:294
  29.0 6.9 %copy-start.23 = (bf16[96,768]{1,0:T(8,128)(2,1)S(1)}, bf16[96,768]{1,0:T(8,128)(2,1)}, u32[]{:S(2)}) copy-start(bf16[96,768]{1,0:T(8,128)(2,1)} %param.26) | copy-start | bytes 442372
  29.5 3.8 %collective-permute-start.7 = (bf16[8,768]{1,0:T(8,128)(2,1)S(1)}, bf16[8,768]{1,0:T(8,128)(2,1)S(1)}, u32[]{:S(2)}, u32[]{:S(2)}) collective-permute-start(bf16[8,768]{1,0:T(8,128)(2,1)S(1)} %get-tuple-element.332), channel_id=1, source_target_pairs={{0,1},{1,0},{2,3},{3,2},{4,5},{5,4},{6,7},{7,6},{8,9},{9,8},{10,11... | collective-permute-start | bytes 36872 | tf_op jit(solution)/shard_map/ppermute | solution.py:253
  29.6 29.8 %collective-permute-start.14 = (bf16[96,576]{1,0:T(8,128)(2,1)S(1)}, bf16[96,576]{1,0:T(8,128)(2,1)S(1)}, u32[]{:S(2)}, u32[]{:S(2)}) collective-permute-start(bf16[96,576]{1,0:T(8,128)(2,1)S(1)} %dynamic-slice_bitcast_fusion.6), channel_id=1, source_target_pairs={{0,24},{8,0},{16,8},{24,16},{1,25},{9,1},{17,9},{25,17},{2,26},{10... | collective-permute-start | bytes 331784 | tf_op jit(solution)/shard_map/ppermute | solution.py:294
  32.3 27.1 %collective-permute-start.13 = (bf16[96,576]{1,0:T(8,128)(2,1)S(1)}, bf16[96,576]{1,0:T(8,128)(2,1)S(1)}, u32[]{:S(2)}, u32[]{:S(2)}) collective-permute-start(bf16[96,576]{1,0:T(8,128)(2,1)S(1)} %dynamic-slice_bitcast_fusion.6), channel_id=1, source_target_pairs={{0,16},{8,24},{16,0},{24,8},{1,17},{9,25},{17,1},{25,9},{2,18},{10... | collective-permute-start | bytes 331784 | tf_op jit(solution)/shard_map/ppermute | solution.py:294
  32.7 26.7 %collective-permute-start.12 = (bf16[96,576]{1,0:T(8,128)(2,1)S(1)}, bf16[96,576]{1,0:T(8,128)(2,1)S(1)}, u32[]{:S(2)}, u32[]{:S(2)}) collective-permute-start(bf16[96,576]{1,0:T(8,128)(2,1)S(1)} %dynamic-slice_bitcast_fusion.6), channel_id=1, source_target_pairs={{0,8},{8,16},{16,24},{24,0},{1,9},{9,17},{17,25},{25,1},{2,10},{10... | collective-permute-start | bytes 331784 | tf_op jit(solution)/shard_map/ppermute | solution.py:294
  33.4 12.3 %copy-start.9 = (bf16[2,136,768]{2,1,0:T(8,128)(2,1)}, bf16[2,136,768]{2,1,0:T(8,128)(2,1)S(1)}, u32[]{:S(2)}) copy-start(bf16[2,136,768]{2,1,0:T(8,128)(2,1)S(1)} %pad_maximum_fusion.5.own_ref) | copy-start | bytes 1253380
  33.4 12.3 %collective-permute-start.10 = (bf16[2,136,768]{2,1,0:T(8,128)(2,1)S(1)}, bf16[2,136,768]{2,1,0:T(8,128)(2,1)S(1)}, u32[]{:S(2)}, u32[]{:S(2)}) collective-permute-start(bf16[2,136,768]{2,1,0:T(8,128)(2,1)S(1)} %pad_maximum_fusion.5.own_ref), channel_id=1, source_target_pairs={{0,6},{1,7},{2,4},{3,5},{4,2},{5,3},{6,0},{7,1},{8,14},{9,15},{10,... | collective-permute-start | bytes 1253384 | tf_op jit(solution)/shard_map/ppermute | solution.py:253
  37.1 46.6 %all-to-all-start.1 = ((bf16[4,96,1536]{2,1,0:T(8,128)(2,1)}), bf16[4,96,1536]{2,1,0:T(8,128)(2,1)S(1)}, u32[]{:S(2)}, u32[]{:S(2)}) async-start(bf16[4,96,1536]{2,1,0:T(8,128)(2,1)} %broadcast_in_dim.32), calls=%async_computation.1 | async-start | bytes 2359296 | tf_op jit(solution)/shard_map/all_to_all | solution.py:802
  41.8 12.7 %collective-permute-start.9 = (bf16[2,136,768]{2,1,0:T(8,128)(2,1)S(1)}, bf16[2,136,768]{2,1,0:T(8,128)(2,1)S(1)}, u32[]{:S(2)}, u32[]{:S(2)}) collective-permute-start(bf16[2,136,768]{2,1,0:T(8,128)(2,1)S(1)} %pad_maximum_fusion.5.own_ref), channel_id=1, source_target_pairs={{0,4},{1,5},{2,6},{3,7},{4,0},{5,1},{6,2},{7,3},{8,12},{9,13},{10,... | collective-permute-start | bytes 1253384 | tf_op jit(solution)/shard_map/ppermute | solution.py:253
  45.7 14.4 %copy-start.37 = (bf16[2,136,768]{2,1,0:T(8,128)(2,1)}, bf16[2,136,768]{2,1,0:T(8,128)(2,1)S(1)}, u32[]{:S(2)}) copy-start(bf16[2,136,768]{2,1,0:T(8,128)(2,1)S(1)} %collective-permute-done.10.across_ref) | copy-start | bytes 1253380
  45.7 10.2 %collective-permute-start.8 = (bf16[2,136,768]{2,1,0:T(8,128)(2,1)S(1)}, bf16[2,136,768]{2,1,0:T(8,128)(2,1)S(1)}, u32[]{:S(2)}, u32[]{:S(2)}) collective-permute-start(bf16[2,136,768]{2,1,0:T(8,128)(2,1)S(1)} %pad_maximum_fusion.5.own_ref), channel_id=1, source_target_pairs={{0,2},{1,3},{2,0},{3,1},{4,6},{5,7},{6,4},{7,5},{8,10},{9,11},{10,... | collective-permute-start | bytes 1253384 | tf_op jit(solution)/shard_map/ppermute | solution.py:253
  59.6 6.9 %copy-start.8 = (bf16[4,96,576]{2,1,0:T(8,128)(2,1)}, bf16[4,96,576]{2,1,0:T(8,128)(2,1)S(1)}, u32[]{:S(2)}) copy-start(bf16[4,96,576]{2,1,0:T(8,128)(2,1)S(1)} %pad_maximum_fusion.4.w_near) | copy-start | bytes 1327108
  59.6 6.9 %collective-permute-start.15 = (bf16[4,96,576]{2,1,0:T(8,128)(2,1)S(1)}, bf16[4,96,576]{2,1,0:T(8,128)(2,1)S(1)}, u32[]{:S(2)}, u32[]{:S(2)}) collective-permute-start(bf16[4,96,576]{2,1,0:T(8,128)(2,1)S(1)} %pad_maximum_fusion.4.w_near), channel_id=1, source_target_pairs={{0,1},{1,0},{2,3},{3,2},{4,5},{5,4},{6,7},{7,6},{8,9},{9,8},{10,11... | collective-permute-start | bytes 1327112 | tf_op jit(solution)/shard_map/ppermute | solution.py:253
  60.0 1.7 collective-permute-start.11
  61.7 21.9 %collective-permute-start.18 = (bf16[2,96,768]{2,1,0:T(8,128)(2,1)S(1)}, bf16[2,96,768]{2,1,0:T(8,128)(2,1)S(1)}, u32[]{:S(2)}, u32[]{:S(2)}) collective-permute-start(bf16[2,96,768]{2,1,0:T(8,128)(2,1)S(1)} %maximum_select_fusion.3), channel_id=1, source_target_pairs={{0,6},{1,7},{2,4},{3,5},{4,2},{5,3},{6,0},{7,1},{8,14},{9,15},{10,... | collective-permute-start | bytes 884744 | tf_op jit(solution)/shard_map/ppermute | solution.py:253
  64.4 19.3 %collective-permute-start.17 = (bf16[2,96,768]{2,1,0:T(8,128)(2,1)S(1)}, bf16[2,96,768]{2,1,0:T(8,128)(2,1)}, u32[]{:S(2)}, u32[]{:S(2)}) collective-permute-start(bf16[2,96,768]{2,1,0:T(8,128)(2,1)S(1)} %maximum_select_fusion.3), channel_id=1, source_target_pairs={{0,4},{1,5},{2,6},{3,7},{4,0},{5,1},{6,2},{7,3},{8,12},{9,13},{10,... | collective-permute-start | bytes 884744 | tf_op jit(solution)/shard_map/ppermute | solution.py:253
  64.9 18.8 %collective-permute-start.16 = (bf16[2,96,768]{2,1,0:T(8,128)(2,1)S(1)}, bf16[2,96,768]{2,1,0:T(8,128)(2,1)S(1)}, u32[]{:S(2)}, u32[]{:S(2)}) collective-permute-start(bf16[2,96,768]{2,1,0:T(8,128)(2,1)S(1)} %maximum_select_fusion.3), channel_id=1, source_target_pairs={{0,2},{1,3},{2,0},{3,1},{4,6},{5,7},{6,4},{7,5},{8,10},{9,11},{10,... | collective-permute-start | bytes 884744 | tf_op jit(solution)/shard_map/ppermute | solution.py:253
  83.7 21.4 %collective-permute-start.19 = (bf16[4,96,1536]{2,1,0:T(8,128)(2,1)S(1)}, bf16[4,96,1536]{2,1,0:T(8,128)(2,1)S(1)}, u32[]{:S(2)}, u32[]{:S(2)}) collective-permute-start(bf16[4,96,1536]{2,1,0:T(8,128)(2,1)S(1)} %all-to-all-done.1), channel_id=1, source_target_pairs={{0,1},{1,0},{2,3},{3,2},{4,5},{5,4},{6,7},{7,6},{8,9},{9,8},{10,11... | collective-permute-start | bytes 3538952 | tf_op jit(solution)/shard_map/ppermute | solution.py:253
  85.5 12.3 %all-to-all-start.2 = ((bf16[8,192,128]{2,1,0:T(8,128)(2,1)}), bf16[8,192,128]{2,1,0:T(8,128)(2,1)S(1)}, u32[]{:S(2)}, u32[]{:S(2)}) async-start(bf16[8,192,128]{2,1,0:T(8,128)(2,1)} %get-tuple-element.179), calls=%async_computation.2 | async-start | bytes 786432 | tf_op jit(solution)/shard_map/all_to_all | solution.py:835
  101.6 13.2 %collective-permute-start.22 = (bf16[256,768]{1,0:T(8,128)(2,1)}, bf16[256,768]{1,0:T(8,128)(2,1)S(1)}, u32[]{:S(2)}, u32[]{:S(2)}) collective-permute-start(bf16[256,768]{1,0:T(8,128)(2,1)} %get-tuple-element.188.refs_0_), channel_id=1, source_target_pairs={{0,6},{1,7},{2,4},{3,5},{4,2},{5,3},{6,0},{7,1},{8,14},{9,15},{10,... | collective-permute-start | bytes 1179656 | tf_op jit(solution)/shard_map/ppermute | solution.py:253
  102.1 18.2 %collective-permute-start.21 = (bf16[256,768]{1,0:T(8,128)(2,1)}, bf16[256,768]{1,0:T(8,128)(2,1)S(1)}, u32[]{:S(2)}, u32[]{:S(2)}) collective-permute-start(bf16[256,768]{1,0:T(8,128)(2,1)} %get-tuple-element.188.refs_0_), channel_id=1, source_target_pairs={{0,4},{1,5},{2,6},{3,7},{4,0},{5,1},{6,2},{7,3},{8,12},{9,13},{10,... | collective-permute-start | bytes 1179656 | tf_op jit(solution)/shard_map/ppermute | solution.py:253
  103.6 16.7 %collective-permute-start.20 = (bf16[256,768]{1,0:T(8,128)(2,1)}, bf16[256,768]{1,0:T(8,128)(2,1)S(1)}, u32[]{:S(2)}, u32[]{:S(2)}) collective-permute-start(bf16[256,768]{1,0:T(8,128)(2,1)} %get-tuple-element.188.refs_0_), channel_id=1, source_target_pairs={{0,2},{1,3},{2,0},{3,1},{4,6},{5,7},{6,4},{7,5},{8,10},{9,11},{10,... | collective-permute-start | bytes 1179656 | tf_op jit(solution)/shard_map/ppermute | solution.py:253
  128.0 16.0 %collective-permute-start.23 = (bf16[256,768]{1,0:T(8,128)(2,1)}, bf16[256,768]{1,0:T(8,128)(2,1)S(1)}, u32[]{:S(2)}, u32[]{:S(2)}) collective-permute-start(bf16[256,768]{1,0:T(8,128)(2,1)} %get-tuple-element.199), channel_id=1, source_target_pairs={{0,2},{1,3},{2,0},{3,1},{4,6},{5,7},{6,4},{7,5},{8,10},{9,11},{10,... | collective-permute-start | bytes 1179656 | tf_op jit(solution)/shard_map/ppermute | solution.py:253
  129.5 17.6 %collective-permute-start.24 = (bf16[256,768]{1,0:T(8,128)(2,1)}, bf16[256,768]{1,0:T(8,128)(2,1)S(1)}, u32[]{:S(2)}, u32[]{:S(2)}) collective-permute-start(bf16[256,768]{1,0:T(8,128)(2,1)} %get-tuple-element.200), channel_id=1, source_target_pairs={{0,4},{1,5},{2,6},{3,7},{4,0},{5,1},{6,2},{7,3},{8,12},{9,13},{10,... | collective-permute-start | bytes 1179656 | tf_op jit(solution)/shard_map/ppermute | solution.py:253
  130.9 17.5 %collective-permute-start.25 = (bf16[256,768]{1,0:T(8,128)(2,1)}, bf16[256,768]{1,0:T(8,128)(2,1)S(1)}, u32[]{:S(2)}, u32[]{:S(2)}) collective-permute-start(bf16[256,768]{1,0:T(8,128)(2,1)} %get-tuple-element.201), channel_id=1, source_target_pairs={{0,6},{1,7},{2,4},{3,5},{4,2},{5,3},{6,0},{7,1},{8,14},{9,15},{10,... | collective-permute-start | bytes 1179656 | tf_op jit(solution)/shard_map/ppermute | solution.py:253
  144.0 6.1 %copy-start.11 = (bf16[256,768]{1,0:T(8,128)(2,1)}, bf16[256,768]{1,0:T(8,128)(2,1)S(1)}, u32[]{:S(2)}) copy-start(bf16[256,768]{1,0:T(8,128)(2,1)S(1)} %collective-permute-done.23.x_ref) | copy-start | bytes 1179652
  148.3 12.3 %collective-permute-start.26 = (bf16[4,192,768]{2,1,0:T(8,128)(2,1)}, bf16[4,192,768]{2,1,0:T(8,128)(2,1)S(1)}, u32[]{:S(2)}, u32[]{:S(2)}) collective-permute-start(bf16[4,192,768]{2,1,0:T(8,128)(2,1)} %get-tuple-element.228), channel_id=1, source_target_pairs={{0,1},{1,0},{2,3},{3,2},{4,5},{5,4},{6,7},{7,6},{8,9},{9,8},{10,11... | collective-permute-start | bytes 3538952 | tf_op jit(solution)/shard_map/ppermute | solution.py:253
  155.7 4.7 %collective-permute-start.28 = (bf16[4,4,24,768]{3,2,1,0:T(8,128)(2,1)}, bf16[4,4,24,768]{3,2,1,0:T(8,128)(2,1)S(1)}, u32[]{:S(2)}, u32[]{:S(2)}) collective-permute-start(bf16[4,4,24,768]{3,2,1,0:T(8,128)(2,1)} %get-tuple-element.240), channel_id=1, source_target_pairs={{0,1},{1,0},{2,3},{3,2},{4,5},{5,4},{6,7},{7,6},{8,9},{9,8},{10,11... | collective-permute-start | bytes 1769480 | tf_op jit(solution)/shard_map/ppermute | solution.py:253
  156.2 13.1 %all-to-all-start.3 = ((bf16[8,192,128]{2,1,0:T(8,128)(2,1)}), bf16[8,192,128]{2,1,0:T(8,128)(2,1)}, u32[]{:S(2)}, u32[]{:S(2)}) async-start(bf16[8,192,128]{2,1,0:T(8,128)(2,1)} %get-tuple-element.222), calls=%async_computation.3 | async-start | bytes 786432 | tf_op jit(solution)/shard_map/all_to_all | solution.py:912
  161.8 16.7 %copy-start.21 = (bf16[192,768]{1,0:T(8,128)(2,1)S(1)}, bf16[192,768]{1,0:T(8,128)(2,1)}, u32[]{:S(2)}) copy-start(bf16[192,768]{1,0:T(8,128)(2,1)} %get-tuple-element.296) | copy-start | bytes 884740
  161.8 11.1 %collective-permute-start.27 = (bf16[192,768]{1,0:T(8,128)(2,1)S(1)}, bf16[192,768]{1,0:T(8,128)(2,1)S(1)}, u32[]{:S(2)}, u32[]{:S(2)}) collective-permute-start(bf16[192,768]{1,0:T(8,128)(2,1)S(1)} %get-tuple-element.298), channel_id=1, source_target_pairs={{0,8},{8,16},{16,24},{24,0},{1,9},{9,17},{17,25},{25,1},{2,10},{10... | collective-permute-start | bytes 884744 | tf_op jit(solution)/shard_map/ppermute | solution.py:309
  163.8 12.3 %collective-permute-start.31 = (bf16[4,24,768]{2,1,0:T(8,128)(2,1)S(1)}, bf16[4,24,768]{2,1,0:T(8,128)(2,1)S(1)}, u32[]{:S(2)}, u32[]{:S(2)}) collective-permute-start(bf16[4,24,768]{2,1,0:T(8,128)(2,1)S(1)} %get-tuple-element.303), channel_id=1, source_target_pairs={{0,6},{1,7},{2,4},{3,5},{4,2},{5,3},{6,0},{7,1},{8,14},{9,15},{10,... | collective-permute-start | bytes 442376 | tf_op jit(solution)/shard_map/ppermute | solution.py:253
  166.7 10.3 %collective-permute-start.30 = (bf16[4,24,768]{2,1,0:T(8,128)(2,1)S(1)}, bf16[4,24,768]{2,1,0:T(8,128)(2,1)S(1)}, u32[]{:S(2)}, u32[]{:S(2)}) collective-permute-start(bf16[4,24,768]{2,1,0:T(8,128)(2,1)S(1)} %get-tuple-element.304), channel_id=1, source_target_pairs={{0,4},{1,5},{2,6},{3,7},{4,0},{5,1},{6,2},{7,3},{8,12},{9,13},{10,... | collective-permute-start | bytes 442376 | tf_op jit(solution)/shard_map/ppermute | solution.py:253
  167.2 11.3 %collective-permute-start.29 = (bf16[4,24,768]{2,1,0:T(8,128)(2,1)S(1)}, bf16[4,24,768]{2,1,0:T(8,128)(2,1)}, u32[]{:S(2)}, u32[]{:S(2)}) collective-permute-start(bf16[4,24,768]{2,1,0:T(8,128)(2,1)S(1)} %get-tuple-element.305), channel_id=1, source_target_pairs={{0,2},{1,3},{2,0},{3,1},{4,6},{5,7},{6,4},{7,5},{8,10},{9,11},{10,... | collective-permute-start | bytes 442376 | tf_op jit(solution)/shard_map/ppermute | solution.py:253
  172.9 24.8 %collective-permute-start.32 = (bf16[256,768]{1,0:T(8,128)(2,1)}, bf16[256,768]{1,0:T(8,128)(2,1)S(1)}, u32[]{:S(2)}, u32[]{:S(2)}) collective-permute-start(bf16[256,768]{1,0:T(8,128)(2,1)} %get-tuple-element.242), channel_id=1, source_target_pairs={{0,2},{1,3},{2,0},{3,1},{4,6},{5,7},{6,4},{7,5},{8,10},{9,11},{10,... | collective-permute-start | bytes 1179656 | tf_op jit(solution)/shard_map/ppermute | solution.py:253
  174.6 23.2 %collective-permute-start.33 = (bf16[256,768]{1,0:T(8,128)(2,1)}, bf16[256,768]{1,0:T(8,128)(2,1)S(1)}, u32[]{:S(2)}, u32[]{:S(2)}) collective-permute-start(bf16[256,768]{1,0:T(8,128)(2,1)} %get-tuple-element.243), channel_id=1, source_target_pairs={{0,4},{1,5},{2,6},{3,7},{4,0},{5,1},{6,2},{7,3},{8,12},{9,13},{10,... | collective-permute-start | bytes 1179656 | tf_op jit(solution)/shard_map/ppermute | solution.py:253
  176.1 21.7 %collective-permute-start.34 = (bf16[256,768]{1,0:T(8,128)(2,1)}, bf16[256,768]{1,0:T(8,128)(2,1)S(1)}, u32[]{:S(2)}, u32[]{:S(2)}) collective-permute-start(bf16[256,768]{1,0:T(8,128)(2,1)} %get-tuple-element.244), channel_id=1, source_target_pairs={{0,6},{1,7},{2,4},{3,5},{4,2},{5,3},{6,0},{7,1},{8,14},{9,15},{10,... | collective-permute-start | bytes 1179656 | tf_op jit(solution)/shard_map/ppermute | solution.py:253
  177.0 15.5 %collective-permute-start.36 = (bf16[192,768]{1,0:T(8,128)(2,1)}, bf16[192,768]{1,0:T(8,128)(2,1)S(1)}, u32[]{:S(2)}, u32[]{:S(2)}) collective-permute-start(bf16[192,768]{1,0:T(8,128)(2,1)} %get-tuple-element.295), channel_id=1, source_target_pairs={{0,24},{8,0},{16,8},{24,16},{1,25},{9,1},{17,9},{25,17},{2,26},{10... | collective-permute-start | bytes 884744 | tf_op jit(solution)/shard_map/ppermute | solution.py:309
  178.5 19.2 %collective-permute-start.35 = (bf16[192,768]{1,0:T(8,128)(2,1)S(1)}, bf16[192,768]{1,0:T(8,128)(2,1)S(1)}, u32[]{:S(2)}, u32[]{:S(2)}) collective-permute-start(bf16[192,768]{1,0:T(8,128)(2,1)S(1)} %copy-done.21), channel_id=1, source_target_pairs={{0,16},{8,24},{16,0},{24,8},{1,17},{9,25},{17,1},{25,9},{2,18},{10... | collective-permute-start | bytes 884744 | tf_op jit(solution)/shard_map/ppermute | solution.py:309
  178.7 23.6 %copy-start.25 = (bf16[4,24,768]{2,1,0:T(8,128)(2,1)S(1)}, bf16[4,24,768]{2,1,0:T(8,128)(2,1)}, u32[]{:S(2)}) copy-start(bf16[4,24,768]{2,1,0:T(8,128)(2,1)} %copy-done.24) | copy-start | bytes 442372
  192.5 11.0 %copy-start.7 = (bf16[4,96,576]{2,1,0:T(8,128)(2,1)S(1)}, bf16[4,96,576]{2,1,0:T(8,128)(2,1)}, u32[]{:S(2)}) copy-start(bf16[4,96,576]{2,1,0:T(8,128)(2,1)} %get-tuple-element.255) | copy-start | bytes 1327108
  192.5 9.7 %copy-start.17 = (bf16[192,768]{1,0:T(8,128)(2,1)}, bf16[192,768]{1,0:T(8,128)(2,1)S(1)}, u32[]{:S(2)}) copy-start(bf16[192,768]{1,0:T(8,128)(2,1)S(1)} %collective-permute-done.36) | copy-start | bytes 884740
  198.4 5.1 %collective-permute-start.41 = (bf16[4,96,576]{2,1,0:T(8,128)(2,1)}, bf16[4,96,576]{2,1,0:T(8,128)(2,1)S(1)}, u32[]{:S(2)}, u32[]{:S(2)}) collective-permute-start(bf16[4,96,576]{2,1,0:T(8,128)(2,1)} %get-tuple-element.256), channel_id=1, source_target_pairs={{0,1},{1,0},{2,3},{3,2},{4,5},{5,4},{6,7},{7,6},{8,9},{9,8},{10,11... | collective-permute-start | bytes 1327112 | tf_op jit(solution)/shard_map/ppermute | solution.py:253
  198.7 12.3 %collective-permute-start.37 = (bf16[256,768]{1,0:T(8,128)(2,1)}, bf16[256,768]{1,0:T(8,128)(2,1)}, u32[]{:S(2)}, u32[]{:S(2)}) collective-permute-start(bf16[256,768]{1,0:T(8,128)(2,1)} %get-tuple-element.252), channel_id=1, source_target_pairs={{0,2},{1,3},{2,0},{3,1},{4,6},{5,7},{6,4},{7,5},{8,10},{9,11},{10,... | collective-permute-start | bytes 1179656 | tf_op jit(solution)/shard_map/ppermute | solution.py:253
  199.8 20.0 %collective-permute-start.38 = (bf16[256,768]{1,0:T(8,128)(2,1)}, bf16[256,768]{1,0:T(8,128)(2,1)}, u32[]{:S(2)}, u32[]{:S(2)}) collective-permute-start(bf16[256,768]{1,0:T(8,128)(2,1)} %get-tuple-element.253), channel_id=1, source_target_pairs={{0,4},{1,5},{2,6},{3,7},{4,0},{5,1},{6,2},{7,3},{8,12},{9,13},{10,... | collective-permute-start | bytes 1179656 | tf_op jit(solution)/shard_map/ppermute | solution.py:253
  201.1 18.7 %collective-permute-start.39 = (bf16[256,768]{1,0:T(8,128)(2,1)}, bf16[256,768]{1,0:T(8,128)(2,1)}, u32[]{:S(2)}, u32[]{:S(2)}) collective-permute-start(bf16[256,768]{1,0:T(8,128)(2,1)} %get-tuple-element.254), channel_id=1, source_target_pairs={{0,6},{1,7},{2,4},{3,5},{4,2},{5,3},{6,0},{7,1},{8,14},{9,15},{10,... | collective-permute-start | bytes 1179656 | tf_op jit(solution)/shard_map/ppermute | solution.py:253
  203.7 6.3 %copy-start.26 = (f32[32,24]{1,0:T(8,128)S(1)}, f32[32,24]{1,0:T(8,128)}, u32[]{:S(2)}) copy-start(f32[32,24]{1,0:T(8,128)} %get-tuple-element.273) | copy-start | bytes 9220
  205.5 23.3 %all-to-all-start.4 = ((bf16[4,144,576]{2,1,0:T(8,128)(2,1)}), bf16[4,144,576]{2,1,0:T(8,128)(2,1)S(1)}, u32[]{:S(2)}, u32[]{:S(2)}) async-start(bf16[4,144,576]{2,1,0:T(8,128)(2,1)} %pad_maximum_fusion.3), calls=%async_computation.4 | async-start | bytes 1474560 | tf_op jit(solution)/shard_map/all_to_all | solution.py:931
  221.5 1.5 collective-permute-start.40
  223.0 6.4 %copy-start.16 = (bf16[192,768]{1,0:T(8,128)(2,1)S(1)}, bf16[192,768]{1,0:T(8,128)(2,1)}, u32[]{:S(2)}) copy-start(bf16[192,768]{1,0:T(8,128)(2,1)} %copy-done.15) | copy-start | bytes 884740
  223.0 6.4 %copy-start.18 = (bf16[192,768]{1,0:T(8,128)(2,1)S(1)}, bf16[192,768]{1,0:T(8,128)(2,1)}, u32[]{:S(2)}) copy-start(bf16[192,768]{1,0:T(8,128)(2,1)} %copy-done.17) | copy-start | bytes 884740
  223.0 6.4 %copy-start.20 = (bf16[192,768]{1,0:T(8,128)(2,1)S(1)}, bf16[192,768]{1,0:T(8,128)(2,1)}, u32[]{:S(2)}) copy-start(bf16[192,768]{1,0:T(8,128)(2,1)} %copy-done.19) | copy-start | bytes 884740
  229.3 1.4 collective-permute-start.42
  231.7 11.7 %all-to-all-start.5 = ((bf16[8,24,984]{2,1,0:T(8,128)(2,1)}), bf16[8,24,984]{2,1,0:T(8,128)(2,1)S(1)}, u32[]{:S(2)}, u32[]{:S(2)}) async-start(bf16[8,24,984]{2,1,0:T(8,128)(2,1)} %pad_maximum_fusion.7), calls=%async_computation.5 | async-start | bytes 786432 | tf_op jit(solution)/shard_map/all_to_all | solution.py:948
  (33 other events, 115.9 us)
